TPU v7x, 32 devices: a whole 2x2x4 slice. The times are simulated.
32 devices in a mesh: rows: 16 (over z, y, x), hid: 2 (over core).
Axes of the slice: x: 2, y: 2, z: 4, core: 2. Of those that a mesh axis runs over, the one named last changes fastest.
Arguments:
- hidden_in: bfloat16 [4096, 768], P('rows', 'hid'), may hold values from -6 to 6
- d_out: bfloat16 [4096, 768], P('rows', 'hid'), may hold values from -6 to 6
- gains: float32 [2, 2, 768], P(None, None, 'hid'), may hold values from 0.25 to 1.75
- mixer: bfloat16 [2, 3, 4, 192, 192], P(None, None, 'hid'), may hold values from -0.4375 to 0.4375
- skip: float32 [2, 768], P(None, 'hid'), may hold values from -3 to 3
- filters: float32 [2, 2, 128, 768], P(None, None, None, 'hid'), may hold values from -0.5 to 0.5
- gate_up: bfloat16 [2, 2, 768, 3072], P(None, None, None, 'hid'), may hold values from -0.21875 to 0.21875
- down: bfloat16 [2, 768, 3072], P(None, None, 'hid'), may hold values from -0.109375 to 0.109375
Outputs:
- hidden_out: bfloat16 [4096, 768], P('rows', 'hid')
- grad_in: float32 [4096, 768], P('rows', 'hid')
- grad_gains: float32 [2, 2, 768], P(None, None, 'hid')
- grad_mixer: float32 [2, 3, 4, 192, 192], P(None, None, 'hid')
- grad_skip: float32 [2, 768], P(None, 'hid')
- grad_filters: float32 [2, 2, 128, 768], P(None, None, None, 'hid')
- grad_gate_up: float32 [2, 2, 768, 3072], P(None, None, 'rows', 'hid')
- grad_down: float32 [2, 768, 3072], P(None, 'rows', 'hid')
All inputs are finite; a program needn't handle non-finite values.
Results may differ from a plain program's by a relative error of at most 0.019.
Values may be sent and summed in bfloat16 or wider, within the bound.
A program may use at most 192 MiB of HBM per device.

v0:
```python
import math

import jax
import jax.numpy as jnp
from jax import lax
from jax.sharding import PartitionSpec as P

ORDER = 128
SEQ_LEN = 8192


norm_eps = 1e-05
filter_decay = 0.02
exact = lax.Precision.HIGHEST


def positions(length):
    half_order = ORDER // 2
    steps = jnp.arange(length, dtype=jnp.int32)
    index_list = jnp.arange(half_order, dtype=jnp.int32)
    multiple = 1 + index_list * index_list * (length // 4) // (half_order * half_order)
    phase = (steps[:, None] * multiple[None, :] % length).astype(jnp.float32) * (
        2.0 * math.pi / length
    )
    return jnp.concatenate([jnp.sin(phase), jnp.cos(phase)], axis=1)


def envelope(length, channels, width):
    fraction = (channels * 37 % width).astype(jnp.float32) / (width - 1)
    start_log = math.log(1.0 / 40.0)
    rate_list = jnp.exp(start_log + (math.log(1.5 / length) - start_log) * fraction)
    steps = jnp.arange(length, dtype=jnp.int32).astype(jnp.float32)
    decay = jnp.exp(-steps[:, None] * rate_list[None, :])
    return decay * lax.rsqrt(2.0 * jnp.sum(decay * decay, axis=0))


def angle_table(count_a, count_b, modulus):
    first_index = jnp.arange(count_a, dtype=jnp.int32)
    second = jnp.arange(count_b, dtype=jnp.int32)
    angle_grid = (first_index[:, None] * second[None, :] % modulus).astype(jnp.float32) * (
        2.0 * math.pi / modulus
    )
    return (jnp.cos(angle_grid), jnp.sin(angle_grid))


def make_tables(length):
    total_size = 2 * length
    outer_size = total_size // 128
    cos_outer, sin_outer = angle_table(outer_size, outer_size, outer_size)
    cos_inner, sin_inner = angle_table(128, 128, 128)
    cos_twist, sin_twist = angle_table(outer_size, 128, total_size)
    return (cos_outer, sin_outer, cos_inner, sin_inner, cos_twist, sin_twist)


def forward_dft(signal, tables):
    cos_outer, sin_outer, cos_inner, sin_inner, cos_twist, sin_twist = tables
    grid_rows = signal.reshape(signal.shape[:-1] + (cos_outer.shape[0], 128))
    real_a = jnp.einsum("nk,...nm->...km", cos_outer, grid_rows, precision=exact)
    imag_a = -jnp.einsum("nk,...nm->...km", sin_outer, grid_rows, precision=exact)
    real_b = real_a * cos_twist + imag_a * sin_twist
    imag_b = imag_a * cos_twist - real_a * sin_twist
    real_c = jnp.einsum("...km,mj->...kj", real_b, cos_inner, precision=exact) + jnp.einsum(
        "...km,mj->...kj", imag_b, sin_inner, precision=exact
    )
    imag_c = jnp.einsum("...km,mj->...kj", imag_b, cos_inner, precision=exact) - jnp.einsum(
        "...km,mj->...kj", real_b, sin_inner, precision=exact
    )
    return (real_c, imag_c)


def inverse_dft(real_c, imag_c, tables, row_count):
    cos_outer, sin_outer, cos_inner, sin_inner, cos_twist, sin_twist = tables
    real_b = jnp.einsum("...kj,mj->...km", real_c, cos_inner, precision=exact) - jnp.einsum(
        "...kj,mj->...km", imag_c, sin_inner, precision=exact
    )
    imag_b = jnp.einsum("...kj,mj->...km", imag_c, cos_inner, precision=exact) + jnp.einsum(
        "...kj,mj->...km", real_c, sin_inner, precision=exact
    )
    real_a = real_b * cos_twist - imag_b * sin_twist
    imag_a = imag_b * cos_twist + real_b * sin_twist
    signal = jnp.einsum(
        "nk,...km->...nm", cos_outer[:row_count], real_a, precision=exact
    ) - jnp.einsum("nk,...km->...nm", sin_outer[:row_count], imag_a, precision=exact)
    return signal.reshape(signal.shape[:-2] + (row_count * 128,)) / (cos_twist.shape[0] * 128)


def channel_spectra(channel_rows, length, tables):
    signal = channel_rows.astype(jnp.float32).reshape(-1, length)
    padded = jnp.concatenate([signal, jnp.zeros_like(signal)], axis=1)
    real_part, imag_part = forward_dft(padded, tables)
    new_shape = (channel_rows.shape[0], -1) + real_part.shape[1:]
    return (real_part.reshape(new_shape), imag_part.reshape(new_shape))


def circular(forward_taps, backward_taps):
    return jnp.concatenate(
        [forward_taps, jnp.zeros_like(forward_taps[:, :1]), backward_taps[:, 1:][:, ::-1]], axis=1
    )


def block_apply(values, weight):
    blocks = values.reshape(values.shape[0], weight.shape[0], weight.shape[1])
    return jnp.einsum("tbi,bio->tbo", blocks, weight, preferred_element_type=jnp.float32).reshape(
        values.shape[0], -1
    )


def block_input_grad(grad_rows, weight):
    blocks = grad_rows.reshape(grad_rows.shape[0], weight.shape[0], weight.shape[2])
    return jnp.einsum("tbo,bio->tbi", blocks, weight, preferred_element_type=jnp.float32).reshape(
        grad_rows.shape[0], -1
    )


def block_weight_grad(values, grad_rows, weight):
    blocks_in = values.reshape(values.shape[0], weight.shape[0], weight.shape[1])
    blocks_out = grad_rows.reshape(grad_rows.shape[0], weight.shape[0], weight.shape[2])
    return jnp.einsum("tbi,tbo->bio", blocks_in, blocks_out, preferred_element_type=jnp.float32)


def norm_forward(values, width):
    row_total, square = lax.psum(
        (jnp.sum(values, axis=1, keepdims=True), jnp.sum(values * values, axis=1, keepdims=True)),
        "hid",
    )
    mean_row = row_total / width
    inv_scale = lax.rsqrt(square / width - mean_row * mean_row + norm_eps)
    return ((values - mean_row) * inv_scale, inv_scale)


def norm_backward(grad_rows, normal, inv_scale, gain, width):
    grad_normal = grad_rows * gain
    row_total, cross_total = lax.psum(
        (
            jnp.sum(grad_normal, axis=1, keepdims=True),
            jnp.sum(grad_normal * normal, axis=1, keepdims=True),
        ),
        "hid",
    )
    return inv_scale * (grad_normal - row_total / width - normal * cross_total / width)


def glu_unit(gate_in, up_in):
    return jax.nn.gelu(gate_in, approximate=True) * up_in


def layer_forward(stream, gains, mixer, skip, filters, gate_up, down, context):
    pos_table, shape_env, tables, length, chan_start, chan_count, width = context
    normal_one, inv_one = norm_forward(stream, width)
    normed = (normal_one * gains[0]).astype(jnp.bfloat16)
    inner_rows = block_apply(normed, mixer[0]).astype(jnp.bfloat16)
    gate_v = block_apply(normed, mixer[1])
    channel_in = lax.all_to_all(inner_rows.T, "rows", split_axis=0, concat_axis=1, tiled=True)
    spec_re, spec_im = channel_spectra(channel_in, length, tables)
    local_filters = lax.dynamic_slice_in_dim(filters, chan_start, chan_count, 2)
    raw_filter = jnp.einsum("eoc,to->ect", local_filters, pos_table, precision=exact)
    kernels = raw_filter * shape_env
    filt_re, filt_im = forward_dft(circular(kernels[0], kernels[1]), tables)
    prod_re = spec_re * filt_re[:, None] - spec_im * filt_im[:, None]
    prod_im = spec_re * filt_im[:, None] + spec_im * filt_re[:, None]
    conv_rows = inverse_dft(prod_re, prod_im, tables, filt_re.shape[1] // 2).reshape(chan_count, -1)
    conv_back = lax.all_to_all(
        conv_rows.astype(jnp.bfloat16), "rows", split_axis=1, concat_axis=0, tiled=True
    ).T
    inner_wide = inner_rows.astype(jnp.float32)
    summed = conv_back.astype(jnp.float32) + skip * inner_wide
    mixed_rows = (gate_v * summed).astype(jnp.bfloat16)
    middle = stream + block_apply(mixed_rows, mixer[2])
    normal_two, inv_two = norm_forward(middle, width)
    normed_two = (normal_two * gains[1]).astype(jnp.bfloat16)
    gathered = lax.all_gather(normed_two, "hid", axis=1, tiled=True)
    gate_act = jnp.dot(gathered, gate_up[0], preferred_element_type=jnp.float32)
    up_act = jnp.dot(gathered, gate_up[1], preferred_element_type=jnp.float32)
    hidden = glu_unit(gate_act, up_act).astype(jnp.bfloat16)
    partial_value = lax.dot_general(
        hidden, down, (((1,), (1,)), ((), ())), preferred_element_type=jnp.float32
    )
    result = middle + lax.psum_scatter(
        partial_value.astype(jnp.bfloat16), "hid", scatter_dimension=1, tiled=True
    ).astype(jnp.float32)
    stored = (
        normal_one,
        inv_one,
        normed,
        inner_rows,
        gate_v,
        channel_in,
        raw_filter,
        filt_re,
        filt_im,
        summed,
        mixed_rows,
        normal_two,
        inv_two,
        gathered,
        gate_act,
        up_act,
        hidden,
    )
    return (result, stored)


def layer_backward(grad_next, stored, gains, mixer, skip, gate_up, down, context):
    pos_table, shape_env, tables, length, chan_start, chan_count, width = context
    (
        normal_one,
        inv_one,
        normed,
        inner_rows,
        gate_v,
        spectra,
        raw_filter,
        filt_re,
        filt_im,
        summed,
        mixed_rows,
        normal_two,
        inv_two,
        gathered,
        gate_act,
        up_act,
        hidden,
    ) = stored
    grad_ff = grad_next.astype(jnp.bfloat16)
    grad_wide = lax.all_gather(grad_ff, "hid", axis=1, tiled=True)
    grad_hidden = jnp.dot(grad_wide, down, preferred_element_type=jnp.float32)
    grad_down = jnp.einsum("td,tf->df", grad_wide, hidden, preferred_element_type=jnp.float32)
    unused_value, glu_pull = jax.vjp(glu_unit, gate_act, up_act)
    grad_gate, grad_up = glu_pull(grad_hidden)
    grad_gate = grad_gate.astype(jnp.bfloat16)
    grad_up = grad_up.astype(jnp.bfloat16)
    grad_pair = jnp.stack(
        [
            jnp.einsum("td,tf->df", gathered, grad_gate, preferred_element_type=jnp.float32),
            jnp.einsum("td,tf->df", gathered, grad_up, preferred_element_type=jnp.float32),
        ]
    )
    partial_value = lax.dot_general(
        grad_gate, gate_up[0], (((1,), (1,)), ((), ())), preferred_element_type=jnp.float32
    ) + lax.dot_general(
        grad_up, gate_up[1], (((1,), (1,)), ((), ())), preferred_element_type=jnp.float32
    )
    grad_normed_two = lax.psum_scatter(
        partial_value.astype(jnp.bfloat16), "hid", scatter_dimension=1, tiled=True
    ).astype(jnp.float32)
    gain_two = jnp.sum(grad_normed_two * normal_two, axis=0)
    grad_middle = grad_next + norm_backward(grad_normed_two, normal_two, inv_two, gains[1], width)
    grad_mix_out = grad_middle.astype(jnp.bfloat16)
    weight_out = block_weight_grad(mixed_rows, grad_mix_out, mixer[2])
    grad_mixed = block_input_grad(grad_mix_out, mixer[2])
    grad_gate_v = (grad_mixed * summed).astype(jnp.bfloat16)
    grad_summed = grad_mixed * gate_v
    inner_wide = inner_rows.astype(jnp.float32)
    grad_skip = jnp.sum(grad_summed * inner_wide, axis=0)
    grad_conv = grad_summed.astype(jnp.bfloat16)
    channel_grad = lax.all_to_all(grad_conv.T, "rows", split_axis=0, concat_axis=1, tiled=True)
    grad_re, grad_im = channel_spectra(channel_grad, length, tables)
    spec_re, spec_im = channel_spectra(spectra, length, tables)
    back_re = grad_re * filt_re[:, None] + grad_im * filt_im[:, None]
    back_im = grad_im * filt_re[:, None] - grad_re * filt_im[:, None]
    grad_in_rows = inverse_dft(back_re, back_im, tables, filt_re.shape[1] // 2).reshape(
        chan_count, -1
    )
    grad_conv_in = lax.all_to_all(
        grad_in_rows.astype(jnp.bfloat16), "rows", split_axis=1, concat_axis=0, tiled=True
    ).T
    kernel_re = jnp.sum(grad_re * spec_re + grad_im * spec_im, axis=1)
    kernel_im = jnp.sum(grad_im * spec_re - grad_re * spec_im, axis=1)
    grad_circle = inverse_dft(kernel_re, kernel_im, tables, filt_re.shape[1])
    grad_forward = grad_circle[:, :length]
    grad_backward = jnp.concatenate(
        [jnp.zeros_like(grad_circle[:, :1]), grad_circle[:, length + 1 :][:, ::-1]], axis=1
    )
    grad_raw = (
        jnp.stack([grad_forward, grad_backward]) * shape_env + 2.0 * filter_decay * raw_filter
    )
    grad_local = jnp.einsum("ect,to->eoc", grad_raw, pos_table, precision=exact)
    grad_filter = lax.dynamic_update_slice_in_dim(
        jnp.zeros((2, pos_table.shape[1], normed.shape[1]), jnp.float32), grad_local, chan_start, 2
    )
    grad_inner = (skip * grad_summed + grad_conv_in.astype(jnp.float32)).astype(jnp.bfloat16)
    weight_in = block_weight_grad(normed, grad_inner, mixer[0])
    weight_gate = block_weight_grad(normed, grad_gate_v, mixer[1])
    grad_normed = block_input_grad(grad_inner, mixer[0]) + block_input_grad(grad_gate_v, mixer[1])
    gain_one = jnp.sum(grad_normed * normal_one, axis=0)
    grad_stream = grad_middle + norm_backward(grad_normed, normal_one, inv_one, gains[0], width)
    small_grads = (
        jnp.stack([gain_one, gain_two]),
        jnp.stack([weight_in, weight_gate, weight_out]),
        grad_skip,
        grad_filter,
    )
    large_grads = (grad_pair, grad_down)
    return (grad_stream, small_grads, large_grads)


def on_device(hidden_in, d_out, gains, mixer, skip, filters, gate_up, down):
    local_width = hidden_in.shape[1]
    token_count = hidden_in.shape[0]
    width = gate_up.shape[2]
    layers = gate_up.shape[0]
    row_devices = lax.axis_size("rows")
    chan_count = local_width // row_devices
    length = min(SEQ_LEN, token_count * row_devices)
    chan_start = lax.axis_index("rows") * chan_count
    channels = (
        lax.axis_index("hid") * local_width + chan_start + jnp.arange(chan_count, dtype=jnp.int32)
    )
    context = (
        positions(length),
        envelope(length, channels, width).T,
        make_tables(length),
        length,
        chan_start,
        chan_count,
        width,
    )
    stream = hidden_in.astype(jnp.float32)
    stored_list = []
    for layer_index in range(layers):
        stream, stored = layer_forward(
            stream,
            gains[layer_index],
            mixer[layer_index],
            skip[layer_index],
            filters[layer_index],
            gate_up[layer_index],
            down[layer_index],
            context,
        )
        stored_list.append(stored)
    hidden_out = stream.astype(jnp.bfloat16)
    grad_stream = d_out.astype(jnp.float32)
    small_list = []
    large_list = []
    for layer_index in reversed(range(layers)):
        grad_stream, small_grads, large_grads = layer_backward(
            grad_stream,
            stored_list[layer_index],
            gains[layer_index],
            mixer[layer_index],
            skip[layer_index],
            gate_up[layer_index],
            down[layer_index],
            context,
        )
        small_list.insert(0, small_grads)
        large_list.insert(0, large_grads)
    small_stacked = tuple(
        (jnp.stack([grads_entry[member] for grads_entry in small_list]) for member in range(4))
    )
    large_stacked = tuple(
        (jnp.stack([grads_entry[member] for grads_entry in large_list]) for member in range(2))
    )
    small_stacked = lax.psum(small_stacked, "rows")
    large_stacked = (
        lax.psum_scatter(large_stacked[0], "rows", scatter_dimension=2, tiled=True),
        lax.psum_scatter(large_stacked[1], "rows", scatter_dimension=1, tiled=True),
    )
    return (
        hidden_out,
        grad_stream,
        small_stacked[0],
        small_stacked[1],
        small_stacked[2],
        small_stacked[3],
        large_stacked[0],
        large_stacked[1],
    )


def solution(mesh):
    placed = (
        P("rows", "hid"),
        P("rows", "hid"),
        P(None, None, "hid"),
        P(None, None, "hid", None, None),
        P(None, "hid"),
        P(None, None, None, "hid"),
        P(None, None, None, "hid"),
        P(None, None, "hid"),
    )
    return jax.shard_map(
        on_device,
        mesh=mesh,
        in_specs=placed,
        out_specs=(
            P("rows", "hid"),
            P("rows", "hid"),
            P(None, None, "hid"),
            P(None, None, "hid", None, None),
            P(None, "hid"),
            P(None, None, None, "hid"),
            P(None, None, "rows", "hid"),
            P(None, "rows", "hid"),
        ),
        check_vma=False,
    )
```

profile of v0, /device:TPU:0, one launch (start us, length us, event | category | flops | bytes accessed | tf_op | source)
XLA Modules:
  0.0 1055.7 jit_solution(11574295154970917816)
XLA Ops:
  9.8 2.6 all-reduce.15
  14.4 8.2 all-to-all-start
  26.9 9.2 fusion.95
  36.1 2.8 maximum_bitcast_fusion.2
  39.0 4.5 fusion.264
  43.5 5.6 broadcast_multiply_fusion
  50.9 12.7 %reverse = f32[24,4096]{1,0:T(8,128)S(1)} reverse(f32[24,4096]{1,0:T(8,128)} %bitcast.783), dimensions={1} | reverse | bytes 786432
  94.3 9.0 convolution_subtract_fusion.11
  108.1 6.8 all-to-all-start.1
  115.0 3.0 convolution_bitcast_fusion.6
  118.0 5.4 all-to-all-done.1
  132.2 2.6 fusion.22
  134.8 4.4 multiply_convert_fusion.3
  140.1 3.2 fusion.76
  159.2 6.3 all-to-all-start.2
  165.5 4.1 all_gather.14
  169.7 3.3 convolution_add_fusion.7
  190.7 5.1 all-to-all-start.3
  195.9 3.8 fusion
  200.9 4.1 all-to-all-done.3
  212.4 2.6 fusion.6
  215.0 4.6 fusion.55
  219.7 3.0 fusion.4
  222.7 3.2 fusion.70
  229.7 3.8 reduce-scatter.23.cloned.1.call-done
  242.0 6.8 all-to-all-start.4
  248.9 3.5 fusion.79
  283.2 5.3 all-to-all-start.5
  292.2 15.3 %reverse.2 = f32[24,4096]{1,0:T(8,128)} reverse(f32[24,4096]{1,0:T(8,128)} %bitcast.785), dimensions={1} | reverse | bytes 786432
  321.5 3.6 fusion.48
  325.1 3.0 fusion.16
  328.2 3.2 fusion.73
  334.6 2.7 convolution_bitcast_fusion.18
  350.4 7.0 all-to-all-start.6
  362.8 3.6 all-to-all-done.6
  383.8 15.3 %reverse.3 = f32[24,4096]{1,0:T(8,128)} reverse(f32[24,4096]{1,0:T(8,128)} %bitcast.782), dimensions={1} | reverse | bytes 786432
  411.8 4.2 all-to-all-start.7
  417.2 2.8 convolution_bitcast_fusion.19
  431.4 4.8 pad_maximum_fusion.1
  441.1 4.3 convolution_bitcast_fusion.5
  445.4 3.0 convolution_bitcast_fusion.4
  448.4 4.8 maximum_bitcast_fusion
  453.2 6.7 pad_maximum_fusion
  468.1 42.7 %all-reduce.6 = (f32[2,2,384]{2,1,0:T(2,128)}, f32[2,384]{1,0:T(2,128)}) all-reduce(f32[2,2,384]{2,1,0:T(2,128)S(1)} %pad_maximum_fusion.4, f32[2,384]{1,0:T(2,128)S(1)} %pad_maximum_fusion.5), channel_id=1, replica_groups=mesh['rows'=16,'hid'=2] {'rows'}, use_global_device_ids=true, to_apply=%region_41.42 | all-reduce | flops 2304 | bytes 18432 | tf_op jit(solution)/shard_map/psum | solution.py:355
  510.8 65.7 %all-reduce.18.cloned.1.call-done = (f32[2,3,2,192,192]{4,3,2,1,0:T(8,128)}, f32[2,2,128,384]{3,2,1,0:T(8,128)}) async-done(((f32[2,3,2,192,192]{4,3,2,1,0:T(8,128)}, f32[2,2,128,384]{3,2,1,0:T(8,128)}), (f32[2,3,2,192,192]{4,3,2,1,0:T(8,128)}, f32[2,2,128,384]{3,2,1,0:T(8,128)})) %all-reduce.18.cloned.1.call-update) | async-done | bytes 2555920 | tf_op jit(solution)/shard_map/psum | solution.py:355
  576.5 177.3 %reduce-scatter.17.cloned.1.call-done = f32[2,48,1536]{2,1,0:T(8,128)} async-done(((f32[2,768,1536]{2,1,0:T(8,128)}), f32[2,48,1536]{2,1,0:T(8,128)}) %reduce-scatter.17.cloned.1.call-update) | async-done | bytes 589840 | tf_op jit(solution)/shard_map/reduce_scatter | solution.py:358
  753.9 290.3 %reduce-scatter.15.cloned.1.call-done = f32[2,2,48,1536]{3,2,1,0:T(8,128)} async-done(((f32[2,2,768,1536]{3,2,1,0:T(8,128)}), f32[2,2,48,1536]{3,2,1,0:T(8,128)}) %reduce-scatter.15.cloned.1.call-update) | async-done | bytes 1179664 | tf_op jit(solution)/shard_map/reduce_scatter | solution.py:357
  1044.2 3.3 copy.269
  (446 shorter events, 235.7 us)
Async XLA Ops:
  7.2 18.8 %copy-start.79 = (f32[2,2,128,384]{3,2,1,0:T(8,128)S(1)}, f32[2,2,128,384]{3,2,1,0:T(8,128)}, u32[]{:S(2)}) copy-start(f32[2,2,128,384]{3,2,1,0:T(8,128)} %param.13) | copy-start | bytes 2359300
  8.6 18.3 %copy-start.88 = (f32[384]{0:T(512)}, f32[384]{0:T(512)S(1)}, u32[]{:S(2)}) copy-start(f32[384]{0:T(512)S(1)} %get-tuple-element.44) | copy-start | bytes 4612
  9.7 17.2 %copy-start.30 = (bf16[256,384]{0,1:T(8,128)(2,1)}, bf16[256,384]{0,1:T(8,128)(2,1)S(1)}, u32[]{:S(2)}) copy-start(bf16[256,384]{0,1:T(8,128)(2,1)S(1)} %copy.159) | copy-start | bytes 589828
  12.3 14.5 %copy-start.94 = (f32[256,1]{0,1:T(1,128)}, f32[256,1]{0,1:T(1,128)S(1)}, u32[]{:S(2)}) copy-start(f32[256,1]{0,1:T(1,128)S(1)} %get-tuple-element.113) | copy-start | bytes 3076
  12.3 14.5 %copy-start.96 = (f32[256,1]{0,1:T(1,128)}, f32[256,1]{0,1:T(1,128)S(1)}, u32[]{:S(2)}) copy-start(f32[256,1]{0,1:T(1,128)S(1)} %get-tuple-element.114) | copy-start | bytes 3076
  12.5 23.6 %copy-start.34 = (bf16[256,384]{0,1:T(8,128)(2,1)}, bf16[256,384]{0,1:T(8,128)(2,1)S(1)}, u32[]{:S(2)}) copy-start(bf16[256,384]{0,1:T(8,128)(2,1)S(1)} %fusion.169) | copy-start | bytes 589828
  14.4 70.8 %all-to-all-start = ((bf16[16,24,256]{2,1,0:T(8,128)(2,1)}), bf16[16,24,256]{2,1,0:T(8,128)(2,1)S(1)}, u32[]{:S(2)}, u32[]{:S(2)}) async-start(bf16[16,24,256]{2,1,0:T(8,128)(2,1)} %bitcast.12), calls=%async_computation | async-start | bytes 393216 | tf_op jit(solution)/shard_map/all_to_all | solution.py:153
  24.8 98.7 %copy-start.10 = (f32[2,256,192]{1,2,0:T(8,128)}, f32[2,256,192]{1,2,0:T(8,128)S(1)}, u32[]{:S(2)}) copy-start(f32[2,256,192]{1,2,0:T(8,128)S(1)} %fusion.246) | copy-start | bytes 1179652
  38.9 4.5 copy-start.32
  43.5 5.6 copy-start.29
  68.9 4.8 copy-start.1
  94.3 10.1 copy-start.81
  105.0 9.9 copy-start.101
  108.1 15.3 %all-to-all-start.1 = ((bf16[24,16,256]{2,0,1:T(8,128)(2,1)}), bf16[24,16,256]{2,0,1:T(8,128)(2,1)S(1)}, u32[]{:S(2)}, u32[]{:S(2)}) async-start(bf16[24,16,256]{2,0,1:T(8,128)(2,1)} %copy.168), calls=%async_computation.1 | async-start | bytes 393216 | tf_op jit(solution)/shard_map/all_to_all | solution.py:162
  114.9 36.5 %reduce-scatter.19.cloned.1.call-start = ((), (), s32[]{:S(2)}) async-start(), calls=%async_computation.16 | async-start | bytes 589824
  115.0 12.5 %copy-start.90 = (f32[384]{0:T(512)}, f32[384]{0:T(512)S(1)}, u32[]{:S(2)}) copy-start(f32[384]{0:T(512)S(1)} %get-tuple-element.47) | copy-start | bytes 4612
  115.0 90.1 %copy-start.92 = (f32[384]{0:T(512)}, f32[384]{0:T(512)S(1)}, u32[]{:S(2)}) copy-start(f32[384]{0:T(512)S(1)} %get-tuple-element.46) | copy-start | bytes 4612
  115.0 15.0 %copy-start.87 = (f32[384]{0:T(512)S(1)}, f32[384]{0:T(512)}, u32[]{:S(2)}) copy-start(f32[384]{0:T(512)} %get-tuple-element.43) | copy-start | bytes 4612
  134.8 4.4 copy-start.65
  149.4 6.1 copy-start.86
  159.2 15.5 %all-to-all-start.2 = ((bf16[16,24,256]{2,1,0:T(8,128)(2,1)}), bf16[16,24,256]{2,1,0:T(8,128)(2,1)}, u32[]{:S(2)}, u32[]{:S(2)}) async-start(bf16[16,24,256]{2,1,0:T(8,128)(2,1)} %bitcast.745), calls=%async_computation.2 | async-start | bytes 393216 | tf_op jit(solution)/shard_map/all_to_all | solution.py:153
  190.7 14.4 %all-to-all-start.3 = ((bf16[24,16,256]{2,0,1:T(8,128)(2,1)}), bf16[24,16,256]{2,0,1:T(8,128)(2,1)}, u32[]{:S(2)}, u32[]{:S(2)}) async-start(bf16[24,16,256]{2,0,1:T(8,128)(2,1)} %copy.179), calls=%async_computation.3 | async-start | bytes 393216 | tf_op jit(solution)/shard_map/all_to_all | solution.py:162
  195.9 37.7 %reduce-scatter.23.cloned.1.call-start = ((), (), s32[]{:S(2)}) async-start(), calls=%async_computation.18 | async-start | bytes 589824
  199.7 7.9 copy-start.8
  200.9 5.4 copy-start.12
  212.4 223.9 %copy-start.7 = (bf16[256,768]{0,1:T(8,128)(2,1)}, bf16[256,768]{0,1:T(8,128)(2,1)S(1)}, u32[]{:S(2)}) copy-start(bf16[256,768]{0,1:T(8,128)(2,1)S(1)} %all_gather.13) | copy-start | bytes 1179652
  242.0 16.0 %all-to-all-start.4 = ((bf16[16,24,256]{2,1,0:T(8,128)(2,1)}), bf16[16,24,256]{2,1,0:T(8,128)(2,1)}, u32[]{:S(2)}, u32[]{:S(2)}) async-start(bf16[16,24,256]{2,1,0:T(8,128)(2,1)} %bitcast.791), calls=%async_computation.4 | async-start | bytes 393216 | tf_op jit(solution)/shard_map/all_to_all | solution.py:256
  248.8 68.0 %reduce-scatter.21.cloned.1.call-start = ((), (), s32[]{:S(2)}) async-start(), calls=%async_computation.17 | async-start | bytes 589824
  279.9 29.6 %copy-start.93 = (f32[384]{0:T(512)S(1)}, f32[384]{0:T(512)}, u32[]{:S(2)}) copy-start(f32[384]{0:T(512)} %copy-done.92) | copy-start | bytes 4612
  283.2 26.2 %all-to-all-start.5 = ((bf16[24,16,256]{2,0,1:T(8,128)(2,1)}), bf16[24,16,256]{2,0,1:T(8,128)(2,1)}, u32[]{:S(2)}, u32[]{:S(2)}) async-start(bf16[24,16,256]{2,0,1:T(8,128)(2,1)} %copy.188), calls=%async_computation.5 | async-start | bytes 393216 | tf_op jit(solution)/shard_map/all_to_all | solution.py:264
  288.5 54.1 %reduce-scatter.25.cloned.1.call-start = ((), (), s32[]{:S(2)}) async-start(), calls=%async_computation.19 | async-start | bytes 589824
  309.4 4.1 copy-start.9
  316.8 4.7 copy-start.66
  316.8 4.7 copy-start.103
  337.3 10.1 copy-start.11
  350.4 16.0 %all-to-all-start.6 = ((bf16[16,24,256]{2,1,0:T(8,128)(2,1)}), bf16[16,24,256]{2,1,0:T(8,128)(2,1)}, u32[]{:S(2)}, u32[]{:S(2)}) async-start(bf16[16,24,256]{2,1,0:T(8,128)(2,1)} %bitcast.792), calls=%async_computation.6 | async-start | bytes 393216 | tf_op jit(solution)/shard_map/all_to_all | solution.py:256
  399.2 4.1 copy-start.28
  411.8 12.3 %all-to-all-start.7 = ((bf16[24,16,256]{2,0,1:T(8,128)(2,1)}), bf16[24,16,256]{2,0,1:T(8,128)(2,1)}, u32[]{:S(2)}, u32[]{:S(2)}) async-start(bf16[24,16,256]{2,0,1:T(8,128)(2,1)} %copy.196), calls=%async_computation.7 | async-start | bytes 393216 | tf_op jit(solution)/shard_map/all_to_all | solution.py:264
  415.9 160.6 %all-reduce.18.cloned.1.call-start = ((), (), s32[]{:S(2)}) async-start(), calls=%async_computation.20 | async-start | bytes 6291456 | tf_op jit(solution)/shard_map/psum | solution.py:355
  420.0 4.1 copy-start.42
  420.0 4.1 copy-start.59
  420.0 5.3 copy-start.35
  428.6 325.3 %reduce-scatter.17.cloned.1.call-start = ((), (), s32[]{:S(2)}) async-start(), calls=%async_computation.15 | async-start | bytes 10027008 | tf_op jit(solution)/shard_map/reduce_scatter | solution.py:358
  436.2 608.0 %reduce-scatter.15.cloned.1.call-start = ((), (), s32[]{:S(2)}) async-start(), calls=%async_computation.14 | async-start | bytes 20054016 | tf_op jit(solution)/shard_map/reduce_scatter | solution.py:357
  441.1 4.3 copy-start.6
  441.1 4.3 copy-start.76
  460.6 6.3 copy-start.40
  460.6 6.3 copy-start.60
  (71 other events, 149.5 us)
Sparse Core Ops, SparseCore 0:
  145.4 5.4 reduce-scatter.18
  228.0 5.5 reduce-scatter.22
  254.4 8.9 reduce-scatter.20
  333.5 8.9 reduce-scatter.24
  428.7 147.7 all-reduce.17
  583.6 170.2 reduce-scatter.16
  760.2 283.9 reduce-scatter.14
where the time goes:
time: 1070 us; the launch traced here: 1060 us
  waiting for transfers between devices  556 us (52%)
  matrix products  187 us (17%)
  local copies, waits for them, and re-layouts  114 us (11%)
  blocking collectives  72.9 us (7%)
  other arithmetic  59.5 us (6%)
  starting transfers between devices  50.2 us (5%)
  between operations  16.5 us (2%)
    reduce_scatter x1, waiting for transfers between devices, on_device(): lax.psum_scatter(large_stacked[0], 'rows', scatter_dimension=2, tiled=True)  290 us
    reduce_scatter x1, waiting for transfers between devices, on_device(): lax.psum_scatter(large_stacked[1], 'rows', scatter_dimension=1, tiled=True)  177 us
    unnamed x238, local copies, waits for them, and re-layouts  81 us
    psum x1, waiting for transfers between devices, on_device(): small_stacked = lax.psum(small_stacked, 'rows')  65.7 us
    psum x1, blocking collectives, on_device(): small_stacked = lax.psum(small_stacked, 'rows')  42.7 us
  transfers between devices with their start and end apart: 15, of which 11 were waited for; matrix products, arithmetic and copies ran while one was open for 18% of the time, Pallas kernels for 0%

commit v1 on v0

v1 whole, which is shorter than its diff:
```python
import functools
import math

import jax
import jax.numpy as jnp
import numpy as np
from jax import lax
from jax.experimental import pallas as pl
from jax.experimental.pallas import tpu as pltpu
from jax.sharding import PartitionSpec as P

ORDER = 128
SEQ_LEN = 8192
LANES = 128
NORM_EPS = 1e-05
DECAY = 0.02
MESH = pl.DeviceIdType.MESH
BF16 = jnp.bfloat16
F32 = jnp.float32
MIB = 2**20
GELU_C = math.sqrt(2.0 / math.pi)


def round_up(value, step):
    return -(-value // step) * step


def whole():
    return pl.BlockSpec(memory_space=pltpu.VMEM)


def nn(a, b):
    return lax.dot_general(a, b, (((1,), (0,)), ((), ())), preferred_element_type=F32)


def nt(a, b):
    return lax.dot_general(a, b, (((1,), (1,)), ((), ())), preferred_element_type=F32)


def tn(a, b):
    return lax.dot_general(a, b, (((0,), (0,)), ((), ())), preferred_element_type=F32)


def position_table(length):
    half_order = ORDER // 2
    index_list = np.arange(half_order)
    multiple = 1 + index_list * index_list * (length // 4) // (half_order * half_order)
    phase = (np.arange(length)[:, None] * multiple[None, :] % length) * (2.0 * math.pi / length)
    return np.concatenate([np.sin(phase), np.cos(phase)], axis=1)


def dft_tables(length):
    blocks = length // LANES
    size = 2 * length
    outer = 2 * blocks
    k = np.arange(outer)
    n = np.arange(blocks)
    m = np.arange(LANES)
    angle = 2.0 * math.pi * (np.outer(k, n) % outer) / outer
    outer_fwd = np.concatenate([np.cos(angle), -np.sin(angle)], axis=0)
    outer_inv = np.concatenate([np.cos(angle), -np.sin(angle)], axis=0).T / size
    angle = 2.0 * math.pi * (np.outer(m, m) % LANES) / LANES
    cos, sin = np.cos(angle), np.sin(angle)
    inner_fwd = np.block([[cos, -sin], [sin, cos]])
    inner_inv = np.block([[cos, sin], [-sin, cos]])
    angle = 2.0 * math.pi * np.outer(k, m) / size
    twist = np.concatenate([np.cos(angle), np.sin(angle)], axis=1)
    half = lambda table: jnp.asarray(table, F32).astype(BF16)
    return (half(outer_fwd), half(outer_inv), half(inner_fwd), half(inner_inv), jnp.asarray(twist, F32))


def normalize(values):
    mean = jnp.mean(values, axis=1, keepdims=True)
    square = jnp.mean(values * values, axis=1, keepdims=True)
    inv = lax.rsqrt(square - mean * mean + NORM_EPS)
    return (values - mean) * inv, inv


def norm_back(grad, normal, inv, gain):
    scaled = grad * gain
    mean = jnp.mean(scaled, axis=1, keepdims=True)
    cross = jnp.mean(scaled * normal, axis=1, keepdims=True)
    return inv * (scaled - mean - normal * cross), jnp.sum(grad * normal, axis=0, keepdims=True)


def gelu_parts(gate):
    square = gate * gate
    tanh = jnp.tanh(GELU_C * gate * (1.0 + 0.044715 * square))
    half = 0.5 * (1.0 + tanh)
    value = gate * half
    slope = half + 0.5 * gate * (1.0 - tanh * tanh) * (GELU_C * (1.0 + 3.0 * 0.044715 * square))
    return value, slope


def enter(count, hid):
    me = lax.axis_index("rows") * hid + lax.axis_index("hid")
    barrier = pltpu.get_barrier_semaphore()

    def greet(step, carry):
        peer = lax.rem(me + step, count)
        pl.semaphore_signal(
            barrier, inc=1, device_id=(peer // hid, lax.rem(peer, hid)), device_id_type=MESH
        )
        return carry

    lax.fori_loop(1, count, greet, 0)
    return barrier


def exchange_start(source, target, sems, count, rows, hid, piece, by_owner):
    send, recv, local = sems
    row = lax.axis_index("rows")
    col = lax.axis_index("hid")
    token_id = row * hid + col
    owner_id = col * rows + row
    mine_there = token_id if by_owner else owner_id
    mine_here = owner_id if by_owner else token_id
    at = lambda index: pl.ds(pl.multiple_of(index * piece, piece), piece)
    pltpu.make_async_copy(source.at[at(mine_here)], target.at[at(mine_there)], local).start()

    def post(step, carry):
        peer = lax.rem(token_id + step, count)
        peer_row = peer // hid
        peer_col = lax.rem(peer, hid)
        there = (peer_col * rows + peer_row) if by_owner else peer
        pltpu.make_async_remote_copy(
            src_ref=source.at[at(there)],
            dst_ref=target.at[at(mine_there)],
            send_sem=send,
            recv_sem=recv,
            device_id=(peer_row, peer_col),
            device_id_type=MESH,
        ).start()
        return carry

    lax.fori_loop(1, count, post, 0)


def exchange_wait(source, target, sems, count, rows, hid, piece):
    send, recv, local = sems
    row = lax.axis_index("rows")
    col = lax.axis_index("hid")
    pltpu.make_async_copy(
        source.at[pl.ds(0, piece)], target.at[pl.ds(0, piece)], local
    ).wait()
    span = pl.ds(0, (count - 1) * piece)
    pltpu.make_async_remote_copy(
        src_ref=source.at[span],
        dst_ref=target.at[span],
        send_sem=send,
        recv_sem=recv,
        device_id=(row, hid - 1 - col),
        device_id_type=MESH,
    ).wait()


class Sizes:
    def __init__(self, rows, hid, width, hidden, tokens):
        self.rows, self.hid, self.width, self.hidden = rows, hid, width, hidden
        self.count = rows * hid
        self.chans = width // self.count
        self.piece = round_up(self.chans, 16)
        self.length = min(SEQ_LEN, tokens)
        self.seqs = tokens // self.length
        self.blocks = self.length // LANES
        self.outer = 2 * self.blocks
        self.pairs = self.seqs * self.chans
        self.half = width // hid
        self.padded = rows * self.piece
        self.channels = self.count * self.piece


def spread_in(source, wide, lines, stride, blocks):
    for place, line in enumerate(lines):
        wide[:, place * LANES : (place + 1) * LANES] = source[
            pl.ds(line, blocks, stride=stride), :
        ].astype(wide.dtype)


def dft(wide, spectrum, tables, mid, flat, lines, outer, offset=0):
    outer_fwd, inner_fwd, twist = tables
    mid[:, : lines * LANES] = nn(outer_fwd[...], wide[:, : lines * LANES])
    cos = twist[:, :LANES]
    sin = twist[:, LANES:]
    for line in range(lines):
        lanes = pl.ds(line * LANES, LANES)
        real = mid[0:outer, lanes]
        imag = mid[outer : 2 * outer, lanes]
        rows = pl.ds(line * outer, outer)
        flat[rows, 0:LANES] = (real * cos + imag * sin).astype(BF16)
        flat[rows, LANES:] = (imag * cos - real * sin).astype(BF16)
    spectrum[0 : lines * outer, :] = nn(flat[0 : lines * outer, :], inner_fwd[...])


def inverse_dft(flat, tables, mid_half, lines, outer):
    outer_inv, inner_inv, twist = tables
    cos = twist[:, :LANES]
    sin = twist[:, LANES:]
    for line in range(lines):
        rows = pl.ds(line * outer, outer)
        lanes = pl.ds(line * LANES, LANES)
        part = nn(flat[rows, :], inner_inv[...])
        real = part[:, :LANES]
        imag = part[:, LANES:]
        mid_half[0:outer, lanes] = (real * cos - imag * sin).astype(BF16)
        mid_half[outer : 2 * outer, lanes] = (imag * cos + real * sin).astype(BF16)
    return nn(outer_inv[...], mid_half[:, : lines * LANES])


def spread_out(value, target, lines, stride, blocks):
    for place, line in enumerate(lines):
        target[pl.ds(line, blocks, stride=stride), :] = value[
            :, place * LANES : (place + 1) * LANES
        ]


def signal_lines(sz):
    return [seq * sz.blocks * sz.piece + chan for seq in range(sz.seqs) for chan in range(sz.chans)]


def conv_forward_kernel(
    sz,
    inner_ref,
    taps_ref,
    pos_ref,
    env_ref,
    outer_fwd,
    outer_inv,
    inner_fwd,
    inner_inv,
    twist,
    conv_ref,
    filt_spec,
    sig_spec,
    landed,
    staged,
    tall,
    wide,
    mid,
    flat,
    mid_half,
    sems_in,
    sems_out,
):
    barrier = enter(sz.count, sz.hid)
    pl.semaphore_wait(barrier, sz.count - 1)
    into = tuple(sems_in.at[i] for i in range(3))
    back = tuple(sems_out.at[i] for i in range(3))
    exchange_start(inner_ref, landed, into, sz.count, sz.rows, sz.hid, sz.piece, True)

    piece, blocks, outer = sz.piece, sz.blocks, sz.outer
    step = 4
    for start in range(0, blocks, step):
        span = slice(start * LANES, (start + step) * LANES)
        raw = nn(taps_ref[...], pos_ref[:, span])
        kernels = raw * env_ref[:, span]
        for block in range(step):
            tall[pl.ds((start + block) * 2 * piece, 2 * piece), :] = kernels[
                :, block * LANES : (block + 1) * LANES
            ]
    lines = [way * piece + chan for way in range(2) for chan in range(sz.chans)]
    spread_in(tall, wide, lines, 2 * piece, blocks)
    dft(wide, sig_spec, (outer_fwd, inner_fwd, twist), mid, flat, len(lines), outer)
    span = sz.chans * outer
    filt_spec[:, :LANES] = sig_spec[0:span, :LANES] + sig_spec[span : 2 * span, :LANES]
    filt_spec[:, LANES:] = sig_spec[0:span, LANES:] - sig_spec[span : 2 * span, LANES:]

    exchange_wait(inner_ref, landed, into, sz.count, sz.rows, sz.hid, piece)
    tall[0 : sz.channels, :] = landed[...].astype(F32)
    lines = signal_lines(sz)
    spread_in(tall, wide, lines, piece, blocks)
    dft(wide, sig_spec, (outer_fwd, inner_fwd, twist), mid, flat, sz.pairs, outer)
    for seq in range(sz.seqs):
        rows = pl.ds(seq * span, span)
        sig_re, sig_im = sig_spec[rows, :LANES], sig_spec[rows, LANES:]
        fil_re, fil_im = filt_spec[:, :LANES], filt_spec[:, LANES:]
        flat[rows, :LANES] = (sig_re * fil_re - sig_im * fil_im).astype(BF16)
        flat[rows, LANES:] = (sig_re * fil_im + sig_im * fil_re).astype(BF16)
    result = inverse_dft(flat, (outer_inv, inner_inv, twist), mid_half, sz.pairs, outer)
    spread_out(result, tall, lines, piece, blocks)
    staged[...] = tall[0 : sz.channels, :].astype(BF16)
    exchange_start(staged, conv_ref, back, sz.count, sz.rows, sz.hid, piece, False)
    exchange_wait(staged, conv_ref, back, sz.count, sz.rows, sz.hid, piece)


def conv_forward(sz, inner, taps, pos, env, tables, cid):
    outer_fwd, outer_inv, inner_fwd, inner_inv, twist = tables
    wide_lines = max(2 * sz.chans, sz.pairs)
    return pl.pallas_call(
        functools.partial(conv_forward_kernel, sz),
        out_shape=(
            jax.ShapeDtypeStruct((sz.channels, LANES), BF16),
            jax.ShapeDtypeStruct((sz.chans * sz.outer, 2 * LANES), F32),
            jax.ShapeDtypeStruct((wide_lines * sz.outer, 2 * LANES), F32),
        ),
        in_specs=[whole()] * 9,
        out_specs=(whole(),) * 3,
        scratch_shapes=[
            pltpu.VMEM((sz.channels, LANES), BF16),
            pltpu.VMEM((sz.channels, LANES), BF16),
            pltpu.VMEM((max(2 * sz.piece * sz.blocks, sz.channels), LANES), F32),
            pltpu.VMEM((sz.blocks, wide_lines * LANES), BF16),
            pltpu.VMEM((2 * sz.outer, wide_lines * LANES), F32),
            pltpu.VMEM((wide_lines * sz.outer, 2 * LANES), BF16),
            pltpu.VMEM((2 * sz.outer, sz.pairs * LANES), BF16),
            pltpu.SemaphoreType.DMA((3,)),
            pltpu.SemaphoreType.DMA((3,)),
        ],
        compiler_params=pltpu.CompilerParams(
            collective_id=cid, has_side_effects=True, vmem_limit_bytes=48 * MIB
        ),
        name="conv_forward",
    )(inner, taps, pos, env, outer_fwd, outer_inv, inner_fwd, inner_inv, twist)


def conv_backward_kernel(
    sz,
    grad_ref,
    filt_spec,
    sig_spec,
    taps_ref,
    pos_ref,
    env_ref,
    outer_fwd,
    outer_inv,
    inner_fwd,
    inner_inv,
    twist,
    back_ref,
    taps_grad,
    landed,
    staged,
    tall,
    wide,
    mid,
    flat,
    mid_half,
    grad_spec,
    sems_in,
    sems_out,
):
    barrier = enter(sz.count, sz.hid)
    pl.semaphore_wait(barrier, sz.count - 1)
    into = tuple(sems_in.at[i] for i in range(3))
    back = tuple(sems_out.at[i] for i in range(3))
    piece, blocks, outer = sz.piece, sz.blocks, sz.outer
    exchange_start(grad_ref, landed, into, sz.count, sz.rows, sz.hid, piece, True)
    exchange_wait(grad_ref, landed, into, sz.count, sz.rows, sz.hid, piece)
    tall[0 : sz.channels, :] = landed[...].astype(F32)
    lines = signal_lines(sz)
    spread_in(tall, wide, lines, piece, blocks)
    dft(wide, grad_spec, (outer_fwd, inner_fwd, twist), mid, flat, sz.pairs, outer)
    span = sz.chans * outer
    for seq in range(sz.seqs):
        rows = pl.ds(seq * span, span)
        re, im = grad_spec[rows, :LANES], grad_spec[rows, LANES:]
        fil_re, fil_im = filt_spec[:, :LANES], filt_spec[:, LANES:]
        flat[rows, :LANES] = (re * fil_re + im * fil_im).astype(BF16)
        flat[rows, LANES:] = (im * fil_re - re * fil_im).astype(BF16)
    inv_tables = (outer_inv, inner_inv, twist)
    result = inverse_dft(flat, inv_tables, mid_half, sz.pairs, outer)
    spread_out(result, tall, lines, piece, blocks)
    staged[...] = tall[0 : sz.channels, :].astype(BF16)
    exchange_start(staged, back_ref, back, sz.count, sz.rows, sz.hid, piece, False)

    total_re = jnp.zeros((span, LANES), F32)
    total_im = jnp.zeros((span, LANES), F32)
    for seq in range(sz.seqs):
        rows = pl.ds(seq * span, span)
        re, im = grad_spec[rows, :LANES], grad_spec[rows, LANES:]
        sig_re, sig_im = sig_spec[rows, :LANES], sig_spec[rows, LANES:]
        total_re += re * sig_re + im * sig_im
        total_im += im * sig_re - re * sig_im
    flat[0:span, :LANES] = total_re.astype(BF16)
    flat[span : 2 * span, :LANES] = total_re.astype(BF16)
    flat[0:span, LANES:] = total_im.astype(BF16)
    flat[span : 2 * span, LANES:] = (-total_im).astype(BF16)
    result = inverse_dft(flat, inv_tables, mid_half, 2 * sz.chans, outer)
    lines = [way * piece + chan for way in range(2) for chan in range(sz.chans)]
    if sz.chans < piece:
        tall[...] = jnp.zeros_like(tall)
    spread_out(result, tall, lines, 2 * piece, blocks)
    total = jnp.zeros((2 * piece, ORDER), F32)
    step = 4
    for start in range(0, blocks, step):
        span = slice(start * LANES, (start + step) * LANES)
        raw = nn(taps_ref[...], pos_ref[:, span])
        grads = jnp.concatenate(
            [
                tall[pl.ds((start + block) * 2 * piece, 2 * piece), :]
                for block in range(step)
            ],
            axis=1,
        )
        grads = grads * env_ref[:, span] + (2.0 * DECAY) * raw
        total += nt(grads.astype(BF16), pos_ref[:, span])
    taps_grad[...] = total

    exchange_wait(staged, back_ref, back, sz.count, sz.rows, sz.hid, piece)


def conv_backward(sz, grad, filt_spec, sig_spec, taps, pos, env, tables, cid):
    outer_fwd, outer_inv, inner_fwd, inner_inv, twist = tables
    wide_lines = max(2 * sz.chans, sz.pairs)
    return pl.pallas_call(
        functools.partial(conv_backward_kernel, sz),
        out_shape=(
            jax.ShapeDtypeStruct((sz.channels, LANES), BF16),
            jax.ShapeDtypeStruct((2 * sz.piece, ORDER), F32),
        ),
        in_specs=[whole()] * 11,
        out_specs=(whole(),) * 2,
        scratch_shapes=[
            pltpu.VMEM((sz.channels, LANES), BF16),
            pltpu.VMEM((sz.channels, LANES), BF16),
            pltpu.VMEM((max(2 * sz.piece * sz.blocks, sz.channels), LANES), F32),
            pltpu.VMEM((sz.blocks, wide_lines * LANES), BF16),
            pltpu.VMEM((2 * sz.outer, wide_lines * LANES), F32),
            pltpu.VMEM((wide_lines * sz.outer, 2 * LANES), BF16),
            pltpu.VMEM((2 * sz.outer, wide_lines * LANES), BF16),
            pltpu.VMEM((sz.pairs * sz.outer, 2 * LANES), F32),
            pltpu.SemaphoreType.DMA((3,)),
            pltpu.SemaphoreType.DMA((3,)),
        ],
        compiler_params=pltpu.CompilerParams(
            collective_id=cid, has_side_effects=True, vmem_limit_bytes=48 * MIB
        ),
        name="conv_backward",
    )(grad, filt_spec, sig_spec, taps, pos, env, outer_fwd, outer_inv, inner_fwd, inner_inv, twist)


def project(sz, normed, w_in, w_gate, inner_ref, gate_ref):
    for side in range(sz.hid):
        rows = slice(side * sz.padded, (side + 1) * sz.padded)
        part = normed[:, side * sz.half : (side + 1) * sz.half]
        inner_ref[rows, :] = nt(w_in[side], part).astype(BF16)
        gate_ref[rows, :] = nt(w_gate[side], part)


def first_kernel(sz, x_ref, gain_ref, w_in, w_gate, normed_ref, inner_ref, gate_ref):
    normal, _ = normalize(x_ref[...].astype(F32))
    normed = (normal * gain_ref[0:1, :]).astype(BF16)
    normed_ref[...] = normed
    project(sz, normed, w_in, w_gate, inner_ref, gate_ref)


def first(sz, x, gains, w_in, w_gate):
    tokens = x.shape[0]
    return pl.pallas_call(
        functools.partial(first_kernel, sz),
        out_shape=(
            jax.ShapeDtypeStruct((tokens, sz.width), BF16),
            jax.ShapeDtypeStruct((sz.channels, tokens), BF16),
            jax.ShapeDtypeStruct((sz.channels, tokens), F32),
        ),
        in_specs=[whole()] * 4,
        out_specs=(whole(),) * 3,
        compiler_params=pltpu.CompilerParams(vmem_limit_bytes=32 * MIB),
        name="first_projection",
    )(x, gains, w_in, w_gate)


def mix_out(sz, mixed, w_out):
    parts = []
    for side in range(sz.hid):
        rows = slice(side * sz.padded, (side + 1) * sz.padded)
        parts.append(tn(mixed[rows, :], w_out[side]))
    return jnp.concatenate(parts, axis=1)


def ff_specs(sz, layer, tile):
    steps = sz.hidden // sz.hid // tile
    first_half = lambda i: jnp.minimum(i, steps - 1)
    second = lambda i: jnp.maximum(i - steps, 0)
    specs = []
    for place in (first_half, second):
        specs.append(
            pl.BlockSpec((1, 2, sz.width, tile), lambda i, place=place: (layer, 0, 0, place(i)))
        )
        specs.append(pl.BlockSpec((1, sz.width, tile), lambda i, place=place: (layer, 0, place(i))))
    return specs, steps


def forward_kernel(
    sz,
    steps,
    conv_ref,
    inner_ref,
    gate_ref,
    skip_ref,
    x_ref,
    gain_ref,
    next_gain,
    w_out,
    w_in,
    w_gate,
    up_a,
    down_a,
    up_b,
    down_b,
    summed_ref,
    mixed_ref,
    middle_ref,
    normed_two,
    next_x,
    next_normed,
    next_inner,
    next_gate,
):
    index = pl.program_id(0)

    @pl.when(index == 0)
    def _():
        summed = conv_ref[...].astype(F32) + skip_ref[...] * inner_ref[...].astype(F32)
        summed_ref[...] = summed
        mixed_ref[...] = (gate_ref[...] * summed).astype(BF16)
        middle = x_ref[...].astype(F32) + mix_out(sz, mixed_ref, w_out)
        middle_ref[...] = middle
        normal, _ = normalize(middle)
        normed_two[...] = (normal * gain_ref[1:2, :]).astype(BF16)
        next_x[...] = middle

    def accumulate(up_ref, down_ref):
        gate = nn(normed_two[...], up_ref[0, 0])
        up = nn(normed_two[...], up_ref[0, 1])
        value, _ = gelu_parts(gate)
        next_x[...] += nt((value * up).astype(BF16), down_ref[0])

    pl.when(index < steps)(lambda: accumulate(up_a, down_a))
    pl.when(index >= steps)(lambda: accumulate(up_b, down_b))

    @pl.when(index == 2 * steps - 1)
    def _():
        normal, _ = normalize(next_x[...])
        normed = (normal * next_gain[0:1, :]).astype(BF16)
        next_normed[...] = normed
        project(sz, normed, w_in, w_gate, next_inner, next_gate)


def full(shape):
    return pl.BlockSpec(shape, lambda i: (0,) * len(shape))


def forward(sz, layer, conv, inner, gate, skip, x, gains, next_gains, w_out, w_in, w_gate, ff):
    tokens = x.shape[0]
    tile = 512
    specs, steps = ff_specs(sz, layer, tile)
    small = (conv, inner, gate, skip, x, gains, next_gains, w_out, w_in, w_gate)
    outs = (
        ((sz.channels, tokens), F32),
        ((sz.channels, tokens), BF16),
        ((tokens, sz.width), F32),
        ((tokens, sz.width), BF16),
        ((tokens, sz.width), F32),
        ((tokens, sz.width), BF16),
        ((sz.channels, tokens), BF16),
        ((sz.channels, tokens), F32),
    )
    return pl.pallas_call(
        functools.partial(forward_kernel, sz, steps),
        grid=(2 * steps,),
        out_shape=tuple(jax.ShapeDtypeStruct(shape, kind) for shape, kind in outs),
        in_specs=[full(entry.shape) for entry in small] + specs,
        out_specs=tuple(full(shape) for shape, kind in outs),
        compiler_params=pltpu.CompilerParams(
            dimension_semantics=("arbitrary",), vmem_limit_bytes=48 * MIB
        ),
        name="token_forward",
    )(*small, *ff)


def block_grads(sz, tall, flat, target, slot):
    blocks_side = target.shape[1] // sz.hid
    size = sz.half // blocks_side
    rows = sz.padded // blocks_side
    for side in range(sz.hid):
        for block in range(blocks_side):
            begin = side * sz.padded + block * rows
            place = side * sz.half + block * size
            target[slot, side * blocks_side + block] = nn(
                tall[begin : begin + rows, :], flat[:, place : place + size]
            ).astype(target.dtype)


def ff_backward_tile(normed, grad, up_ref, down_ref, total, out_total):
    gate = nn(normed, up_ref[0, 0])
    up = nn(normed, up_ref[0, 1])
    grad_hidden = nn(grad, down_ref[0])
    value, slope = gelu_parts(gate)
    if out_total is not None:
        out_total[...] += nt((value * up).astype(BF16), down_ref[0])
    grad_gate = (slope * up * grad_hidden).astype(BF16)
    grad_up = (value * grad_hidden).astype(BF16)
    total[...] += nt(grad_gate, up_ref[0, 0]) + nt(grad_up, up_ref[0, 1])


def mixer_backward(
    sz, grad_next, middle, total, gain, mixed, summed, gate, w_out, outs
):
    grad_middle, mixer_grad, grad_gate, grad_summed, grad_conv, gain_grad = outs
    normal, inv = normalize(middle)
    back, gain_grad[...] = norm_back(total, normal, inv, gain)
    result = grad_next + back
    grad_middle[...] = result
    grad_o = result.astype(BF16)
    block_grads(sz, mixed, grad_o, mixer_grad, 0)
    for side in range(sz.hid):
        rows = slice(side * sz.padded, (side + 1) * sz.padded)
        grad_mixed = nt(w_out[side], grad_o[:, side * sz.half : (side + 1) * sz.half])
        grad_gate[rows, :] = (grad_mixed * summed[rows, :]).astype(BF16)
        through = grad_mixed * gate[rows, :]
        grad_summed[rows, :] = through
        grad_conv[rows, :] = through.astype(BF16)


def mixer_outs(sz, tokens, blocks):
    size = sz.width // blocks
    return (
        ((tokens, sz.width), F32),
        ((1, blocks, sz.channels // blocks, size), BF16),
        ((sz.channels, tokens), BF16),
        ((sz.channels, tokens), F32),
        ((sz.channels, tokens), BF16),
        ((1, sz.width), F32),
    )


def turn_kernel(
    sz,
    steps,
    conv_ref,
    inner_ref,
    gate_ref,
    skip_ref,
    x_ref,
    gain_ref,
    grad_ref,
    w_out,
    up_a,
    down_a,
    up_b,
    down_b,
    hidden_out,
    normed_two,
    grad_middle,
    mixer_grad,
    grad_gate,
    grad_summed,
    grad_conv,
    gain_grad,
    summed,
    mixed,
    middle,
    out_total,
    total,
):
    index = pl.program_id(0)

    @pl.when(index == 0)
    def _():
        summed[...] = conv_ref[...].astype(F32) + skip_ref[...] * inner_ref[...].astype(F32)
        mixed[...] = (gate_ref[...] * summed[...]).astype(BF16)
        middle[...] = x_ref[...].astype(F32) + mix_out(sz, mixed, w_out)
        normal, _ = normalize(middle[...])
        normed_two[...] = (normal * gain_ref[1:2, :]).astype(BF16)
        out_total[...] = middle[...]
        total[...] = jnp.zeros_like(total)

    def accumulate(up_ref, down_ref):
        ff_backward_tile(normed_two[...], grad_ref[...], up_ref, down_ref, total, out_total)

    pl.when(index < steps)(lambda: accumulate(up_a, down_a))
    pl.when(index >= steps)(lambda: accumulate(up_b, down_b))

    @pl.when(index == 2 * steps - 1)
    def _():
        hidden_out[...] = out_total[...].astype(BF16)
        outs = (grad_middle, mixer_grad, grad_gate, grad_summed, grad_conv, gain_grad)
        mixer_backward(
            sz,
            grad_ref[...].astype(F32),
            middle[...],
            total[...],
            gain_ref[1:2, :],
            mixed,
            summed,
            gate_ref,
            w_out,
            outs,
        )


def turn(sz, layer, blocks, conv, inner, gate, skip, x, gains, grad, w_out, ff):
    tokens = x.shape[0]
    specs, steps = ff_specs(sz, layer, 512)
    small = (conv, inner, gate, skip, x, gains, grad, w_out)
    outs = (((tokens, sz.width), BF16), ((tokens, sz.width), BF16)) + mixer_outs(sz, tokens, blocks)
    return pl.pallas_call(
        functools.partial(turn_kernel, sz, steps),
        grid=(2 * steps,),
        out_shape=tuple(jax.ShapeDtypeStruct(shape, kind) for shape, kind in outs),
        in_specs=[full(entry.shape) for entry in small] + specs,
        out_specs=tuple(full(shape) for shape, kind in outs),
        scratch_shapes=[
            pltpu.VMEM((sz.channels, tokens), F32),
            pltpu.VMEM((sz.channels, tokens), BF16),
            pltpu.VMEM((tokens, sz.width), F32),
            pltpu.VMEM((tokens, sz.width), F32),
            pltpu.VMEM((tokens, sz.width), F32),
        ],
        compiler_params=pltpu.CompilerParams(
            dimension_semantics=("arbitrary",), vmem_limit_bytes=48 * MIB
        ),
        name="token_turn",
    )(*small, *ff)


def input_backward(
    sz, back, through, grad_gate, skip, normed, x, gain, w_in, w_gate, grad_middle, mixer_grad
):
    inner_grad = (skip * through + back.astype(F32)).astype(BF16)
    block_grads(sz, inner_grad, normed, mixer_grad, 0)
    block_grads(sz, grad_gate, normed, mixer_grad, 1)
    parts = []
    for side in range(sz.hid):
        rows = slice(side * sz.padded, (side + 1) * sz.padded)
        parts.append(tn(inner_grad[rows, :], w_in[side]) + tn(grad_gate[rows, :], w_gate[side]))
    normal, inv = normalize(x)
    result, gain_grad = norm_back(jnp.concatenate(parts, axis=1), normal, inv, gain)
    return grad_middle + result, gain_grad


def backward_kernel(
    sz,
    steps,
    back_ref,
    through_ref,
    gate_grad_ref,
    skip_ref,
    normed_ref,
    x_ref,
    gain_ref,
    w_in,
    w_gate,
    grad_middle_ref,
    normed_two,
    middle_ref,
    summed_ref,
    gate_ref,
    mixed_ref,
    low_gain,
    w_out,
    up_a,
    down_a,
    up_b,
    down_b,
    input_grad,
    input_gain,
    grad_ff,
    grad_middle,
    mixer_grad,
    grad_gate,
    grad_summed,
    grad_conv,
    gain_grad,
    grad_next,
    total,
):
    index = pl.program_id(0)

    @pl.when(index == 0)
    def _():
        result, input_gain[...] = input_backward(
            sz,
            back_ref[...],
            through_ref[...],
            gate_grad_ref[...],
            skip_ref[...],
            normed_ref[...],
            x_ref[...],
            gain_ref[0:1, :],
            w_in,
            w_gate,
            grad_middle_ref[...],
            input_grad,
        )
        grad_next[...] = result
        grad_ff[...] = result.astype(BF16)
        total[...] = jnp.zeros_like(total)

    def accumulate(up_ref, down_ref):
        ff_backward_tile(normed_two[...], grad_ff[...], up_ref, down_ref, total, None)

    pl.when(index < steps)(lambda: accumulate(up_a, down_a))
    pl.when(index >= steps)(lambda: accumulate(up_b, down_b))

    @pl.when(index == 2 * steps - 1)
    def _():
        outs = (grad_middle, mixer_grad, grad_gate, grad_summed, grad_conv, gain_grad)
        mixer_backward(
            sz,
            grad_next[...],
            middle_ref[...],
            total[...],
            low_gain[1:2, :],
            mixed_ref,
            summed_ref,
            gate_ref,
            w_out,
            outs,
        )


def input_outs(sz, blocks):
    size = sz.width // blocks
    return (((2, blocks, sz.channels // blocks, size), BF16), ((1, sz.width), F32))


def backward(
    sz,
    layer,
    blocks,
    back,
    through,
    gate_grad,
    skip,
    normed,
    x,
    gains,
    w_in,
    w_gate,
    grad_middle,
    normed_two,
    middle,
    summed,
    gate,
    mixed,
    low_gains,
    w_out,
    ff,
):
    tokens = x.shape[0]
    specs, steps = ff_specs(sz, layer, 512)
    small = (
        back,
        through,
        gate_grad,
        skip,
        normed,
        x,
        gains,
        w_in,
        w_gate,
        grad_middle,
        normed_two,
        middle,
        summed,
        gate,
        mixed,
        low_gains,
        w_out,
    )
    outs = (
        input_outs(sz, blocks) + (((tokens, sz.width), BF16),) + mixer_outs(sz, tokens, blocks)
    )
    return pl.pallas_call(
        functools.partial(backward_kernel, sz, steps),
        grid=(2 * steps,),
        out_shape=tuple(jax.ShapeDtypeStruct(shape, kind) for shape, kind in outs),
        in_specs=[full(entry.shape) for entry in small] + specs,
        out_specs=tuple(full(shape) for shape, kind in outs),
        scratch_shapes=[
            pltpu.VMEM((tokens, sz.width), F32),
            pltpu.VMEM((tokens, sz.width), F32),
        ],
        compiler_params=pltpu.CompilerParams(
            dimension_semantics=("arbitrary",), vmem_limit_bytes=48 * MIB
        ),
        name="token_backward",
    )(*small, *ff)


def last_kernel(
    sz,
    back_ref,
    through_ref,
    gate_grad_ref,
    skip_ref,
    normed_ref,
    x_ref,
    gain_ref,
    w_in,
    w_gate,
    grad_middle_ref,
    input_grad,
    input_gain,
    grad_in,
):
    grad_in[...], input_gain[...] = input_backward(
        sz,
        back_ref[...],
        through_ref[...],
        gate_grad_ref[...],
        skip_ref[...],
        normed_ref[...],
        x_ref[...].astype(F32),
        gain_ref[0:1, :],
        w_in,
        w_gate,
        grad_middle_ref[...],
        input_grad,
    )


def last(sz, blocks, *args):
    tokens = args[5].shape[0]
    outs = input_outs(sz, blocks) + (((tokens, sz.width), F32),)
    return pl.pallas_call(
        functools.partial(last_kernel, sz),
        out_shape=tuple(jax.ShapeDtypeStruct(shape, kind) for shape, kind in outs),
        in_specs=[whole()] * len(args),
        out_specs=(whole(),) * len(outs),
        compiler_params=pltpu.CompilerParams(vmem_limit_bytes=32 * MIB),
        name="last_projection",
    )(*args)


def ff_grads_kernel(normed_ref, grad_ref, up_ref, down_ref, out_ref, hidden, grad_gate, grad_up):
    tokens = normed_ref.shape[0]
    chunk = 256
    for start in range(0, tokens, chunk):
        rows = pl.ds(start, chunk)
        normed = normed_ref[rows, :]
        gate = nn(normed, up_ref[0])
        up = nn(normed, up_ref[1])
        through = nn(grad_ref[rows, :], down_ref[...])
        value, slope = gelu_parts(gate)
        hidden[rows, :] = (value * up).astype(BF16)
        grad_gate[rows, :] = (slope * up * through).astype(BF16)
        grad_up[rows, :] = (value * through).astype(BF16)
    out_ref[0] = tn(normed_ref[...], grad_gate[...]).astype(BF16)
    out_ref[1] = tn(normed_ref[...], grad_up[...]).astype(BF16)
    out_ref[2] = tn(grad_ref[...], hidden[...]).astype(BF16)


def ff_grads(normed, grad, up, down):
    tokens, width = normed.shape
    units = down.shape[1]
    return pl.pallas_call(
        ff_grads_kernel,
        out_shape=jax.ShapeDtypeStruct((3, width, units), BF16),
        in_specs=[whole()] * 4,
        out_specs=whole(),
        scratch_shapes=[pltpu.VMEM((tokens, units), BF16)] * 3,
        compiler_params=pltpu.CompilerParams(vmem_limit_bytes=48 * MIB),
        name="ff_weight_grads",
    )(normed, grad, up, down)


def row_exchange_kernel(rows, parts, *refs):
    sources, targets, sems = refs[:parts], refs[parts : 2 * parts], refs[2 * parts]
    row = lax.axis_index("rows")
    col = lax.axis_index("hid")
    barrier = pltpu.get_barrier_semaphore()

    def greet(step, carry):
        peer = lax.rem(row + step, rows)
        pl.semaphore_signal(barrier, inc=1, device_id=(peer, col), device_id_type=MESH)
        return carry

    lax.fori_loop(1, rows, greet, 0)
    for part in range(parts):
        pltpu.make_async_copy(
            sources[part].at[row], targets[part].at[row], sems.at[part, 2]
        ).start()
    pl.semaphore_wait(barrier, rows - 1)

    def post(step, carry):
        peer = lax.rem(row + step, rows)
        for part in range(parts):
            pltpu.make_async_remote_copy(
                src_ref=sources[part].at[peer],
                dst_ref=targets[part].at[row],
                send_sem=sems.at[part, 0],
                recv_sem=sems.at[part, 1],
                device_id=(peer, col),
                device_id_type=MESH,
            ).start()
        return carry

    lax.fori_loop(1, rows, post, 0)
    for part in range(parts):
        pltpu.make_async_copy(
            sources[part].at[0], targets[part].at[0], sems.at[part, 2]
        ).wait()
        span = pl.ds(0, rows - 1)
        pltpu.make_async_remote_copy(
            src_ref=sources[part].at[span],
            dst_ref=targets[part].at[span],
            send_sem=sems.at[part, 0],
            recv_sem=sems.at[part, 1],
            device_id=(lax.rem(row + 1, rows), col),
            device_id_type=MESH,
        ).wait()


def row_exchange(arrays, rows, cid):
    parts = len(arrays)
    return pl.pallas_call(
        functools.partial(row_exchange_kernel, rows, parts),
        out_shape=tuple(jax.ShapeDtypeStruct(entry.shape, entry.dtype) for entry in arrays),
        in_specs=[pl.BlockSpec(memory_space=pl.ANY)] * parts,
        out_specs=(pl.BlockSpec(memory_space=pl.ANY),) * parts,
        scratch_shapes=[pltpu.SemaphoreType.DMA((parts, 3))],
        compiler_params=pltpu.CompilerParams(collective_id=cid, has_side_effects=True),
        name="row_exchange",
    )(*arrays)


def swap(value):
    return lax.ppermute(value, "hid", [(0, 1), (1, 0)])


def both_halves(own, axis):
    other = swap(own)
    low = lax.axis_index("hid") == 0
    return jnp.concatenate([jnp.where(low, own, other), jnp.where(low, other, own)], axis=axis)


def own_tokens(part):
    tokens = part.shape[0] // 2
    side = lax.axis_index("hid")
    keep = lax.dynamic_slice_in_dim(part, side * tokens, tokens, 0)
    other = swap(lax.dynamic_slice_in_dim(part, (1 - side) * tokens, tokens, 0))
    low = side == 0
    return jnp.concatenate([jnp.where(low, keep, other), jnp.where(low, other, keep)], axis=1)


def own_features(part):
    half = part.shape[1] // 2
    side = lax.axis_index("hid")
    keep = lax.dynamic_slice_in_dim(part, side * half, half, 1)
    other = swap(lax.dynamic_slice_in_dim(part, (1 - side) * half, half, 1))
    low = side == 0
    return jnp.concatenate([jnp.where(low, keep, other), jnp.where(low, other, keep)], axis=0)


def padded_mixer(sz, mixer):
    layers, kinds, blocks, size, _ = mixer.shape
    chan_first = jnp.concatenate([jnp.swapaxes(mixer[:, :2], 3, 4), mixer[:, 2:]], axis=1)
    grouped = chan_first.reshape(layers, kinds, blocks, size // sz.chans, sz.chans, size)
    grouped = jnp.pad(grouped, ((0, 0),) * 4 + ((0, sz.piece - sz.chans), (0, 0)))
    grouped = grouped.reshape(layers, kinds, blocks, -1, size)
    parts = [
        jnp.pad(grouped[:, :, block], ((0, 0),) * 3 + ((block * size, (blocks - 1 - block) * size),))
        for block in range(blocks)
    ]
    return jnp.concatenate(parts, axis=2)


def padded_channels(sz, values):
    lead = values.shape[:-1]
    grouped = values.reshape(lead + (sz.rows, sz.chans))
    grouped = jnp.pad(grouped, ((0, 0),) * (len(lead) + 1) + ((0, sz.piece - sz.chans),))
    return grouped.reshape(lead + (sz.padded,))


def envelopes(sz):
    row = lax.axis_index("rows")
    first_chan = lax.axis_index("hid") * sz.half + row * sz.chans
    channels = first_chan + jnp.arange(sz.piece, dtype=jnp.int32)
    fraction = (channels * 37 % sz.width).astype(F32) / (sz.width - 1)
    start_log = math.log(1.0 / 40.0)
    rate = jnp.exp(start_log + (math.log(1.5 / sz.length) - start_log) * fraction)
    steps = jnp.arange(sz.length, dtype=jnp.int32).astype(F32)
    decay = jnp.exp(-steps[None, :] * rate[:, None])
    shape = decay * lax.rsqrt(2.0 * jnp.sum(decay * decay, axis=1, keepdims=True))
    return jnp.concatenate([shape, shape * (steps > 0)[None, :]], axis=0)


def plane_gather(value):
    size = lax.axis_size("rows")
    for bit in (1, 2):
        other = lax.ppermute(value, "rows", [(r, r ^ bit) for r in range(size)])
        value = jnp.concatenate([value, other], axis=0)
    return jnp.concatenate([value, swap(value)], axis=0)


def on_device(hidden_in, d_out, gains, mixer, skip, filters, gate_up, down):
    layers = gate_up.shape[0]
    rows = lax.axis_size("rows")
    hid = lax.axis_size("hid")
    width = gate_up.shape[2]
    hidden = gate_up.shape[3] * hid
    blocks = mixer.shape[2] * hid
    block_size = mixer.shape[3]
    sz = Sizes(rows, hid, width, hidden, hidden_in.shape[0] * rows)
    row = lax.axis_index("rows")

    x = own_tokens(hidden_in)
    gains_all = both_halves(gains, 2)
    skip_all = both_halves(padded_channels(sz, skip), 1)[:, :, None]
    weights = both_halves(padded_mixer(sz, mixer)[:, :, None], 2)
    gate_up_b = swap(gate_up)
    down_b = swap(down)
    ff = (gate_up, down, gate_up_b, down_b)
    grad_out = own_tokens(d_out)

    tables = dft_tables(sz.length)
    pos = jnp.asarray(position_table(sz.length).T, F32).astype(BF16)
    env = envelopes(sz)
    taps = lax.dynamic_slice_in_dim(filters, row * sz.chans, sz.chans, 3)
    taps = jnp.pad(taps, ((0, 0),) * 3 + ((0, sz.piece - sz.chans),))
    taps = jnp.swapaxes(taps, 2, 3).reshape(layers, 2 * sz.piece, ORDER).astype(BF16)

    normed, inner, gate = first(sz, x, gains_all[0], weights[0, 0], weights[0, 1])
    stored = []
    for layer in range(layers):
        conv, filt_spec, sig_spec = conv_forward(sz, inner, taps[layer], pos, env, tables, 0)
        stored.append(dict(x=x, normed=normed, inner=inner, gate=gate, f=filt_spec, s=sig_spec))
        if layer < layers - 1:
            summed, mixed, middle, normed_two, x, normed, next_inner, next_gate = forward(
                sz,
                layer,
                conv,
                inner,
                gate,
                skip_all[layer],
                x,
                gains_all[layer],
                gains_all[layer + 1],
                weights[layer, 2],
                weights[layer + 1, 0],
                weights[layer + 1, 1],
                ff,
            )
            stored[-1].update(summed=summed, mixed=mixed, middle=middle, normed_two=normed_two)
            inner, gate = next_inner, next_gate

    top = layers - 1
    hidden_out, normed_two, *rest = turn(
        sz,
        top,
        blocks,
        conv,
        inner,
        gate,
        skip_all[top],
        x,
        gains_all[top],
        grad_out,
        weights[top, 2],
        ff,
    )
    stored[top].update(normed_two=normed_two)
    grad_ff = grad_out
    units = sz.hidden // hid // 4
    unit_start = lax.rem(row, 4) * units
    ff_parts, mixer_parts, gain_parts, skip_parts, taps_parts = [], [], [], [], []
    for layer in reversed(range(layers)):
        kept = stored[layer]
        grad_middle, out_grad, grad_gate, grad_summed, grad_conv, gain_two = rest
        ff_parts.insert(
            0,
            ff_grads(
                plane_gather(kept["normed_two"]),
                plane_gather(grad_ff),
                lax.dynamic_slice_in_dim(gate_up[layer], unit_start, units, 2),
                lax.dynamic_slice_in_dim(down[layer], unit_start, units, 1),
            ),
        )
        back, taps_grad = conv_backward(
            sz, grad_conv, kept["f"], kept["s"], taps[layer], pos, env, tables, 1
        )
        skip_parts.insert(0, jnp.sum(grad_summed * kept["inner"].astype(F32), axis=1))
        taps_parts.insert(0, taps_grad)
        common = (
            back,
            grad_summed,
            grad_gate,
            skip_all[layer],
            kept["normed"],
            kept["x"],
            gains_all[layer],
            weights[layer, 0],
            weights[layer, 1],
            grad_middle,
        )
        if layer > 0:
            low = stored[layer - 1]
            in_grad, gain_one, grad_ff, *rest = backward(
                sz,
                layer - 1,
                blocks,
                *common,
                low["normed_two"],
                low["middle"],
                low["summed"],
                low["gate"],
                low["mixed"],
                gains_all[layer - 1],
                weights[layer - 1, 2],
                ff,
            )
        else:
            in_grad, gain_one, grad_in = last(sz, blocks, *common)
        mixer_parts.insert(0, jnp.concatenate([in_grad, out_grad], axis=0))
        gain_parts.insert(0, jnp.concatenate([gain_one, gain_two], axis=0))

    piece_rows = width // rows
    padded_rows = round_up(piece_rows, 16)
    pieces = jnp.stack(ff_parts).reshape(layers, 3, rows, piece_rows, units)
    pieces = jnp.pad(pieces, ((0, 0),) * 3 + ((0, padded_rows - piece_rows), (0, 0)))
    pieces = jnp.moveaxis(pieces, 2, 0)
    (arrived,) = row_exchange((pieces,), rows, 2)
    arrived = arrived.reshape(rows // 4, 4, layers, 3, padded_rows, units)[:, :, :, :, :piece_rows]
    summed_ff = jnp.sum(arrived.astype(F32), axis=0)
    summed_ff = jnp.moveaxis(summed_ff, 0, 3).reshape(layers, 3, piece_rows, 4 * units)

    mixers = jnp.stack(mixer_parts).reshape(layers, 3, blocks, -1, sz.piece, block_size)
    mixers = mixers[:, :, :, :, : sz.chans].reshape(layers, 3, blocks, block_size, block_size)
    small = jnp.concatenate(
        [jnp.stack(gain_parts).reshape(-1), jnp.stack(skip_parts).reshape(-1)]
    )
    mixers, small = lax.psum((mixers.astype(F32), small), ("rows", "hid"))
    side = lax.axis_index("hid")
    mixers = lax.dynamic_slice_in_dim(mixers, side * (blocks // hid), blocks // hid, 2)
    mixers = jnp.concatenate([jnp.swapaxes(mixers[:, :2], 3, 4), mixers[:, 2:]], axis=1)
    gain_size = layers * 2 * width
    gain_out = lax.dynamic_slice_in_dim(
        small[:gain_size].reshape(layers, 2, width), side * sz.half, sz.half, 2
    )
    skip_out = small[gain_size:].reshape(layers, hid, rows, sz.piece)[..., : sz.chans]
    skip_out = lax.dynamic_index_in_dim(skip_out, side, 1, False).reshape(layers, sz.half)
    taps_out = jnp.stack(taps_parts).reshape(layers, 2, sz.piece, ORDER)[:, :, : sz.chans]
    taps_out = lax.all_gather(taps_out, "rows", axis=2, tiled=True)
    return (
        own_features(hidden_out),
        own_features(grad_in),
        gain_out,
        mixers,
        skip_out,
        jnp.swapaxes(taps_out, 2, 3),
        summed_ff[:, :2],
        summed_ff[:, 2],
    )


def solution(mesh):
    placed = (
        P("rows", "hid"),
        P("rows", "hid"),
        P(None, None, "hid"),
        P(None, None, "hid", None, None),
        P(None, "hid"),
        P(None, None, None, "hid"),
        P(None, None, None, "hid"),
        P(None, None, "hid"),
    )
    return jax.shard_map(
        on_device,
        mesh=mesh,
        in_specs=placed,
        out_specs=(
            P("rows", "hid"),
            P("rows", "hid"),
            P(None, None, "hid"),
            P(None, None, "hid", None, None),
            P(None, "hid"),
            P(None, None, None, "hid"),
            P(None, None, "rows", "hid"),
            P(None, "rows", "hid"),
        ),
        check_vma=False,
    )
```

time: 1070 us -> 526 us (0.49)
  waiting for transfers between devices: 556 us -> 112 us
  Pallas kernels: 0 us -> 213 us
  matrix products: 187 us -> 0 us
  local copies, waits for them, and re-layouts: 114 us -> 38.9 us
  starting transfers between devices: 50.2 us -> 12.8 us
  other arithmetic: 59.5 us -> 40.6 us
  blocking collectives: 72.9 us -> 88.3 us
    reduce_scatter x2 -> x0, waiting for transfers between devices: 468 us -> none  [the longest x1 290 us: on_device(): lax.psum_scatter(large_stacked[0], 'rows', scatter_dimension=2, tiled=True)]
    pallas_call x0 -> x12, Pallas kernels: none -> 213 us  [the longest x1 71 us: row_exchange(): pl.pallas_call(functools.partial(row_exchange_kernel, rows, parts), out_s...]
    dot_general x112 -> x0, matrix products: 187 us -> none  [the longest x6 14.1 us: inverse_dft(): jnp.einsum('...kj,mj->...km', imag_c, sin_inner, precision=exact)]
    unnamed x238 -> x103, local copies, waits for them, and re-layouts: 81 us -> 8.61 us
    all_to_all x8 -> x0, starting transfers between devices: 49.6 us -> none  [the longest x2 14.5 us: layer_forward(): lax.all_to_all(inner_rows.T, 'rows', split_axis=0, concat_axis=1, tiled=T...]
    ppermute x0 -> x21, waiting for transfers between devices: none -> 38.5 us  [the longest x8 37.8 us: plane_gather(): other = lax.ppermute(value, 'rows', [(r, r ^ bit) for r in range(size)])]
    all_gather x4 -> x1, blocking collectives: 10.4 us -> 47.8 us  [on_device(): taps_out = lax.all_gather(taps_out, 'rows', axis=2, tiled=True)]
    another operation x12 -> x5, other arithmetic: 24.2 us -> 0.8 us  [the longest x1 0.77 us: on_device(): jnp.stack(mixer_parts).reshape(layers, 3, blocks, -1, sz.piece, block_size)]
  transfers between devices with their start and end apart: 15 -> 22, of which waited for: 11 -> 7; matrix products, arithmetic and copies ran while one was open for 18% -> 13% of each run, Pallas kernels for 0% -> 39%
where the time goes in v1:
time: 526 us; the launch traced here: 521 us
  Pallas kernels  213 us (40%)
  waiting for transfers between devices  112 us (21%)
  blocking collectives  88.3 us (17%)
  other arithmetic  40.6 us (8%)
  local copies, waits for them, and re-layouts  38.9 us (7%)
  between operations  15.3 us (3%)
  starting transfers between devices  12.8 us (2%)
    psum x1, waiting for transfers between devices, on_device(): mixers, small = lax.psum((mixers.astype(F32), small), ('rows', 'hid'))  73.7 us
    pallas_call x1, Pallas kernels, row_exchange(): pl.pallas_call(functools.partial(row_exchange_kernel, rows, parts), out_s...  71 us
    all_gather x1, blocking collectives, on_device(): taps_out = lax.all_gather(taps_out, 'rows', axis=2, tiled=True)  47.8 us
    pallas_call x2, Pallas kernels, conv_backward(): pl.pallas_call(functools.partial(conv_backward_kernel, sz), out_shape=(ja...  45 us
    pallas_call x2, Pallas kernels, conv_forward(): pl.pallas_call(functools.partial(conv_forward_kernel, sz), out_shape=(jax...  44.5 us
    psum x1, blocking collectives, on_device(): mixers, small = lax.psum((mixers.astype(F32), small), ('rows', 'hid'))  40.4 us
    ppermute x8, waiting for transfers between devices, plane_gather(): other = lax.ppermute(value, 'rows', [(r, r ^ bit) for r in range(size)])  37.8 us
    pallas_call x1, Pallas kernels, backward(): pl.pallas_call(functools.partial(backward_kernel, sz, steps), grid=(2 * s...  14.1 us
  transfers between devices with their start and end apart: 22, of which 7 were waited for; matrix products, arithmetic and copies ran while one was open for 13% of the time, Pallas kernels for 39%

profile of v1, /device:TPU:0, one launch (start us, length us, event | category | flops | bytes accessed | tf_op | source)
XLA Modules:
  0.0 520.9 jit_solution(11229542524807578396)
XLA Ops:
  13.0 3.0 fusion.3
  17.0 6.5 %fusion.27 = (bf16[1,2,768,1536]{3,2,1,0:T(8,128)(2,1)S(1)}, bf16[1,2,768,1536]{3,2,1,0:T(8,128)(2,1)}) fusion(bf16[2,2,768,1536]{3,2,1,0:T(8,128)(2,1)} %up_a.5), kind=kLoop, calls=%fused_computation.119 | loop fusion | bytes 18874368 | tf_op jit(solution)/shard_map/slice | solution.py:1168
  23.5 1.1 dynamic-slice_bitcast_fusion.2.up_ref
  24.7 2.7 fusion.28
  30.0 1.7 broadcast_select_fusion.5
  31.7 2.7 collective-permute-start.18
  36.4 2.4 dynamic-slice_bitcast_fusion.1.up_ref
  38.8 1.2 collective-permute-done.18
  40.9 1.8 collective-permute-start.19
  42.8 1.1 pad_maximum_fusion.10.env_ref
  43.9 7.9 %collective-permute-done.19 = bf16[256,768]{1,0:T(8,128)(2,1)S(1)} collective-permute-done((bf16[256,768]{1,0:T(8,128)(2,1)S(1)}, bf16[256,768]{1,0:T(8,128)(2,1)S(1)}, u32[]{:S(2)}, u32[]{:S(2)}) %collective-permute-start.19) | collective-permute-done | bytes 393248 | tf_op jit(solution)/shard_map/ppermute | solution.py:1084
  51.8 1.1 pad_maximum_fusion.15
  53.4 1.1 copy.61.skip_ref
  55.4 1.4 pad_maximum_fusion.8.grad_ref
  56.8 3.1 broadcast_select_fusion
  60.0 1.3 fusion.14
  62.1 1.2 copy-done.2
  63.3 22.1 %conv_forward.2 = (bf16[1024,128]{1,0:T(8,128)(2,1)S(1)}, f32[1536,256]{1,0:T(8,128)S(1)}, f32[3072,256]{1,0:T(8,128)}) custom-call(bf16[1024,128]{1,0:T(8,128)(2,1)S(1)} %get-tuple-element.49.inner_ref, bf16[64,128]{1,0:T(8,128)(2,1)S(1)} %bitcast.80, bf16[128,4096]{1,0:T(8,128)(2,1)S(1)} %copy-done.2, f32[64,4096]{1,0:T(8,128)S(1)} %pad_maximum_fusion.10.env_ref, ...), custom_call_target="tpu_custom_call" | custom-call | tf_op jit(solution)/shard_map/conv_forward/pallas_call | solution.py:289
  85.5 1.1 copy-done.17
  86.6 10.6 %token_forward.1 = (f32[1024,128]{1,0:T(8,128)S(1)}, bf16[1024,128]{1,0:T(8,128)(2,1)S(1)}, f32[128,768]{1,0:T(8,128)S(1)}, bf16[128,768]{1,0:T(8,128)(2,1)S(1)}...) custom-call(bf16[1024,128]{1,0:T(8,128)(2,1)S(1)} %get-tuple-element, ...), custom_call_target="tpu_custom_call" | custom-call | tf_op jit(solution)/shard_map/token_forward/pallas_call | solution.py:559
  98.4 22.4 %conv_forward.3 = (bf16[1024,128]{1,0:T(8,128)(2,1)S(1)}, f32[1536,256]{1,0:T(8,128)S(1)}, f32[3072,256]{1,0:T(8,128)}) custom-call(bf16[1024,128]{1,0:T(8,128)(2,1)S(1)} %get-tuple-element.52.inner_ref, bf16[64,128]{1,0:T(8,128)(2,1)S(1)} %bitcast.82, bf16[128,4096]{1,0:T(8,128)(2,1)S(1)} %copy-done.2, f32[64,4096]{1,0:T(8,128)S(1)} %pad_maximum_fusion.10.env_ref, ...), custom_call_target="tpu_custom_call" | custom-call | tf_op jit(solution)/shard_map/conv_forward/pallas_call | solution.py:289
  120.7 13.1 %token_turn.1 = (bf16[128,768]{1,0:T(8,128)(2,1)S(1)}, bf16[128,768]{1,0:T(8,128)(2,1)S(1)}, f32[128,768]{1,0:T(8,128)S(1)}, bf16[1,4,256,192]{3,2,1,0:T(8,128)(...) custom-call(bf16[1024,128]{1,0:T(8,128)(2,1)S(1)} %get-tuple-element, ...), custom_call_target="tpu_custom_call" | custom-call | tf_op jit(solution)/shard_map/token_turn/pallas_call | solution.py:698
  134.7 22.4 %conv_backward.2 = (bf16[1024,128]{1,0:T(8,128)(2,1)S(1)}, f32[64,128]{1,0:T(8,128)S(1)}) custom-call(bf16[1024,128]{1,0:T(8,128)(2,1)S(1)} %get-tuple-element.57.grad_ref, f32[1536,256]{1,0:T(8,128)S(1)} %get-tuple-element.58.filt_spec, f32[3072,256]{1,0:T(8,128)} %get-tuple-element.59.sig_spec, bf16[64,128]{1,0:T(8,128)(2,1)S(1)} %bitcast.83, ...), custom_call_target="tpu_custom_call" | custom-call | tf_op jit(solution)/shard_map/conv_backward/pallas_call | solution.py:405
  157.2 14.1 %token_backward.1 = (bf16[2,4,256,192]{3,2,1,0:T(8,128)(2,1)}, f32[1,768]{1,0:T(1,128)S(1)}, bf16[128,768]{1,0:T(8,128)(2,1)S(1)}, f32[128,768]{1,0:T(8,128)S(1)...) custom-call(bf16[1024,128]{1,0:T(8,128)(2,1)S(1)} %get-tuple-element, ...), custom_call_target="tpu_custom_call" | custom-call | tf_op jit(solution)/shard_map/token_backward/pallas_call | solution.py:866
  172.1 22.6 %conv_backward.3 = (bf16[1024,128]{1,0:T(8,128)(2,1)S(1)}, f32[64,128]{1,0:T(8,128)S(1)}) custom-call(bf16[1024,128]{1,0:T(8,128)(2,1)S(1)} %get-tuple-element.69.grad_ref, f32[1536,256]{1,0:T(8,128)S(1)} %copy-done.18, f32[3072,256]{1,0:T(8,128)} %get-tuple-element.71.sig_spec, bf16[64,128]{1,0:T(8,128)(2,1)S(1)} %bitcast.81, ...), custom_call_target="tpu_custom_call" | custom-call | tf_op jit(solution)/shard_map/conv_backward/pallas_call | solution.py:405
  196.6 40.4 %psum.14 = f32[5120]{0:T(1024)S(1)} all-reduce(f32[5120]{0:T(1024)S(1)} %pad_maximum_fusion.25), channel_id=1, replica_groups=mesh['rows'=16,'hid'=2] {'rows','hid'}, use_global_device_ids=true, to_apply=%region_3.4 | all-reduce | flops 5120 | bytes 40960 | tf_op jit(solution)/shard_map/psum | solution.py:1225
  237.1 2.3 collective-permute-start.12
  239.4 47.8 %all_gather.3 = f32[2,2,384,128]{3,1,0,2:T(2,128)} all-gather(f32[2,2,24,128]{3,1,0,2:T(2,128)S(1)} %copy.74), channel_id=1, replica_groups=mesh['rows'=16,'hid'=2] {'rows'}, dimensions={2}, use_global_device_ids=true | all-gather | bytes 835584 | tf_op jit(solution)/shard_map/all_gather | solution.py:1236
  287.2 2.2 copy.71
  289.5 1.4 pad_maximum_fusion.3
  292.1 2.9 bitcast_convert_fusion
  298.7 2.1 collective-permute-start.10
  302.5 12.4 %collective-permute-done.13 = bf16[256,768]{1,0:T(8,128)(2,1)S(1)} collective-permute-done((bf16[256,768]{1,0:T(8,128)(2,1)S(1)}, bf16[256,768]{1,0:T(8,128)(2,1)S(1)}, u32[]{:S(2)}, u32[]{:S(2)}) %collective-permute-start.13) | collective-permute-done | bytes 393248 | tf_op jit(solution)/shard_map/ppermute | solution.py:1084
  316.0 9.1 %collective-permute-done.10 = bf16[256,768]{1,0:T(8,128)(2,1)S(1)} collective-permute-done((bf16[256,768]{1,0:T(8,128)(2,1)S(1)}, bf16[256,768]{1,0:T(8,128)(2,1)S(1)}, u32[]{:S(2)}, u32[]{:S(2)}) %collective-permute-start.10) | collective-permute-done | bytes 393248 | tf_op jit(solution)/shard_map/ppermute | solution.py:1084
  326.1 7.2 %collective-permute-done.16 = bf16[256,768]{1,0:T(8,128)(2,1)S(1)} collective-permute-done((bf16[256,768]{1,0:T(8,128)(2,1)S(1)}, bf16[256,768]{1,0:T(8,128)(2,1)S(1)}, u32[]{:S(2)}, u32[]{:S(2)}) %collective-permute-start.16) | collective-permute-done | bytes 393248 | tf_op jit(solution)/shard_map/ppermute | solution.py:1084
  337.0 1.2 pad_maximum_fusion.5.normed_ref
  338.5 6.4 %ff_weight_grads.2 = bf16[3,768,384]{2,1,0:T(8,128)(2,1)} custom-call(bf16[1024,768]{1,0:T(8,128)(2,1)S(1)} %pad_maximum_fusion.5.normed_ref, bf16[1024,768]{1,0:T(8,128)(2,1)S(1)} %pad_maximum_fusion.6.grad_ref, bf16[2,768,384]{2,1,0:T(8,128)(2,1)S(1)} %copy-done.6, bf16[768,384]{1,0:T(8,128)(2,1)S(1)} %copy-done.8), custom_call_target="tpu_custom_call" | custom-call | tf_op jit(solution)/shard_map/ff_weight_grads/pallas_call | solution.py:949
  344.9 1.2 pad_maximum_fusion.7.normed_ref
  346.4 6.6 %ff_weight_grads.3 = bf16[3,768,384]{2,1,0:T(8,128)(2,1)} custom-call(bf16[1024,768]{1,0:T(8,128)(2,1)S(1)} %pad_maximum_fusion.7.normed_ref, bf16[1024,768]{1,0:T(8,128)(2,1)S(1)} %pad_maximum_fusion.8.grad_ref, bf16[2,768,384]{2,1,0:T(8,128)(2,1)S(1)} %copy-done.7, bf16[768,384]{1,0:T(8,128)(2,1)S(1)} %copy-done.9), custom_call_target="tpu_custom_call" | custom-call | tf_op jit(solution)/shard_map/ff_weight_grads/pallas_call | solution.py:949
  353.0 3.7 copy_bitcast_fusion.refs_0_
  356.7 71.0 %row_exchange.1 = bf16[16,2,3,48,384]{4,3,2,1,0:T(8,128)(2,1)} custom-call(bf16[16,2,3,48,384]{4,3,2,1,0:T(8,128)(2,1)} %copy_bitcast_fusion.refs_0_), custom_call_target="tpu_custom_call" | custom-call | tf_op jit(solution)/shard_map/row_exchange/pallas_call | solution.py:1009
  427.7 2.7 convert_reduce_fusion
  430.6 1.1 slice.163
  432.6 73.7 %all-reduce.7.cloned.1.call-done = f32[2,3,4,192,192]{4,3,2,1,0:T(8,128)} async-done(((f32[2,3,4,192,192]{4,3,2,1,0:T(8,128)}), f32[2,3,4,192,192]{4,3,2,1,0:T(8,128)}) %all-reduce.7.cloned.1.call-update) | async-done | bytes 3538960 | tf_op jit(solution)/shard_map/psum | solution.py:1225
  506.3 2.7 dynamic-slice_bitcast_fusion
  508.9 2.0 copy.66
  510.9 1.3 constant_dynamic-slice_fusion.1
  512.2 1.6 pad_maximum_fusion.2
  (205 shorter events, 32.9 us)
Async XLA Ops:
  7.2 9.4 %copy-start = (f32[2,2,128,384]{3,2,1,0:T(8,128)S(1)}, f32[2,2,128,384]{3,2,1,0:T(8,128)}, u32[]{:S(2)}) copy-start(f32[2,2,128,384]{3,2,1,0:T(8,128)} %param.19) | copy-start | bytes 2359300
  7.2 3.4 slice-start.1
  7.2 499.1 %all-reduce.7.cloned.1.call-start = ((), (), s32[]{:S(2)}) async-start(), calls=%async_computation | async-start | bytes 9437184 | tf_op jit(solution)/shard_map/psum | solution.py:1225
  7.3 79.3 %collective-permute-start.4 = (bf16[2,2,768,1536]{3,2,1,0:T(8,128)(2,1)}, bf16[2,2,768,1536]{3,2,1,0:T(8,128)(2,1)}, u32[]{:S(2)}, u32[]{:S(2)}) collective-permute-start(bf16[2,2,768,1536]{3,2,1,0:T(8,128)(2,1)} %up_a.5), channel_id=1, source_target_pairs={{0,1},{1,0},{2,3},{3,2},{4,5},{5,4},{6,7},{7,6},{8,9},{9,8},{10,11... | collective-permute-start | bytes 28311560 | tf_op jit(solution)/shard_map/ppermute | solution.py:1021
  8.7 20.7 %collective-permute-start = (bf16[128,384]{1,0:T(8,128)(2,1)S(1)}, bf16[128,384]{1,0:T(8,128)(2,1)S(1)}, u32[]{:S(2)}, u32[]{:S(2)}) collective-permute-start(bf16[128,384]{1,0:T(8,128)(2,1)S(1)} %constant_dynamic-slice_fusion.6), channel_id=1, source_target_pairs={{0,1},{1,0},{2,3},{3,2},{4,5},{5,4},{6,7},{7,6},{8,9},{9,8},{10,11... | collective-permute-start | bytes 294920 | tf_op jit(solution)/shard_map/ppermute | solution.py:1021
  9.8 20.2 %collective-permute-start.6 = (bf16[128,384]{1,0:T(8,128)(2,1)S(1)}, bf16[128,384]{1,0:T(8,128)(2,1)}, u32[]{:S(2)}, u32[]{:S(2)}) collective-permute-start(bf16[128,384]{1,0:T(8,128)(2,1)S(1)} %constant_dynamic-slice_fusion.5), channel_id=1, source_target_pairs={{0,1},{1,0},{2,3},{3,2},{4,5},{5,4},{6,7},{7,6},{8,9},{9,8},{10,11... | collective-permute-start | bytes 294920 | tf_op jit(solution)/shard_map/ppermute | solution.py:1021
  16.0 40.8 %collective-permute-start.2 = (bf16[2,3,1,512,384]{4,3,2,1,0:T(8,128)(2,1)}, bf16[2,3,1,512,384]{4,3,2,1,0:T(8,128)(2,1)}, u32[]{:S(2)}, u32[]{:S(2)}) collective-permute-start(bf16[2,3,1,512,384]{4,3,2,1,0:T(8,128)(2,1)} %fusion.3), channel_id=1, source_target_pairs={{0,1},{1,0},{2,3},{3,2},{4,5},{5,4},{6,7},{7,6},{8,9},{9,8},{10,11... | collective-permute-start | bytes 7077896 | tf_op jit(solution)/shard_map/ppermute | solution.py:1021
  16.2 70.4 %collective-permute-start.5 = (bf16[2,768,1536]{2,1,0:T(8,128)(2,1)}, bf16[2,768,1536]{2,1,0:T(8,128)(2,1)}, u32[]{:S(2)}, u32[]{:S(2)}) collective-permute-start(bf16[2,768,1536]{2,1,0:T(8,128)(2,1)} %down_a.5), channel_id=1, source_target_pairs={{0,1},{1,0},{2,3},{3,2},{4,5},{5,4},{6,7},{7,6},{8,9},{9,8},{10,11... | collective-permute-start | bytes 14155784 | tf_op jit(solution)/shard_map/ppermute | solution.py:1021
  29.3 25.4 %collective-permute-start.1 = (f32[2,2,384]{2,1,0:T(2,128)S(1)}, f32[2,2,384]{2,1,0:T(2,128)S(1)}, u32[]{:S(2)}, u32[]{:S(2)}) collective-permute-start(f32[2,2,384]{2,1,0:T(2,128)S(1)} %copy-done.48), channel_id=1, source_target_pairs={{0,1},{1,0},{2,3},{3,2},{4,5},{5,4},{6,7},{7,6},{8,9},{9,8},{10,11... | collective-permute-start | bytes 18440 | tf_op jit(solution)/shard_map/ppermute | solution.py:1021
  31.7 11.0 %copy-start.20 = (bf16[128,768]{1,0:T(8,128)(2,1)}, bf16[128,768]{1,0:T(8,128)(2,1)S(1)}, u32[]{:S(2)}) copy-start(bf16[128,768]{1,0:T(8,128)(2,1)S(1)} %pad_maximum_fusion.22.grad_ref) | copy-start | bytes 589828
  31.7 8.2 %collective-permute-start.18 = (bf16[128,768]{1,0:T(8,128)(2,1)S(1)}, bf16[128,768]{1,0:T(8,128)(2,1)}, u32[]{:S(2)}, u32[]{:S(2)}) collective-permute-start(bf16[128,768]{1,0:T(8,128)(2,1)S(1)} %pad_maximum_fusion.22.grad_ref), channel_id=1, source_target_pairs={{0,2},{2,0},{4,6},{6,4},{8,10},{10,8},{12,14},{14,12},{16,18},{18,... | collective-permute-start | bytes 589832 | tf_op jit(solution)/shard_map/ppermute | solution.py:1084
  36.3 62.0 %copy-start.34 = (bf16[1,2,32,128]{3,2,1,0:T(8,128)(2,1)}, bf16[1,2,32,128]{3,2,1,0:T(8,128)(2,1)S(1)}, u32[]{:S(2)}) copy-start(bf16[1,2,32,128]{3,2,1,0:T(8,128)(2,1)S(1)} %copy.62) | copy-start | bytes 49156
  40.9 10.9 %collective-permute-start.19 = (bf16[256,768]{1,0:T(8,128)(2,1)S(1)}, bf16[256,768]{1,0:T(8,128)(2,1)S(1)}, u32[]{:S(2)}, u32[]{:S(2)}) collective-permute-start(bf16[256,768]{1,0:T(8,128)(2,1)S(1)} %pad_maximum_fusion.20), channel_id=1, source_target_pairs={{0,4},{2,6},{4,0},{6,2},{8,12},{10,14},{12,8},{14,10},{16,20},{18,... | collective-permute-start | bytes 1179656 | tf_op jit(solution)/shard_map/ppermute | solution.py:1084
  42.8 12.0 %copy-start.43 = (bf16[128,384]{1,0:T(8,128)(2,1)S(1)}, bf16[128,384]{1,0:T(8,128)(2,1)}, u32[]{:S(2)}) copy-start(bf16[128,384]{1,0:T(8,128)(2,1)} %get-tuple-element.157) | copy-start | bytes 294916
  51.8 1.2 collective-permute-start.3
  53.0 2.5 collective-permute-start.20
  61.3 35.9 %copy-start.3 = (bf16[2,512,384]{2,1,0:T(8,128)(2,1)}, bf16[2,512,384]{2,1,0:T(8,128)(2,1)S(1)}, u32[]{:S(2)}) copy-start(bf16[2,512,384]{2,1,0:T(8,128)(2,1)S(1)} %get-tuple-element.129.w_out) | copy-start | bytes 2359300
  61.3 35.9 %copy-start.4 = (bf16[2,512,384]{2,1,0:T(8,128)(2,1)}, bf16[2,512,384]{2,1,0:T(8,128)(2,1)S(1)}, u32[]{:S(2)}) copy-start(bf16[2,512,384]{2,1,0:T(8,128)(2,1)S(1)} %get-tuple-element.130.w_in) | copy-start | bytes 2359300
  61.3 25.3 %copy-start.5 = (f32[1024,1]{1,0:T(8,128)S(1)}, f32[1024,1]{1,0:T(8,128)}, u32[]{:S(2)}) copy-start(f32[1024,1]{1,0:T(8,128)} %copy.61.skip_ref) | copy-start | bytes 12292
  62.0 35.2 %copy-start.10 = (f32[1024,128]{1,0:T(8,128)}, f32[1024,128]{1,0:T(8,128)S(1)}, u32[]{:S(2)}) copy-start(f32[1024,128]{1,0:T(8,128)S(1)} %get-tuple-element.51.gate_ref) | copy-start | bytes 1572868
  97.3 23.4 %copy-start.22 = (f32[1024,128]{1,0:T(8,128)}, f32[1024,128]{1,0:T(8,128)S(1)}, u32[]{:S(2)}) copy-start(f32[1024,128]{1,0:T(8,128)S(1)} %get-tuple-element.67.summed_ref) | copy-start | bytes 1572868
  97.3 36.5 %copy-start.15 = (f32[128,768]{1,0:T(8,128)}, f32[128,768]{1,0:T(8,128)S(1)}, u32[]{:S(2)}) copy-start(f32[128,768]{1,0:T(8,128)S(1)} %get-tuple-element.55.x_ref) | copy-start | bytes 1179652
  97.3 36.5 %copy-start.28 = (f32[128,768]{1,0:T(8,128)}, f32[128,768]{1,0:T(8,128)S(1)}, u32[]{:S(2)}) copy-start(f32[128,768]{1,0:T(8,128)S(1)} %get-tuple-element.66.middle_ref) | copy-start | bytes 1179652
  97.3 23.4 %copy-start.21 = (bf16[128,768]{1,0:T(8,128)(2,1)S(1)}, bf16[128,768]{1,0:T(8,128)(2,1)}, u32[]{:S(2)}) copy-start(bf16[128,768]{1,0:T(8,128)(2,1)} %copy-done.20) | copy-start | bytes 589828
  97.3 200.4 %collective-permute-start.9 = (bf16[128,768]{1,0:T(8,128)(2,1)S(1)}, bf16[128,768]{1,0:T(8,128)(2,1)}, u32[]{:S(2)}, u32[]{:S(2)}) collective-permute-start(bf16[128,768]{1,0:T(8,128)(2,1)S(1)} %get-tuple-element.65.normed_two), channel_id=1, source_target_pairs={{0,2},{2,0},{4,6},{6,4},{8,10},{10,8},{12,14},{14,12},{16,18},{18,... | collective-permute-start | bytes 589832 | tf_op jit(solution)/shard_map/ppermute | solution.py:1084
  120.7 14.0 %copy-start.35 = (bf16[1,2,32,128]{3,2,1,0:T(8,128)(2,1)S(1)}, bf16[1,2,32,128]{3,2,1,0:T(8,128)(2,1)}, u32[]{:S(2)}) copy-start(bf16[1,2,32,128]{3,2,1,0:T(8,128)(2,1)} %copy-done.34) | copy-start | bytes 49156
  133.8 23.3 %copy-start.32 = (bf16[128,768]{1,0:T(8,128)(2,1)}, bf16[128,768]{1,0:T(8,128)(2,1)S(1)}, u32[]{:S(2)}) copy-start(bf16[128,768]{1,0:T(8,128)(2,1)S(1)} %get-tuple-element.56) | copy-start | bytes 589828
  134.7 22.5 %copy-start.16 = (f32[128,768]{1,0:T(8,128)S(1)}, f32[128,768]{1,0:T(8,128)}, u32[]{:S(2)}) copy-start(f32[128,768]{1,0:T(8,128)} %copy-done.15) | copy-start | bytes 1179652
  134.7 22.5 %copy-start.23 = (f32[1024,128]{1,0:T(8,128)S(1)}, f32[1024,128]{1,0:T(8,128)}, u32[]{:S(2)}) copy-start(f32[1024,128]{1,0:T(8,128)} %copy-done.22) | copy-start | bytes 1572868
  134.7 22.5 %copy-start.29 = (f32[128,768]{1,0:T(8,128)S(1)}, f32[128,768]{1,0:T(8,128)}, u32[]{:S(2)}) copy-start(f32[128,768]{1,0:T(8,128)} %copy-done.28) | copy-start | bytes 1179652
  157.2 14.2 %copy-start.37 = (f32[64,128]{1,0:T(8,128)}, f32[64,128]{1,0:T(8,128)S(1)}, u32[]{:S(2)}) copy-start(f32[64,128]{1,0:T(8,128)S(1)} %get-tuple-element.87) | copy-start | bytes 98308
  157.2 14.9 %copy-start.18 = (f32[1536,256]{1,0:T(8,128)S(1)}, f32[1536,256]{1,0:T(8,128)}, u32[]{:S(2)}) copy-start(f32[1536,256]{1,0:T(8,128)} %copy-done.17) | copy-start | bytes 4718596
  171.4 23.4 %copy-start.13 = (bf16[128,768]{1,0:T(8,128)(2,1)}, bf16[128,768]{1,0:T(8,128)(2,1)S(1)}, u32[]{:S(2)}) copy-start(bf16[128,768]{1,0:T(8,128)(2,1)S(1)} %get-tuple-element.88) | copy-start | bytes 589828
  194.8 44.6 %copy-start.38 = (f32[64,128]{1,0:T(8,128)S(1)}, f32[64,128]{1,0:T(8,128)}, u32[]{:S(2)}) copy-start(f32[64,128]{1,0:T(8,128)} %copy-done.37) | copy-start | bytes 98308
  194.8 42.3 %copy-start.14 = (bf16[128,768]{1,0:T(8,128)(2,1)S(1)}, bf16[128,768]{1,0:T(8,128)(2,1)}, u32[]{:S(2)}) copy-start(bf16[128,768]{1,0:T(8,128)(2,1)} %copy-done.13) | copy-start | bytes 589828
  237.0 53.9 %copy-start.46 = (f32[5120]{0:T(1024)}, f32[5120]{0:T(1024)S(1)}, u32[]{:S(2)}) copy-start(f32[5120]{0:T(1024)S(1)} %psum.14) | copy-start | bytes 61444
  237.1 59.6 %collective-permute-start.12 = (bf16[128,768]{1,0:T(8,128)(2,1)S(1)}, bf16[128,768]{1,0:T(8,128)(2,1)}, u32[]{:S(2)}, u32[]{:S(2)}) collective-permute-start(bf16[128,768]{1,0:T(8,128)(2,1)S(1)} %copy-done.14), channel_id=1, source_target_pairs={{0,2},{2,0},{4,6},{6,4},{8,10},{10,8},{12,14},{14,12},{16,18},{18,... | collective-permute-start | bytes 589832 | tf_op jit(solution)/shard_map/ppermute | solution.py:1084
  239.3 61.4 %collective-permute-start.15 = (bf16[128,768]{1,0:T(8,128)(2,1)S(1)}, bf16[128,768]{1,0:T(8,128)(2,1)}, u32[]{:S(2)}, u32[]{:S(2)}) collective-permute-start(bf16[128,768]{1,0:T(8,128)(2,1)S(1)} %get-tuple-element.89), channel_id=1, source_target_pairs={{0,2},{2,0},{4,6},{6,4},{8,10},{10,8},{12,14},{14,12},{16,18},{18,... | collective-permute-start | bytes 589832 | tf_op jit(solution)/shard_map/ppermute | solution.py:1084
  295.7 6.0 %copy-start.33 = (bf16[128,768]{1,0:T(8,128)(2,1)S(1)}, bf16[128,768]{1,0:T(8,128)(2,1)}, u32[]{:S(2)}) copy-start(bf16[128,768]{1,0:T(8,128)(2,1)} %copy-done.32) | copy-start | bytes 589828
  296.6 38.6 %collective-permute-start.8 = (f32[128,384]{1,0:T(8,128)S(1)}, f32[128,384]{1,0:T(8,128)S(1)}, u32[]{:S(2)}, u32[]{:S(2)}) collective-permute-start(f32[128,384]{1,0:T(8,128)S(1)} %constant_dynamic-slice_fusion.3), channel_id=1, source_target_pairs={{0,1},{1,0},{2,3},{3,2},{4,5},{5,4},{6,7},{7,6},{8,9},{9,8},{10,11... | collective-permute-start | bytes 589832 | tf_op jit(solution)/shard_map/ppermute | solution.py:1021
  297.6 17.3 %collective-permute-start.13 = (bf16[256,768]{1,0:T(8,128)(2,1)S(1)}, bf16[256,768]{1,0:T(8,128)(2,1)S(1)}, u32[]{:S(2)}, u32[]{:S(2)}) collective-permute-start(bf16[256,768]{1,0:T(8,128)(2,1)S(1)} %pad_maximum_fusion.18), channel_id=1, source_target_pairs={{0,4},{2,6},{4,0},{6,2},{8,12},{10,14},{12,8},{14,10},{16,20},{18,... | collective-permute-start | bytes 1179656 | tf_op jit(solution)/shard_map/ppermute | solution.py:1084
  298.7 26.4 %collective-permute-start.10 = (bf16[256,768]{1,0:T(8,128)(2,1)S(1)}, bf16[256,768]{1,0:T(8,128)(2,1)S(1)}, u32[]{:S(2)}, u32[]{:S(2)}) collective-permute-start(bf16[256,768]{1,0:T(8,128)(2,1)S(1)} %pad_maximum_fusion.17), channel_id=1, source_target_pairs={{0,4},{2,6},{4,0},{6,2},{8,12},{10,14},{12,8},{14,10},{16,20},{18,... | collective-permute-start | bytes 1179656 | tf_op jit(solution)/shard_map/ppermute | solution.py:1084
  301.7 31.6 %collective-permute-start.16 = (bf16[256,768]{1,0:T(8,128)(2,1)S(1)}, bf16[256,768]{1,0:T(8,128)(2,1)S(1)}, u32[]{:S(2)}, u32[]{:S(2)}) collective-permute-start(bf16[256,768]{1,0:T(8,128)(2,1)S(1)} %pad_maximum_fusion.19), channel_id=1, source_target_pairs={{0,4},{2,6},{4,0},{6,2},{8,12},{10,14},{12,8},{14,10},{16,20},{18,... | collective-permute-start | bytes 1179656 | tf_op jit(solution)/shard_map/ppermute | solution.py:1084
  301.8 32.6 %collective-permute-start.7 = (bf16[128,384]{1,0:T(8,128)(2,1)S(1)}, bf16[128,384]{1,0:T(8,128)(2,1)S(1)}, u32[]{:S(2)}, u32[]{:S(2)}) collective-permute-start(bf16[128,384]{1,0:T(8,128)(2,1)S(1)} %constant_dynamic-slice_fusion.4), channel_id=1, source_target_pairs={{0,1},{1,0},{2,3},{3,2},{4,5},{5,4},{6,7},{7,6},{8,9},{9,8},{10,11... | collective-permute-start | bytes 294920 | tf_op jit(solution)/shard_map/ppermute | solution.py:1021
  315.9 20.1 %collective-permute-start.14 = (bf16[512,768]{1,0:T(8,128)(2,1)S(1)}, bf16[512,768]{1,0:T(8,128)(2,1)S(1)}, u32[]{:S(2)}, u32[]{:S(2)}) collective-permute-start(bf16[512,768]{1,0:T(8,128)(2,1)S(1)} %pad_maximum_fusion.13), channel_id=1, source_target_pairs={{0,1},{1,0},{2,3},{3,2},{4,5},{5,4},{6,7},{7,6},{8,9},{9,8},{10,11... | collective-permute-start | bytes 2359304 | tf_op jit(solution)/shard_map/ppermute | solution.py:1021
  326.0 11.0 %collective-permute-start.11 = (bf16[512,768]{1,0:T(8,128)(2,1)S(1)}, bf16[512,768]{1,0:T(8,128)(2,1)S(1)}, u32[]{:S(2)}, u32[]{:S(2)}) collective-permute-start(bf16[512,768]{1,0:T(8,128)(2,1)S(1)} %pad_maximum_fusion.12), channel_id=1, source_target_pairs={{0,1},{1,0},{2,3},{3,2},{4,5},{5,4},{6,7},{7,6},{8,9},{9,8},{10,11... | collective-permute-start | bytes 2359304 | tf_op jit(solution)/shard_map/ppermute | solution.py:1021
  334.3 10.6 %collective-permute-start.17 = (bf16[512,768]{1,0:T(8,128)(2,1)S(1)}, bf16[512,768]{1,0:T(8,128)(2,1)S(1)}, u32[]{:S(2)}, u32[]{:S(2)}) collective-permute-start(bf16[512,768]{1,0:T(8,128)(2,1)S(1)} %pad_maximum_fusion.14), channel_id=1, source_target_pairs={{0,1},{1,0},{2,3},{3,2},{4,5},{5,4},{6,7},{7,6},{8,9},{9,8},{10,11... | collective-permute-start | bytes 2359304 | tf_op jit(solution)/shard_map/ppermute | solution.py:1021
  346.4 6.6 %copy-start.39 = (bf16[3,768,384]{2,1,0:T(8,128)(2,1)S(1)}, bf16[3,768,384]{2,1,0:T(8,128)(2,1)}, u32[]{:S(2)}) copy-start(bf16[3,768,384]{2,1,0:T(8,128)(2,1)} %ff_weight_grads.2) | copy-start | bytes 5308420
  (27 other events, 45.5 us)
Sparse Core Ops, SparseCore 0:
  295.2 211.0 all-reduce.6

commit v2 on v1

--- a/solution.py
+++ b/solution.py
@@ -92,7 +92,1027 @@
     return value, slope
 
 
-def enter(count, hid):
+class Sizes:
+    def __init__(self, rows, hid, tokens, width, hidden, layers, blocks):
+        self.rows, self.hid, self.width, self.layers = rows, hid, width, layers
+        self.count = rows * hid
+        self.own = tokens // self.count
+        self.half = width // hid
+        self.units = hidden // hid
+        self.blocks = blocks
+        self.size = width // blocks
+        self.side_blocks = blocks // hid
+        self.chans = width // self.count
+        self.piece = round_up(self.chans, 16)
+        self.channels = self.count * self.piece
+        self.length = min(SEQ_LEN, tokens)
+        self.seqs = tokens // self.length
+        self.steps = self.length // LANES
+        self.outer = 2 * self.steps
+        self.pairs = self.seqs * self.chans
+        self.lines = max(self.chans, self.pairs)
+        self.group = 4
+        self.peers = rows // self.group
+        self.part = self.units // self.group
+        self.depth = width // rows
+        self.deep = round_up(self.depth, 16)
+        self.early = 3 * layers - 1
+        self.early_rows = round_up(-(-(self.early * self.size + 16) // rows), 16)
+        self.late_rows = round_up(-(-(self.size + 16) // rows), 16)
+        self.taps_rows = round_up(2 * self.chans + 1, 16)
+
+
+    @classmethod
+    def of(cls, hidden_in, d_out, gains, mixer, skip, filters, gate_up, down):
+        rows, hid = lax.axis_size("rows"), lax.axis_size("hid")
+        layers, _, width, units = gate_up.shape
+        tokens = hidden_in.shape[0] * rows
+        return cls(rows, hid, tokens, width, units * hid, layers, mixer.shape[2] * hid)
+
+
+class Links:
+    def __init__(self, sz, sems, local_sems):
+        self.sz, self.sems, self.local_sems = sz, sems, local_sems
+        self.used = 0
+        self.used_local = 0
+        self.row = lax.axis_index("rows")
+        self.col = lax.axis_index("hid")
+        self.plane = lax.rem(self.row, sz.peers)
+        self.line = self.row // sz.peers
+
+    def pair(self):
+        first = self.used
+        self.used += 2
+        return self.sems.at[first], self.sems.at[first + 1]
+
+    def copy(self, source, target, pair, row, col):
+        return pltpu.make_async_remote_copy(
+            src_ref=source,
+            dst_ref=target,
+            send_sem=pair[0],
+            recv_sem=pair[1],
+            device_id=(row, col),
+            device_id_type=MESH,
+        )
+
+    def sibling(self, source, target):
+        copy = self.copy(source, target, self.pair(), self.row, self.sz.hid - 1 - self.col)
+        copy.start()
+        return copy
+
+    def load(self, source, target):
+        copy = pltpu.make_async_copy(source, target, self.local_sems.at[self.used_local])
+        self.used_local += 1
+        copy.start()
+        return copy
+
+    def groups(self, count, me, row_of, source_of, target):
+        pair = self.pair()
+
+        def post(step, carry):
+            member = lax.rem(me + step, count)
+            self.copy(source_of(member), target, pair, row_of(member), self.col).start()
+            return carry
+
+        lax.fori_loop(1, count, post, 0)
+        return pair
+
+    def in_plane(self, source_of, target):
+        row_of = lambda member: self.line * self.sz.peers + member
+        return self.groups(self.sz.peers, self.plane, row_of, source_of, target)
+
+    def in_line(self, source_of, target):
+        row_of = lambda member: member * self.sz.peers + self.plane
+        return self.groups(self.sz.group, self.line, row_of, source_of, target)
+
+    def in_rows(self, source_of, target):
+        return self.groups(self.sz.rows, self.row, lambda member: member, source_of, target)
+
+    def wait(self, pair, span):
+        self.copy(span, span, pair, self.row, self.sz.hid - 1 - self.col).wait()
+
+
+def greet_all(sz):
+    me = lax.axis_index("rows") * sz.hid + lax.axis_index("hid")
+    barrier = pltpu.get_barrier_semaphore()
+
+    def greet(step, carry):
+        peer = lax.rem(me + step, sz.count)
+        pl.semaphore_signal(
+            barrier,
+            inc=1,
+            device_id=(peer // sz.hid, lax.rem(peer, sz.hid)),
+            device_id_type=MESH,
+        )
+        return carry
+
+    lax.fori_loop(1, sz.count, greet, 0)
+    return barrier
+
+
+def pieces_start(sz, links, source, target, by_owner):
+    pair = links.pair()
+    local = links.local_sems.at[links.used_local]
+    links.used_local += 1
+    token_id = links.row * sz.hid + links.col
+    owner_id = links.col * sz.rows + links.row
+    there, here = (token_id, owner_id) if by_owner else (owner_id, token_id)
+    at = lambda index: pl.ds(pl.multiple_of(index * sz.piece, sz.piece), sz.piece)
+    pltpu.make_async_copy(source.at[at(here)], target.at[at(there)], local).start()
+
+    def post(step, carry):
+        peer = lax.rem(token_id + step, sz.count)
+        row, col = peer // sz.hid, lax.rem(peer, sz.hid)
+        index = (col * sz.rows + row) if by_owner else peer
+        links.copy(source.at[at(index)], target.at[at(there)], pair, row, col).start()
+        return carry
+
+    lax.fori_loop(1, sz.count, post, 0)
+    return pair, local
+
+
+def pieces_wait(sz, links, target, tokens):
+    pair, local = tokens
+    first = target.at[pl.ds(0, sz.piece)]
+    pltpu.make_async_copy(first, first, local).wait()
+    links.wait(pair, target.at[pl.ds(0, (sz.count - 1) * sz.piece)])
+
+
+def spread_in(source, wide, lines, stride, steps):
+    for place, line in enumerate(lines):
+        wide[:, place * LANES : (place + 1) * LANES] = source[
+            pl.ds(line, steps, stride=stride), :
+        ].astype(wide.dtype)
+
+
+CHUNK = 8
+
+
+def dft(b, lines, outer, target):
+    cos = b.twist[:, :LANES]
+    sin = b.twist[:, LANES:]
+    for start in range(0, lines, CHUNK):
+        here = min(CHUNK, lines - start)
+        lanes = slice(start * LANES, (start + here) * LANES)
+        b.mid[:, : here * LANES] = nn(b.outer_fwd[...], b.wide[:, lanes])
+        for line in range(here):
+            lanes = slice(line * LANES, (line + 1) * LANES)
+            real = b.mid[0:outer, lanes]
+            imag = b.mid[outer : 2 * outer, lanes]
+            rows = slice((start + line) * outer, (start + line + 1) * outer)
+            b.flat[rows, 0:LANES] = (real * cos + imag * sin).astype(BF16)
+            b.flat[rows, LANES:] = (imag * cos - real * sin).astype(BF16)
+        rows = slice(start * outer, (start + here) * outer)
+        target[rows, :] = nn(b.flat[rows, :], b.inner_fwd[...])
+
+
+def inverse_dft(b, lines, outer, put):
+    cos = b.twist[:, :LANES]
+    sin = b.twist[:, LANES:]
+    for start in range(0, lines, CHUNK):
+        here = min(CHUNK, lines - start)
+        for line in range(here):
+            rows = slice((start + line) * outer, (start + line + 1) * outer)
+            lanes = slice(line * LANES, (line + 1) * LANES)
+            part = nn(b.flat[rows, :], b.inner_inv[...])
+            real = part[:, :LANES]
+            imag = part[:, LANES:]
+            b.mid_half[0:outer, lanes] = (real * cos - imag * sin).astype(BF16)
+            b.mid_half[outer : 2 * outer, lanes] = (imag * cos + real * sin).astype(BF16)
+        value = nn(b.outer_inv[...], b.mid_half[:, : here * LANES])
+        for line in range(here):
+            put(start + line, value[:, line * LANES : (line + 1) * LANES])
+
+
+def put_lines(target, lines, stride, steps):
+    def put(place, value):
+        target[pl.ds(lines[place], steps, stride=stride), :] = value
+
+    return put
+
+
+def signal_lines(sz):
+    return [seq * sz.steps * sz.piece + chan for seq in range(sz.seqs) for chan in range(sz.chans)]
+
+
+def own_taps(sz, filters):
+    start = lax.axis_index("rows") * sz.chans
+    chan = lax.broadcasted_iota(jnp.int32, (sz.piece, sz.half), 0)
+    lane = lax.broadcasted_iota(jnp.int32, (sz.piece, sz.half), 1)
+    pick = jnp.where((lane == start + chan) & (chan < sz.chans), 1.0, 0.0).astype(BF16)
+    parts = [nt(pick, filters[way].astype(BF16)) for way in range(2)]
+    return jnp.concatenate(parts, axis=0).astype(BF16)
+
+
+def own_envelope(sz, env):
+    first_chan = lax.axis_index("hid") * sz.half + lax.axis_index("rows") * sz.chans
+    channel = first_chan + lax.broadcasted_iota(jnp.int32, (sz.piece, LANES), 0)
+    fraction = lax.rem(channel * 37, sz.width).astype(F32) / (sz.width - 1)
+    start_log = math.log(1.0 / 40.0)
+    rate = jnp.exp(start_log + (math.log(1.5 / sz.length) - start_log) * fraction)
+    lane = lax.broadcasted_iota(jnp.int32, (sz.piece, LANES), 1)
+    power = jnp.zeros((sz.piece, LANES), F32)
+    for step in range(sz.steps):
+        decay = jnp.exp(-(lane + step * LANES).astype(F32) * rate)
+        env[0 : sz.piece, step * LANES : (step + 1) * LANES] = decay
+        power += decay * decay
+    scale = lax.rsqrt(2.0 * jnp.sum(power, axis=1, keepdims=True))
+    for step in range(sz.steps):
+        lanes = slice(step * LANES, (step + 1) * LANES)
+        value = env[0 : sz.piece, lanes] * scale
+        env[0 : sz.piece, lanes] = value
+        env[sz.piece :, lanes] = jnp.where(lane + step * LANES > 0, value, 0.0)
+
+
+def filter_spectrum(sz, b, layer):
+    piece, steps, outer = sz.piece, sz.steps, sz.outer
+    taps = own_taps(sz, b.filters[layer])
+    chunk = 4
+    for start in range(0, steps, chunk):
+        span = slice(start * LANES, (start + chunk) * LANES)
+        kernels = nn(taps, b.pos[:, span]) * b.env[:, span]
+        for step in range(chunk):
+            b.tall[pl.ds((start + step) * 2 * piece, 2 * piece), :] = kernels[
+                :, step * LANES : (step + 1) * LANES
+            ]
+    spec = b.filt_spec[layer]
+    span = sz.chans * outer
+    for way in range(2):
+        lines = [way * piece + chan for chan in range(sz.chans)]
+        spread_in(b.tall, b.wide, lines, 2 * piece, steps)
+        dft(b, sz.chans, outer, b.spec)
+        if way == 0:
+            spec[...] = b.spec[0:span, :].astype(BF16)
+        else:
+            spec[:, :LANES] = (spec[:, :LANES].astype(F32) + b.spec[0:span, :LANES]).astype(BF16)
+            spec[:, LANES:] = (spec[:, LANES:].astype(F32) - b.spec[0:span, LANES:]).astype(BF16)
+
+
+def conv_forward(sz, b, layer, landed):
+    b.tall[0 : sz.channels, :] = landed[...].astype(F32)
+    lines = signal_lines(sz)
+    spread_in(b.tall, b.wide, lines, sz.piece, sz.steps)
+    dft(b, sz.pairs, sz.outer, b.spec)
+    span = sz.chans * sz.outer
+    filt = b.filt_spec[layer]
+    for seq in range(sz.seqs):
+        rows = slice(seq * span, (seq + 1) * span)
+        re, im = b.spec[rows, :LANES], b.spec[rows, LANES:]
+        b.sig_spec[layer][rows, :LANES] = re.astype(BF16)
+        b.sig_spec[layer][rows, LANES:] = im.astype(BF16)
+        fil_re, fil_im = filt[:, :LANES].astype(F32), filt[:, LANES:].astype(F32)
+        b.flat[rows, :LANES] = (re * fil_re - im * fil_im).astype(BF16)
+        b.flat[rows, LANES:] = (re * fil_im + im * fil_re).astype(BF16)
+    inverse_dft(b, sz.pairs, sz.outer, put_lines(b.tall, lines, sz.piece, sz.steps))
+    b.staged[...] = b.tall[0 : sz.channels, :].astype(BF16)
+
+
+def conv_backward(sz, b, layer, landed):
+    b.tall[0 : sz.channels, :] = landed[...].astype(F32)
+    lines = signal_lines(sz)
+    spread_in(b.tall, b.wide, lines, sz.piece, sz.steps)
+    dft(b, sz.pairs, sz.outer, b.spec)
+    span = sz.chans * sz.outer
+    filt = b.filt_spec[layer]
+    for seq in range(sz.seqs):
+        rows = slice(seq * span, (seq + 1) * span)
+        re, im = b.spec[rows, :LANES], b.spec[rows, LANES:]
+        fil_re, fil_im = filt[:, :LANES].astype(F32), filt[:, LANES:].astype(F32)
+        b.flat[rows, :LANES] = (re * fil_re + im * fil_im).astype(BF16)
+        b.flat[rows, LANES:] = (im * fil_re - re * fil_im).astype(BF16)
+    inverse_dft(b, sz.pairs, sz.outer, put_lines(b.tall, lines, sz.piece, sz.steps))
+    b.staged[...] = b.tall[0 : sz.channels, :].astype(BF16)
+
+
+def taps_gradient(sz, b, layer, landed, signal):
+    span = sz.chans * sz.outer
+    total_re = jnp.zeros((span, LANES), F32)
+    total_im = jnp.zeros((span, LANES), F32)
+    for seq in range(sz.seqs):
+        rows = slice(seq * span, (seq + 1) * span)
+        re, im = b.spec[rows, :LANES], b.spec[rows, LANES:]
+        sig = b.sig_spec[layer]
+        sig_re, sig_im = sig[rows, :LANES].astype(F32), sig[rows, LANES:].astype(F32)
+        total_re += re * sig_re + im * sig_im
+        total_im += im * sig_re - re * sig_im
+    piece = sz.piece
+    b.tall[...] = jnp.zeros_like(b.tall)
+    for way in range(2):
+        b.flat[0:span, :LANES] = total_re.astype(BF16)
+        b.flat[0:span, LANES:] = (total_im if way == 0 else -total_im).astype(BF16)
+        lines = [way * piece + chan for chan in range(sz.chans)]
+        inverse_dft(b, sz.chans, sz.outer, put_lines(b.tall, lines, 2 * piece, sz.steps))
+    taps = own_taps(sz, b.filters[layer])
+    total = jnp.zeros((2 * piece, ORDER), F32)
+    chunk = 4
+    for start in range(0, sz.steps, chunk):
+        lanes = slice(start * LANES, (start + chunk) * LANES)
+        raw = nn(taps, b.pos[:, lanes])
+        grads = jnp.concatenate(
+            [b.tall[pl.ds((start + step) * 2 * piece, 2 * piece), :] for step in range(chunk)],
+            axis=1,
+        )
+        grads = grads * b.env[:, lanes] + (2.0 * DECAY) * raw
+        total += nt(grads.astype(BF16), b.pos[:, lanes])
+    products = jnp.zeros((piece, LANES), F32)
+    for block in range(sz.count):
+        rows = slice(block * piece, (block + 1) * piece)
+        products += landed[rows, :].astype(F32) * signal[rows, :].astype(F32)
+    column = jnp.sum(products, axis=1, keepdims=True)
+    row = jnp.transpose(jnp.broadcast_to(column, (piece, LANES)))[0:8, :]
+    b.taps_work[...] = jnp.zeros_like(b.taps_work)
+    b.taps_work[0 : sz.chans, :] = total[0 : sz.chans, :]
+    b.taps_work[sz.chans : 2 * sz.chans, :] = total[piece : piece + sz.chans, :]
+    b.taps_work[2 * sz.chans : 2 * sz.chans + 1, 0:piece] = row[0:1, :]
+
+
+def block_of(sz, block):
+    return slice(block * sz.size, (block + 1) * sz.size)
+
+
+def pad_pieces(sz, b, source, target):
+    for owner in range(sz.count):
+        b.tall[owner * sz.piece : owner * sz.piece + sz.chans, :] = source[
+            owner * sz.chans : (owner + 1) * sz.chans, :
+        ]
+    target[...] = b.tall[0 : sz.channels, :].astype(BF16)
+
+
+def unpad_pieces(sz, b, source, target):
+    b.tall[0 : sz.channels, :] = source[...].astype(F32)
+    for owner in range(sz.count):
+        target[owner * sz.chans : (owner + 1) * sz.chans, :] = b.tall[
+            owner * sz.piece : owner * sz.piece + sz.chans, :
+        ]
+
+
+def project(sz, b, layer):
+    for block in range(sz.blocks):
+        rows = block_of(sz, block)
+        part = b.normed[layer][:, rows]
+        b.wide_own[rows, :] = nt(b.mixer[layer, 0, block], part)
+        b.gate[layer][rows, :] = nt(b.mixer[layer, 1, block], part)
+    b.inner[layer][...] = b.wide_own[...].astype(BF16)
+    pad_pieces(sz, b, b.wide_own, b.message)
+
+
+def mix(sz, b, layer, conv):
+    summed, mixed, middle = b.summed[layer], b.mixed[layer], b.middle[layer]
+    unpad_pieces(sz, b, conv, b.wide_own)
+    summed[...] = b.wide_own[...] + b.skip[layer][...] * b.inner[layer][...].astype(F32)
+    mixed[...] = (b.gate[layer][...] * summed[...]).astype(BF16)
+    for block in range(sz.blocks):
+        rows = block_of(sz, block)
+        middle[:, rows] = tn(mixed[rows, :], b.mixer[layer, 2, block])
+    middle[...] = middle[...] + b.stream[layer][...]
+
+
+def mixer_gradient(sz, b, kind_row, values, mine, give):
+    low = lax.axis_index("hid") == 0
+    left = jnp.concatenate(values[: sz.side_blocks], axis=1)
+    right = jnp.concatenate(values[sz.side_blocks :], axis=1)
+    rows = slice(kind_row * sz.size, (kind_row + 1) * sz.size)
+    mine[rows, :] = jnp.where(low, left, right).astype(BF16)
+    give[rows, :] = jnp.where(low, right, left).astype(BF16)
+
+
+def gain_gradient(sz, b, row, value, mine, give):
+    low = lax.axis_index("hid") == 0
+    left, right = value[:, : sz.half], value[:, sz.half :]
+    mine[row : row + 1, :] = jnp.where(low, left, right)
+    give[row : row + 1, :] = jnp.where(low, right, left)
+
+
+def mixer_backward(sz, b, layer, grad_next, total):
+    normal, inv = normalize(b.middle[layer][...])
+    gain = b.gain[layer, 1:2, :]
+    back, gain_grad = norm_back(total, normal, inv, gain)
+    result = grad_next + back
+    b.grad_middle[...] = result
+    b.grad_o[...] = result.astype(BF16)
+    for block in range(sz.blocks):
+        rows = block_of(sz, block)
+        grad_mixed = nt(b.mixer[layer, 2, block], b.grad_o[:, rows])
+        b.gate_grad[rows, :] = (grad_mixed * b.summed[layer][rows, :]).astype(BF16)
+        b.summed_grad[rows, :] = grad_mixed * b.gate[layer][rows, :]
+    pad_pieces(sz, b, b.summed_grad, b.message)
+    return gain_grad
+
+
+def out_gradient(sz, b, layer):
+    return [
+        nn(b.mixed[layer][block_of(sz, block), :], b.grad_o[:, block_of(sz, block)])
+        for block in range(sz.blocks)
+    ]
+
+
+def in_gradient(sz, b, layer, grads):
+    return [
+        jnp.transpose(
+            nn(grads[block_of(sz, block), :], b.normed[layer][:, block_of(sz, block)])
+        )
+        for block in range(sz.blocks)
+    ]
+
+
+def input_backward(sz, b, layer, back):
+    unpad_pieces(sz, b, back, b.wide_own)
+    b.inner_grad[...] = (b.skip[layer][...] * b.summed_grad[...] + b.wide_own[...]).astype(BF16)
+    for block in range(sz.blocks):
+        rows = block_of(sz, block)
+        b.work[:, rows] = tn(b.inner_grad[rows, :], b.mixer[layer, 0, block]) + tn(
+            b.gate_grad[rows, :], b.mixer[layer, 1, block]
+        )
+    normal, inv = normalize(b.stream[layer][...])
+    result, gain_grad = norm_back(
+        b.work[...], normal, inv, b.gain[layer, 0:1, :]
+    )
+    return b.grad_middle[...] + result, gain_grad
+
+
+def ff_forward(sz, b, layer):
+    tile = 512
+    rows = slice(0, 2 * sz.own)
+    b.out_sum[...] = jnp.zeros_like(b.out_sum)
+
+    def body(step, carry):
+        lanes = pl.ds(pl.multiple_of(step * tile, tile), tile)
+        normed = b.nbuf[layer][rows, :]
+        gate = nn(normed, b.up[layer, 0, :, lanes])
+        up = nn(normed, b.up[layer, 1, :, lanes])
+        value, _ = gelu_parts(gate)
+        b.out_sum[...] += nt((value * up).astype(BF16), b.down[layer, :, lanes])
+        return carry
+
+    lax.fori_loop(0, sz.units // tile, body, 0)
+
+
+def ff_backward(sz, b, layer, with_out):
+    tile = 512
+    rows = slice(0, 2 * sz.own)
+    b.grad_sum[...] = jnp.zeros_like(b.grad_sum)
+    if with_out:
+        b.out_sum[...] = jnp.zeros_like(b.out_sum)
+
+    def body(step, carry):
+        lanes = pl.ds(pl.multiple_of(step * tile, tile), tile)
+        normed = b.nbuf[layer][rows, :]
+        gate = nn(normed, b.up[layer, 0, :, lanes])
+        up = nn(normed, b.up[layer, 1, :, lanes])
+        through = nn(b.gbuf[layer][rows, :], b.down[layer, :, lanes])
+        value, slope = gelu_parts(gate)
+        if with_out:
+            b.out_sum[...] += nt((value * up).astype(BF16), b.down[layer, :, lanes])
+        gate_grad = (slope * up * through).astype(BF16)
+        up_grad = (value * through).astype(BF16)
+        b.grad_sum[...] += nt(gate_grad, b.up[layer, 0, :, lanes]) + nt(
+            up_grad, b.up[layer, 1, :, lanes]
+        )
+        return carry
+
+    lax.fori_loop(0, sz.units // tile, body, 0)
+
+
+def ff_gradients(sz, b, layer, links):
+    start = pl.multiple_of(links.line * sz.part, LANES)
+    units = pl.ds(start, sz.part)
+    chunk = 2 * sz.own
+
+    def body(step, carry):
+        rows = pl.ds(pl.multiple_of(step * chunk, chunk), chunk)
+        normed = b.nbuf[layer][rows, :]
+        gate = nn(normed, b.up[layer, 0, :, units])
+        up = nn(normed, b.up[layer, 1, :, units])
+        through = nn(b.gbuf[layer][rows, :], b.down[layer, :, units])
+        value, slope = gelu_parts(gate)
+        b.unit_grad[0, rows, :] = (slope * up * through).astype(BF16)
+        b.unit_grad[1, rows, :] = (value * through).astype(BF16)
+        b.unit_grad[2, rows, :] = (value * up).astype(BF16)
+        return carry
+
+    lax.fori_loop(0, sz.group, body, 0)
+    split = sz.width // 2
+    for begin in (0, split):
+        lanes = slice(begin, begin + split)
+        for kind in range(3):
+            left = b.gbuf[layer] if kind == 2 else b.nbuf[layer]
+            b.product[...] = tn(left[:, lanes], b.unit_grad[kind])
+            for first in range(0, split, sz.depth):
+                owner = (begin + first) // sz.depth
+                line, peer = owner // sz.peers, owner % sz.peers
+                b.pieces[peer, line, kind, 0 : sz.depth, :] = b.product[
+                    first : first + sz.depth, :
+                ].astype(BF16)
+    b.summing[layer][links.plane] = b.pieces[links.plane]
+
+
+def sum_pieces(sz, b, layer, links):
+    for line in range(sz.group):
+        for kind in range(3):
+            total = b.summing[layer][0, line, kind].astype(F32)
+            for peer in range(1, sz.peers):
+                total += b.summing[layer][peer, line, kind].astype(F32)
+            b.part_sum[layer][line, kind] = total.astype(BF16)
+
+
+class Named:
+    pass
+
+
+def layout(sz):
+    layers, own, width = sz.layers, sz.own, sz.width
+    wide = 2 * sz.piece * sz.steps
+    span = sz.early_rows * sz.rows
+    late = sz.late_rows * sz.rows
+    per_layer = dict(
+        stream=((own, width), F32),
+        normed=((own, width), BF16),
+        inner=((width, own), BF16),
+        gate=((width, own), F32),
+        summed=((width, own), F32),
+        mixed=((width, own), BF16),
+        middle=((own, width), F32),
+        nbuf=((2 * sz.group * own, width), BF16),
+        gbuf=((2 * sz.group * own, width), BF16),
+        skip=((width, LANES), F32),
+        filt_spec=((sz.chans * sz.outer, 2 * LANES), BF16),
+        sig_spec=((sz.pairs * sz.outer, 2 * LANES), BF16),
+        fore_in=((sz.channels, LANES), BF16),
+        fore_out=((sz.channels, LANES), BF16),
+        back_in=((sz.channels, LANES), BF16),
+        back_out=((sz.channels, LANES), BF16),
+        summing=((sz.peers, sz.group, 3, sz.deep, sz.part), BF16),
+        part_sum=((sz.group, 3, sz.deep, sz.part), BF16),
+        grad_got=((own, width), BF16),
+        out_got=((own, width), BF16),
+    )
+    single = dict(
+        x=((own, width), BF16),
+        gain=((layers, 2, width), F32),
+        skip_rows=((layers, width), F32),
+        mixer=((layers, 3, sz.blocks, sz.size, sz.size), BF16),
+        filters=((layers, 2, ORDER, sz.half), F32),
+        pos=((ORDER, sz.length), BF16),
+        outer_fwd=((2 * sz.outer, sz.steps), BF16),
+        outer_inv=((sz.steps, 2 * sz.outer), BF16),
+        inner_fwd=((2 * LANES, 2 * LANES), BF16),
+        inner_inv=((2 * LANES, 2 * LANES), BF16),
+        twist=((sz.outer, 2 * LANES), F32),
+        up=((layers, 2, width, sz.units), BF16),
+        down=((layers, width, sz.units), BF16),
+        env=((2 * sz.piece, sz.length), F32),
+        tall=((max(wide, sz.channels), LANES), F32),
+        wide=((sz.steps, sz.lines * LANES), BF16),
+        mid=((2 * sz.outer, CHUNK * LANES), F32),
+        flat=((sz.lines * sz.outer, 2 * LANES), BF16),
+        mid_half=((2 * sz.outer, CHUNK * LANES), BF16),
+        spec=((sz.lines * sz.outer, 2 * LANES), F32),
+        message=((sz.channels, LANES), BF16),
+        staged=((sz.channels, LANES), BF16),
+        wide_own=((width, own), F32),
+        work=((own, width), F32),
+        grad_next=((own, width), F32),
+        grad_middle=((own, width), F32),
+        grad_o=((own, width), BF16),
+        gate_grad=((width, own), BF16),
+        summed_grad=((width, own), F32),
+        inner_grad=((width, own), BF16),
+        out_sum=((2 * own, width), F32),
+        grad_sum=((2 * own, width), F32),
+        out_give=((own, width), BF16),
+        sum_give=((own, width), BF16),
+        unit_grad=((3, 2 * sz.group * own, sz.part), BF16),
+        product=((width // 2, sz.part), F32),
+        pieces=((sz.peers, sz.group, 3, sz.deep, sz.part), BF16),
+        taps_work=((sz.taps_rows, ORDER), F32),
+        gain_mine=((16, sz.half), F32),
+        gain_give=((16, sz.half), F32),
+        early_mine=((span, sz.half), BF16),
+        early_give=((span, sz.half), BF16),
+        early_got=((span, sz.half), BF16),
+        early_plane=((sz.peers, sz.group * sz.early_rows, sz.half), BF16),
+        early_sum=((sz.group * sz.early_rows, sz.half), BF16),
+        early_line=((sz.group, sz.early_rows, sz.half), BF16),
+        late_gain_mine=((16, sz.half), F32),
+        late_gain_give=((16, sz.half), F32),
+        late_mine=((late, sz.half), BF16),
+        late_give=((late, sz.half), BF16),
+        late_got=((late, sz.half), BF16),
+        late_in=((sz.rows, sz.late_rows, sz.half), BF16),
+        late_sum=((sz.late_rows, sz.half), BF16),
+        out_keep=((2, own, sz.half), BF16),
+        in_keep=((2, own, sz.half), F32),
+        taps_send=((layers, sz.taps_rows, ORDER), BF16),
+        late_out=((sz.late_rows, sz.half), BF16),
+        early_out=((sz.early_rows, sz.half), BF16),
+    )
+    names, specs = [], []
+    for name, (shape, kind) in per_layer.items():
+        for layer in range(layers):
+            names.append((name, layer))
+            specs.append(pltpu.VMEM(shape, kind))
+    for name, (shape, kind) in single.items():
+        names.append((name, None))
+        specs.append(pltpu.VMEM(shape, kind))
+    return names, specs
+
+
+TABLES = ("pos", "outer_fwd", "outer_inv", "inner_fwd", "inner_inv", "twist")
+INPUTS = ("hidden_in", "d_out", "gains", "mixer", "skip", "filters", "gate_up", "down") + TABLES
+OUTPUTS = ("hidden_out", "grad_in", "early", "late", "taps", "units")
+
+
+def program_kernel(sz, *refs):
+    names, _ = layout(sz)
+    inputs = dict(zip(INPUTS, refs))
+    outputs = dict(zip(OUTPUTS, refs[len(INPUTS) :]))
+    scratch = refs[len(INPUTS) + len(OUTPUTS) :]
+    b = Named()
+    for (name, layer), ref in zip(names, scratch):
+        if layer is None:
+            setattr(b, name, ref)
+        else:
+            setattr(b, name, getattr(b, name, ()) + (ref,))
+    links = Links(sz, scratch[len(names)], scratch[len(names) + 1])
+    own = sz.own
+    top = sz.layers - 1
+    col = links.col
+    low = col == 0
+    mine_rows = pl.ds(pl.multiple_of(col * own, own), own)
+    other_rows = pl.ds(pl.multiple_of((1 - col) * own, own), own)
+
+    barrier = greet_all(sz)
+    lanes = pl.ds(pl.multiple_of(col * sz.half, sz.half), sz.half)
+    sides = pl.ds(col * sz.side_blocks, sz.side_blocks)
+    halves = (
+        ("x", inputs["hidden_in"], b.x.at[:, lanes]),
+        ("mixer", inputs["mixer"], b.mixer.at[:, :, sides]),
+        ("gains", inputs["gains"], b.gain.at[:, :, lanes]),
+        ("skip", inputs["skip"], b.skip_rows.at[:, lanes]),
+        ("g", inputs["d_out"], b.gbuf[top].at[pl.ds(0, own), lanes]),
+    )
+    loads = {}
+    for name, source, target in halves:
+        if name in ("x", "g"):
+            source = source.at[mine_rows]
+        loads[name] = links.load(source, target)
+    loads["filters"] = links.load(inputs["filters"], b.filters)
+    for name in TABLES:
+        loads[name] = links.load(inputs[name], getattr(b, name))
+    for layer in range(sz.layers):
+        loads["up", layer] = links.load(inputs["gate_up"].at[layer], b.up.at[layer])
+        loads["down", layer] = links.load(inputs["down"].at[layer], b.down.at[layer])
+    b.gain_mine[...] = jnp.zeros_like(b.gain_mine)
+    b.gain_give[...] = jnp.zeros_like(b.gain_give)
+    b.late_gain_mine[...] = jnp.zeros_like(b.late_gain_mine)
+    b.late_gain_give[...] = jnp.zeros_like(b.late_gain_give)
+    pl.semaphore_wait(barrier, sz.count - 1)
+    got = {}
+    for name, source, target in halves:
+        if name in ("x", "g"):
+            source = source.at[other_rows]
+        got[name] = links.sibling(source, target)
+
+    def both(*wanted):
+        for name in wanted:
+            loads[name].wait()
+            got[name].wait()
+
+    def turn_mixer(layer, kind):
+        for block in range(sz.blocks):
+            b.mixer[layer, kind, block] = jnp.transpose(b.mixer[layer, kind, block])
+
+    def norm_to(source, target, layer, which):
+        normal, _ = normalize(source)
+        target[...] = (normal * b.gain[layer, which : which + 1, :]).astype(BF16)
+
+    both("x", "gains")
+    b.stream[0][...] = b.x[...].astype(F32)
+    norm_to(b.stream[0][...], b.normed[0], 0, 0)
+    both("mixer")
+    turn_mixer(0, 0)
+    turn_mixer(0, 1)
+
+    def gather_own(buffer):
+        return links.sibling(buffer.at[pl.ds(0, own)], buffer.at[pl.ds(own, own)])
+
+    def gather_line(buffer):
+        pair = links.pair()
+        for step in range(1, sz.group):
+            member = lax.rem(links.line + step, sz.group)
+            slot = pl.ds((1 + step) * own, own)
+            links.copy(
+                buffer.at[pl.ds(0, own)],
+                buffer.at[slot],
+                pair,
+                member * sz.peers + links.plane,
+                col,
+            ).start()
+        return pair
+
+    def gather_rest(buffer, pair):
+        arrived = buffer.at[pl.ds(2 * own, (sz.group - 1) * own)]
+        links.wait(pair, arrived)
+        return links.sibling(
+            arrived, buffer.at[pl.ds((1 + sz.group) * own, (sz.group - 1) * own)]
+        )
+
+    project(sz, b, 0)
+    for layer in range(sz.layers):
+        moving = pieces_start(sz, links, b.message, b.fore_in[layer], True)
+        if layer == 0:
+            for name in ("filters", "pos", "outer_fwd", "inner_fwd", "twist"):
+                loads[name].wait()
+            own_envelope(sz, b.env)
+        filter_spectrum(sz, b, layer)
+        if layer == 0:
+            for name in ("outer_inv", "inner_inv"):
+                loads[name].wait()
+            both("skip", "g")
+            for each in range(sz.layers):
+                row = b.skip_rows[each : each + 1, :]
+                b.skip[each][...] = jnp.transpose(jnp.broadcast_to(row, (LANES, sz.width)))
+        pieces_wait(sz, links, b.fore_in[layer], moving)
+        conv_forward(sz, b, layer, b.fore_in[layer])
+        moving = pieces_start(sz, links, b.staged, b.fore_out[layer], False)
+        if layer == 0:
+            for each in range(1, sz.layers):
+                turn_mixer(each, 0)
+                turn_mixer(each, 1)
+            top_own = gather_own(b.gbuf[top])
+            top_line = gather_line(b.gbuf[top])
+        loads["up", layer].wait()
+        loads["down", layer].wait()
+        pieces_wait(sz, links, b.fore_out[layer], moving)
+        mix(sz, b, layer, b.fore_out[layer])
+        norm_to(b.middle[layer][...], b.nbuf[layer].at[pl.ds(0, own)], layer, 1)
+        near = gather_own(b.nbuf[layer])
+        far = gather_line(b.nbuf[layer])
+        near.wait()
+        if layer < top:
+            ff_forward(sz, b, layer)
+            b.out_give[...] = b.out_sum[own:, :].astype(BF16)
+            moving = links.sibling(b.out_give, b.out_got[layer])
+            if layer == 0:
+                top_own.wait()
+                top_rest = gather_rest(b.gbuf[top], top_line)
+            moving.wait()
+            value = b.middle[layer][...] + b.out_sum[0:own, :] + b.out_got[layer][...].astype(F32)
+            b.stream[layer + 1][...] = value
+            norm_to(value, b.normed[layer + 1], layer + 1, 0)
+            project(sz, b, layer + 1)
+            low_rest = gather_rest(b.nbuf[layer], far)
+
+    ff_backward(sz, b, top, True)
+    b.sum_give[...] = b.grad_sum[own:, :].astype(BF16)
+    moving = links.sibling(b.sum_give, b.grad_got[top])
+    b.out_give[...] = b.out_sum[own:, :].astype(BF16)
+    out_moving = links.sibling(b.out_give, b.out_got[top])
+    moving.wait()
+    total = b.grad_sum[0:own, :] + b.grad_got[top][...].astype(F32)
+    grad_next = b.gbuf[top][0:own, :].astype(F32)
+    gain_grad = mixer_backward(sz, b, top, grad_next, total)
+    moving = pieces_start(sz, links, b.message, b.back_in[top], True)
+    gain_gradient(sz, b, 2 * top, gain_grad, b.gain_mine, b.gain_give)
+    early_row = 0
+    mixer_gradient(sz, b, early_row, out_gradient(sz, b, top), b.early_mine, b.early_give)
+    early_row += 1
+
+    out_moving.wait()
+    value = b.middle[top][...] + b.out_sum[0:own, :] + b.out_got[top][...].astype(F32)
+    value = value.astype(BF16)
+    left, right = value[:, : sz.half], value[:, sz.half :]
+    b.out_keep[0] = jnp.where(low, left, right)
+    b.out_keep[1] = jnp.where(low, right, left)
+    place = outputs["hidden_out"].at[mine_rows]
+    ending = [links.load(b.out_keep.at[0], place), links.sibling(b.out_keep.at[1], place)]
+    if sz.layers > 1:
+        low_rest.wait()
+        top_rest.wait()
+
+    waiting = {}
+    taps_moving = []
+    units_moving = []
+
+    def send_units(layer):
+        target = outputs["units"].at[layer, links.line]
+        ending.append(links.load(b.part_sum[layer].at[links.line], target))
+        return links.in_line(lambda member: b.part_sum[layer].at[member], target)
+
+    for layer in reversed(range(sz.layers)):
+        if layer == top:
+            rest = gather_rest(b.nbuf[top], far)
+        else:
+            rest = gather_rest(b.gbuf[layer], far)
+            links.wait(waiting["plane"], b.summing[layer + 1].at[pl.ds(0, sz.peers - 1)])
+            sum_pieces(sz, b, layer + 1, links)
+            units_moving.append(send_units(layer + 1))
+            if layer == 0:
+                early_pair.wait()
+                b.early_mine[...] = (
+                    b.early_mine[...].astype(F32) + b.early_got[...].astype(F32)
+                ).astype(BF16)
+                slab = sz.group * sz.early_rows
+                at = lambda index: pl.ds(pl.multiple_of(index * slab, slab), slab)
+                plane_pair = links.in_plane(
+                    lambda member: b.early_mine.at[at(member)], b.early_plane.at[links.plane]
+                )
+        pieces_wait(sz, links, b.back_in[layer], moving)
+        conv_backward(sz, b, layer, b.back_in[layer])
+        moving = pieces_start(sz, links, b.staged, b.back_out[layer], False)
+        taps_gradient(sz, b, layer, b.back_in[layer], b.fore_in[layer])
+        b.taps_send[layer] = b.taps_work[...].astype(BF16)
+        place = outputs["taps"].at[links.row, layer]
+        ending.append(links.load(b.taps_send.at[layer], place))
+        taps_moving.append(links.in_rows(lambda member: b.taps_send.at[layer], place))
+        rest.wait()
+        ff_gradients(sz, b, layer, links)
+        waiting["plane"] = links.in_plane(
+            lambda member: b.pieces.at[member], b.summing[layer].at[links.plane]
+        )
+        pieces_wait(sz, links, b.back_out[layer], moving)
+        value, gain_grad = input_backward(sz, b, layer, b.back_out[layer])
+        if layer > 0:
+            b.grad_next[...] = value
+            b.gbuf[layer - 1][0:own, :] = value.astype(BF16)
+            near = gather_own(b.gbuf[layer - 1])
+            far = gather_line(b.gbuf[layer - 1])
+            gain_gradient(sz, b, 2 * layer - 1, gain_grad, b.gain_mine, b.gain_give)
+            for grads in (b.inner_grad, b.gate_grad):
+                mixer_gradient(
+                    sz, b, early_row, in_gradient(sz, b, layer, grads), b.early_mine, b.early_give
+                )
+                early_row += 1
+            near.wait()
+            ff_backward(sz, b, layer - 1, False)
+            b.sum_give[...] = b.grad_sum[own:, :].astype(BF16)
+            moving = links.sibling(b.sum_give, b.grad_got[layer - 1])
+            moving.wait()
+            total = b.grad_sum[0:own, :] + b.grad_got[layer - 1][...].astype(F32)
+            gain_grad = mixer_backward(sz, b, layer - 1, b.grad_next[...], total)
+            moving = pieces_start(sz, links, b.message, b.back_in[layer - 1], True)
+            gain_gradient(sz, b, 2 * layer - 2, gain_grad, b.gain_mine, b.gain_give)
+            mixer_gradient(
+                sz, b, early_row, out_gradient(sz, b, layer - 1), b.early_mine, b.early_give
+            )
+            early_row += 1
+            if layer == 1:
+                mixer_gradient(
+                    sz,
+                    b,
+                    early_row,
+                    in_gradient(sz, b, 0, b.gate_grad),
+                    b.early_mine,
+                    b.early_give,
+                )
+                early_row += 1
+                rows = slice(early_row * sz.size, early_row * sz.size + 16)
+                b.early_mine[rows, :] = b.gain_mine[...].astype(BF16)
+                b.early_give[rows, :] = b.gain_give[...].astype(BF16)
+                last = slice(early_row * sz.size + 16, sz.rows * sz.early_rows)
+                b.early_mine[last, :] = jnp.zeros_like(b.early_mine[last, :])
+                b.early_give[last, :] = jnp.zeros_like(b.early_give[last, :])
+                early_pair = links.sibling(b.early_give, b.early_got)
+
+    left, right = value[:, : sz.half], value[:, sz.half :]
+    b.in_keep[0] = jnp.where(low, left, right)
+    b.in_keep[1] = jnp.where(low, right, left)
+    place = outputs["grad_in"].at[mine_rows]
+    ending += [links.load(b.in_keep.at[0], place), links.sibling(b.in_keep.at[1], place)]
+    mixer_gradient(
+        sz, b, 0, in_gradient(sz, b, 0, b.inner_grad), b.late_mine, b.late_give
+    )
+    gain_gradient(sz, b, 0, gain_grad, b.late_gain_mine, b.late_gain_give)
+    rows = slice(sz.size, sz.size + 16)
+    b.late_mine[rows, :] = b.late_gain_mine[...].astype(BF16)
+    b.late_give[rows, :] = b.late_gain_give[...].astype(BF16)
+    last = slice(sz.size + 16, sz.rows * sz.late_rows)
+    b.late_mine[last, :] = jnp.zeros_like(b.late_mine[last, :])
+    b.late_give[last, :] = jnp.zeros_like(b.late_give[last, :])
+    late_pair = links.sibling(b.late_give, b.late_got)
+
+    links.wait(plane_pair, b.early_plane.at[pl.ds(0, sz.peers - 1)])
+    b.early_plane[links.plane] = b.early_mine[at(links.plane), :]
+    total = b.early_plane[0].astype(F32)
+    for peer in range(1, sz.peers):
+        total += b.early_plane[peer].astype(F32)
+    b.early_sum[...] = total.astype(BF16)
+    deep = sz.early_rows
+    one = lambda index: pl.ds(pl.multiple_of(index * deep, deep), deep)
+    line_pair = links.in_line(
+        lambda member: b.early_sum.at[one(member)], b.early_line.at[links.line]
+    )
+
+    late_pair.wait()
+    b.late_mine[...] = (b.late_mine[...].astype(F32) + b.late_got[...].astype(F32)).astype(BF16)
+    few = lambda index: pl.ds(pl.multiple_of(index * sz.late_rows, sz.late_rows), sz.late_rows)
+    rows_pair = links.in_rows(
+        lambda member: b.late_mine.at[few(member)], b.late_in.at[links.row]
+    )
+
+    links.wait(line_pair, b.early_line.at[pl.ds(0, sz.group - 1)])
+    b.early_line[links.line] = b.early_sum[one(links.line), :]
+    total = b.early_line[0].astype(F32)
+    for member in range(1, sz.group):
+        total += b.early_line[member].astype(F32)
+    early = outputs["early"]
+    b.early_out[...] = total.astype(BF16)
+    place = early.at[links.plane * sz.group + links.line]
+    early_own = links.load(b.early_out, place)
+    spread_line = links.in_line(lambda member: b.early_out, place)
+
+    links.wait(rows_pair, b.late_in.at[pl.ds(0, sz.rows - 1)])
+    b.late_in[links.row] = b.late_mine[few(links.row), :]
+    late = outputs["late"]
+    b.late_out[...] = jnp.sum(b.late_in[...].astype(F32), axis=0).astype(BF16)
+    ending.append(links.load(b.late_out, late.at[links.row]))
+    spread_rows = links.in_rows(lambda member: b.late_out, late.at[links.row])
+
+    links.wait(waiting["plane"], b.summing[0].at[pl.ds(0, sz.peers - 1)])
+    sum_pieces(sz, b, 0, links)
+    units_moving.append(send_units(0))
+    early_own.wait()
+    links.wait(spread_line, early.at[pl.ds(0, sz.group - 1)])
+    mine = pl.ds(pl.multiple_of(links.plane * sz.group, sz.group), sz.group)
+    spread_plane = links.in_plane(lambda member: early.at[mine], early.at[mine])
+
+    for layer, pair in zip(reversed(range(sz.layers)), units_moving):
+        links.wait(pair, outputs["units"].at[layer, pl.ds(0, sz.group - 1)])
+    links.wait(spread_plane, early.at[pl.ds(0, (sz.peers - 1) * sz.group)])
+    links.wait(spread_rows, late.at[pl.ds(0, sz.rows - 1)])
+    for layer, pair in zip(reversed(range(sz.layers)), taps_moving):
+        links.wait(pair, outputs["taps"].at[pl.ds(0, sz.rows - 1), layer])
+    for copy in ending:
+        copy.wait()
+
+
+def program(sz, arrays):
+    names, scratch = layout(sz)
+    outs = (
+        ((2 * sz.own, sz.half), BF16),
+        ((2 * sz.own, sz.half), F32),
+        ((sz.rows, sz.early_rows, sz.half), BF16),
+        ((sz.rows, sz.late_rows, sz.half), BF16),
+        ((sz.rows, sz.layers, sz.taps_rows, ORDER), BF16),
+        ((sz.layers, sz.group, 3, sz.deep, sz.part), BF16),
+    )
+    return pl.pallas_call(
+        functools.partial(program_kernel, sz),
+        out_shape=tuple(jax.ShapeDtypeStruct(shape, kind) for shape, kind in outs),
+        in_specs=[pl.BlockSpec(memory_space=pl.ANY)] * len(arrays),
+        out_specs=(pl.BlockSpec(memory_space=pl.ANY),) * len(outs),
+        scratch_shapes=scratch
+        + [pltpu.SemaphoreType.DMA((120,)), pltpu.SemaphoreType.DMA((40,))],
+        compiler_params=pltpu.CompilerParams(
+            collective_id=0, has_side_effects=True, vmem_limit_bytes=63 * MIB
+        ),
+        name="program",
+    )(*arrays)
+
+
+def together(sz, hidden_in, d_out, gains, mixer, skip, filters, gate_up, down):
+    rows, layers = sz.rows, sz.layers
+    pos = jnp.asarray(position_table(sz.length).T, F32).astype(BF16)
+    arrays = (hidden_in, d_out, gains, mixer, skip, filters, gate_up, down, pos)
+    hidden_out, grad_in, early, late, taps, units = program(sz, arrays + dft_tables(sz.length))
+
+    def matrix(payload, place):
+        value = payload[place * sz.size : (place + 1) * sz.size].astype(F32)
+        blocks = [value[:, block_of(sz, block)] for block in range(sz.side_blocks)]
+        return jnp.stack(blocks)
+
+    early = early.reshape(-1, sz.half)
+    late = late.reshape(-1, sz.half)
+    places = []
+    for layer in reversed(range(layers)):
+        places += [(layer, 2)]
+        places += [(layer, 0), (layer, 1)] if layer > 0 else [(layer, 1)]
+    found = {place: matrix(early, index) for index, place in enumerate(places)}
+    found[0, 0] = matrix(late, 0)
+    mixers = jnp.stack(
+        [jnp.stack([found[layer, kind] for kind in range(3)]) for layer in range(layers)]
+    )
+    gain_rows = early[sz.early * sz.size : sz.early * sz.size + 2 * layers - 1]
+    gain_rows = jnp.concatenate([late[sz.size : sz.size + 1], gain_rows[: 2 * layers - 1]], axis=0)
+    gain_out = gain_rows.astype(F32).reshape(layers, 2, sz.half)
+    skip_out = jnp.transpose(taps[:, :, 2 * sz.chans, : sz.chans], (1, 0, 2))
+    taps_out = taps[:, :, : 2 * sz.chans].reshape(rows, layers, 2, sz.chans, ORDER)
+    taps_out = jnp.transpose(taps_out, (1, 2, 4, 0, 3)).reshape(layers, 2, ORDER, sz.half)
+    units = jnp.moveaxis(units[:, :, :, : sz.depth].astype(F32), 1, 3)
+    units = units.reshape(layers, 3, sz.depth, sz.units)
+    return (
+        hidden_out,
+        grad_in,
+        gain_out,
+        mixers,
+        skip_out.astype(F32).reshape(layers, sz.half),
+        taps_out.astype(F32),
+        units[:, :2],
+        units[:, 2],
+    )
+
+
+def apart_enter(count, hid):
     me = lax.axis_index("rows") * hid + lax.axis_index("hid")
     barrier = pltpu.get_barrier_semaphore()
 
@@ -107,7 +1127,7 @@
     return barrier
 
 
-def exchange_start(source, target, sems, count, rows, hid, piece, by_owner):
+def apart_exchange_start(source, target, sems, count, rows, hid, piece, by_owner):
     send, recv, local = sems
     row = lax.axis_index("rows")
     col = lax.axis_index("hid")
@@ -136,7 +1156,7 @@
     lax.fori_loop(1, count, post, 0)
 
 
-def exchange_wait(source, target, sems, count, rows, hid, piece):
+def apart_exchange_wait(source, target, sems, count, rows, hid, piece):
     send, recv, local = sems
     row = lax.axis_index("rows")
     col = lax.axis_index("hid")
@@ -154,7 +1174,7 @@
     ).wait()
 
 
-class Sizes:
+class apart_Sizes:
     def __init__(self, rows, hid, width, hidden, tokens):
         self.rows, self.hid, self.width, self.hidden = rows, hid, width, hidden
         self.count = rows * hid
@@ -170,14 +1190,14 @@
         self.channels = self.count * self.piece
 
 
-def spread_in(source, wide, lines, stride, blocks):
+def apart_spread_in(source, wide, lines, stride, blocks):
     for place, line in enumerate(lines):
         wide[:, place * LANES : (place + 1) * LANES] = source[
             pl.ds(line, blocks, stride=stride), :
         ].astype(wide.dtype)
 
 
-def dft(wide, spectrum, tables, mid, flat, lines, outer, offset=0):
+def apart_dft(wide, spectrum, tables, mid, flat, lines, outer, offset=0):
     outer_fwd, inner_fwd, twist = tables
     mid[:, : lines * LANES] = nn(outer_fwd[...], wide[:, : lines * LANES])
     cos = twist[:, :LANES]
@@ -192,7 +1212,7 @@
     spectrum[0 : lines * outer, :] = nn(flat[0 : lines * outer, :], inner_fwd[...])
 
 
-def inverse_dft(flat, tables, mid_half, lines, outer):
+def apart_inverse_dft(flat, tables, mid_half, lines, outer):
     outer_inv, inner_inv, twist = tables
     cos = twist[:, :LANES]
     sin = twist[:, LANES:]
@@ -207,18 +1227,18 @@
     return nn(outer_inv[...], mid_half[:, : lines * LANES])
 
 
-def spread_out(value, target, lines, stride, blocks):
+def apart_spread_out(value, target, lines, stride, blocks):
     for place, line in enumerate(lines):
         target[pl.ds(line, blocks, stride=stride), :] = value[
             :, place * LANES : (place + 1) * LANES
         ]
 
 
-def signal_lines(sz):
+def apart_signal_lines(sz):
     return [seq * sz.blocks * sz.piece + chan for seq in range(sz.seqs) for chan in range(sz.chans)]
 
 
-def conv_forward_kernel(
+def apart_conv_forward_kernel(
     sz,
     inner_ref,
     taps_ref,
@@ -242,11 +1262,11 @@
     sems_in,
     sems_out,
 ):
-    barrier = enter(sz.count, sz.hid)
+    barrier = apart_enter(sz.count, sz.hid)
     pl.semaphore_wait(barrier, sz.count - 1)
     into = tuple(sems_in.at[i] for i in range(3))
     back = tuple(sems_out.at[i] for i in range(3))
-    exchange_start(inner_ref, landed, into, sz.count, sz.rows, sz.hid, sz.piece, True)
+    apart_exchange_start(inner_ref, landed, into, sz.count, sz.rows, sz.hid, sz.piece, True)
 
     piece, blocks, outer = sz.piece, sz.blocks, sz.outer
     step = 4
@@ -259,35 +1279,35 @@
                 :, block * LANES : (block + 1) * LANES
             ]
     lines = [way * piece + chan for way in range(2) for chan in range(sz.chans)]
-    spread_in(tall, wide, lines, 2 * piece, blocks)
-    dft(wide, sig_spec, (outer_fwd, inner_fwd, twist), mid, flat, len(lines), outer)
+    apart_spread_in(tall, wide, lines, 2 * piece, blocks)
+    apart_dft(wide, sig_spec, (outer_fwd, inner_fwd, twist), mid, flat, len(lines), outer)
     span = sz.chans * outer
     filt_spec[:, :LANES] = sig_spec[0:span, :LANES] + sig_spec[span : 2 * span, :LANES]
     filt_spec[:, LANES:] = sig_spec[0:span, LANES:] - sig_spec[span : 2 * span, LANES:]
 
-    exchange_wait(inner_ref, landed, into, sz.count, sz.rows, sz.hid, piece)
+    apart_exchange_wait(inner_ref, landed, into, sz.count, sz.rows, sz.hid, piece)
     tall[0 : sz.channels, :] = landed[...].astype(F32)
-    lines = signal_lines(sz)
-    spread_in(tall, wide, lines, piece, blocks)
-    dft(wide, sig_spec, (outer_fwd, inner_fwd, twist), mid, flat, sz.pairs, outer)
+    lines = apart_signal_lines(sz)
+    apart_spread_in(tall, wide, lines, piece, blocks)
+    apart_dft(wide, sig_spec, (outer_fwd, inner_fwd, twist), mid, flat, sz.pairs, outer)
     for seq in range(sz.seqs):
         rows = pl.ds(seq * span, span)
         sig_re, sig_im = sig_spec[rows, :LANES], sig_spec[rows, LANES:]
         fil_re, fil_im = filt_spec[:, :LANES], filt_spec[:, LANES:]
         flat[rows, :LANES] = (sig_re * fil_re - sig_im * fil_im).astype(BF16)
         flat[rows, LANES:] = (sig_re * fil_im + sig_im * fil_re).astype(BF16)
-    result = inverse_dft(flat, (outer_inv, inner_inv, twist), mid_half, sz.pairs, outer)
-    spread_out(result, tall, lines, piece, blocks)
+    result = apart_inverse_dft(flat, (outer_inv, inner_inv, twist), mid_half, sz.pairs, outer)
+    apart_spread_out(result, tall, lines, piece, blocks)
     staged[...] = tall[0 : sz.channels, :].astype(BF16)
-    exchange_start(staged, conv_ref, back, sz.count, sz.rows, sz.hid, piece, False)
-    exchange_wait(staged, conv_ref, back, sz.count, sz.rows, sz.hid, piece)
-
-
-def conv_forward(sz, inner, taps, pos, env, tables, cid):
+    apart_exchange_start(staged, conv_ref, back, sz.count, sz.rows, sz.hid, piece, False)
+    apart_exchange_wait(staged, conv_ref, back, sz.count, sz.rows, sz.hid, piece)
+
+
+def apart_conv_forward(sz, inner, taps, pos, env, tables, cid):
     outer_fwd, outer_inv, inner_fwd, inner_inv, twist = tables
     wide_lines = max(2 * sz.chans, sz.pairs)
     return pl.pallas_call(
-        functools.partial(conv_forward_kernel, sz),
+        functools.partial(apart_conv_forward_kernel, sz),
         out_shape=(
             jax.ShapeDtypeStruct((sz.channels, LANES), BF16),
             jax.ShapeDtypeStruct((sz.chans * sz.outer, 2 * LANES), F32),
@@ -313,7 +1333,7 @@
     )(inner, taps, pos, env, outer_fwd, outer_inv, inner_fwd, inner_inv, twist)
 
 
-def conv_backward_kernel(
+def apart_conv_backward_kernel(
     sz,
     grad_ref,
     filt_spec,
@@ -339,17 +1359,17 @@
     sems_in,
     sems_out,
 ):
-    barrier = enter(sz.count, sz.hid)
+    barrier = apart_enter(sz.count, sz.hid)
     pl.semaphore_wait(barrier, sz.count - 1)
     into = tuple(sems_in.at[i] for i in range(3))
     back = tuple(sems_out.at[i] for i in range(3))
     piece, blocks, outer = sz.piece, sz.blocks, sz.outer
-    exchange_start(grad_ref, landed, into, sz.count, sz.rows, sz.hid, piece, True)
-    exchange_wait(grad_ref, landed, into, sz.count, sz.rows, sz.hid, piece)
+    apart_exchange_start(grad_ref, landed, into, sz.count, sz.rows, sz.hid, piece, True)
+    apart_exchange_wait(grad_ref, landed, into, sz.count, sz.rows, sz.hid, piece)
     tall[0 : sz.channels, :] = landed[...].astype(F32)
-    lines = signal_lines(sz)
-    spread_in(tall, wide, lines, piece, blocks)
-    dft(wide, grad_spec, (outer_fwd, inner_fwd, twist), mid, flat, sz.pairs, outer)
+    lines = apart_signal_lines(sz)
+    apart_spread_in(tall, wide, lines, piece, blocks)
+    apart_dft(wide, grad_spec, (outer_fwd, inner_fwd, twist), mid, flat, sz.pairs, outer)
     span = sz.chans * outer
     for seq in range(sz.seqs):
         rows = pl.ds(seq * span, span)
@@ -358,10 +1378,10 @@
         flat[rows, :LANES] = (re * fil_re + im * fil_im).astype(BF16)
         flat[rows, LANES:] = (im * fil_re - re * fil_im).astype(BF16)
     inv_tables = (outer_inv, inner_inv, twist)
-    result = inverse_dft(flat, inv_tables, mid_half, sz.pairs, outer)
-    spread_out(result, tall, lines, piece, blocks)
+    result = apart_inverse_dft(flat, inv_tables, mid_half, sz.pairs, outer)
+    apart_spread_out(result, tall, lines, piece, blocks)
     staged[...] = tall[0 : sz.channels, :].astype(BF16)
-    exchange_start(staged, back_ref, back, sz.count, sz.rows, sz.hid, piece, False)
+    apart_exchange_start(staged, back_ref, back, sz.count, sz.rows, sz.hid, piece, False)
 
     total_re = jnp.zeros((span, LANES), F32)
     total_im = jnp.zeros((span, LANES), F32)
@@ -375,11 +1395,11 @@
     flat[span : 2 * span, :LANES] = total_re.astype(BF16)
     flat[0:span, LANES:] = total_im.astype(BF16)
     flat[span : 2 * span, LANES:] = (-total_im).astype(BF16)
-    result = inverse_dft(flat, inv_tables, mid_half, 2 * sz.chans, outer)
+    result = apart_inverse_dft(flat, inv_tables, mid_half, 2 * sz.chans, outer)
     lines = [way * piece + chan for way in range(2) for chan in range(sz.chans)]
     if sz.chans < piece:
         tall[...] = jnp.zeros_like(tall)
-    spread_out(result, tall, lines, 2 * piece, blocks)
+    apart_spread_out(result, tall, lines, 2 * piece, blocks)
     total = jnp.zeros((2 * piece, ORDER), F32)
     step = 4
     for start in range(0, blocks, step):
@@ -396,14 +1416,14 @@
         total += nt(grads.astype(BF16), pos_ref[:, span])
     taps_grad[...] = total
 
-    exchange_wait(staged, back_ref, back, sz.count, sz.rows, sz.hid, piece)
-
-
-def conv_backward(sz, grad, filt_spec, sig_spec, taps, pos, env, tables, cid):
+    apart_exchange_wait(staged, back_ref, back, sz.count, sz.rows, sz.hid, piece)
+
+
+def apart_conv_backward(sz, grad, filt_spec, sig_spec, taps, pos, env, tables, cid):
     outer_fwd, outer_inv, inner_fwd, inner_inv, twist = tables
     wide_lines = max(2 * sz.chans, sz.pairs)
     return pl.pallas_call(
-        functools.partial(conv_backward_kernel, sz),
+        functools.partial(apart_conv_backward_kernel, sz),
         out_shape=(
             jax.ShapeDtypeStruct((sz.channels, LANES), BF16),
             jax.ShapeDtypeStruct((2 * sz.piece, ORDER), F32),
@@ -429,7 +1449,7 @@
     )(grad, filt_spec, sig_spec, taps, pos, env, outer_fwd, outer_inv, inner_fwd, inner_inv, twist)
 
 
-def project(sz, normed, w_in, w_gate, inner_ref, gate_ref):
+def apart_project(sz, normed, w_in, w_gate, inner_ref, gate_ref):
     for side in range(sz.hid):
         rows = slice(side * sz.padded, (side + 1) * sz.padded)
         part = normed[:, side * sz.half : (side + 1) * sz.half]
@@ -437,17 +1457,17 @@
         gate_ref[rows, :] = nt(w_gate[side], part)
 
 
-def first_kernel(sz, x_ref, gain_ref, w_in, w_gate, normed_ref, inner_ref, gate_ref):
+def apart_first_kernel(sz, x_ref, gain_ref, w_in, w_gate, normed_ref, inner_ref, gate_ref):
     normal, _ = normalize(x_ref[...].astype(F32))
     normed = (normal * gain_ref[0:1, :]).astype(BF16)
     normed_ref[...] = normed
-    project(sz, normed, w_in, w_gate, inner_ref, gate_ref)
-
-
-def first(sz, x, gains, w_in, w_gate):
+    apart_project(sz, normed, w_in, w_gate, inner_ref, gate_ref)
+
+
+def apart_first(sz, x, gains, w_in, w_gate):
     tokens = x.shape[0]
     return pl.pallas_call(
-        functools.partial(first_kernel, sz),
+        functools.partial(apart_first_kernel, sz),
         out_shape=(
             jax.ShapeDtypeStruct((tokens, sz.width), BF16),
             jax.ShapeDtypeStruct((sz.channels, tokens), BF16),
@@ -460,7 +1480,7 @@
     )(x, gains, w_in, w_gate)
 
 
-def mix_out(sz, mixed, w_out):
+def apart_mix_out(sz, mixed, w_out):
     parts = []
     for side in range(sz.hid):
         rows = slice(side * sz.padded, (side + 1) * sz.padded)
@@ -468,7 +1488,7 @@
     return jnp.concatenate(parts, axis=1)
 
 
-def ff_specs(sz, layer, tile):
+def apart_ff_specs(sz, layer, tile):
     steps = sz.hidden // sz.hid // tile
     first_half = lambda i: jnp.minimum(i, steps - 1)
     second = lambda i: jnp.maximum(i - steps, 0)
@@ -481,7 +1501,7 @@
     return specs, steps
 
 
-def forward_kernel(
+def apart_forward_kernel(
     sz,
     steps,
     conv_ref,
@@ -514,7 +1534,7 @@
         summed = conv_ref[...].astype(F32) + skip_ref[...] * inner_ref[...].astype(F32)
         summed_ref[...] = summed
         mixed_ref[...] = (gate_ref[...] * summed).astype(BF16)
-        middle = x_ref[...].astype(F32) + mix_out(sz, mixed_ref, w_out)
+        middle = x_ref[...].astype(F32) + apart_mix_out(sz, mixed_ref, w_out)
         middle_ref[...] = middle
         normal, _ = normalize(middle)
         normed_two[...] = (normal * gain_ref[1:2, :]).astype(BF16)
@@ -534,17 +1554,17 @@
         normal, _ = normalize(next_x[...])
         normed = (normal * next_gain[0:1, :]).astype(BF16)
         next_normed[...] = normed
-        project(sz, normed, w_in, w_gate, next_inner, next_gate)
-
-
-def full(shape):
+        apart_project(sz, normed, w_in, w_gate, next_inner, next_gate)
+
+
+def apart_full(shape):
     return pl.BlockSpec(shape, lambda i: (0,) * len(shape))
 
 
-def forward(sz, layer, conv, inner, gate, skip, x, gains, next_gains, w_out, w_in, w_gate, ff):
+def apart_forward(sz, layer, conv, inner, gate, skip, x, gains, next_gains, w_out, w_in, w_gate, ff):
     tokens = x.shape[0]
     tile = 512
-    specs, steps = ff_specs(sz, layer, tile)
+    specs, steps = apart_ff_specs(sz, layer, tile)
     small = (conv, inner, gate, skip, x, gains, next_gains, w_out, w_in, w_gate)
     outs = (
         ((sz.channels, tokens), F32),
@@ -557,11 +1577,11 @@
         ((sz.channels, tokens), F32),
     )
     return pl.pallas_call(
-        functools.partial(forward_kernel, sz, steps),
+        functools.partial(apart_forward_kernel, sz, steps),
         grid=(2 * steps,),
         out_shape=tuple(jax.ShapeDtypeStruct(shape, kind) for shape, kind in outs),
-        in_specs=[full(entry.shape) for entry in small] + specs,
-        out_specs=tuple(full(shape) for shape, kind in outs),
+        in_specs=[apart_full(entry.shape) for entry in small] + specs,
+        out_specs=tuple(apart_full(shape) for shape, kind in outs),
         compiler_params=pltpu.CompilerParams(
             dimension_semantics=("arbitrary",), vmem_limit_bytes=48 * MIB
         ),
@@ -569,7 +1589,7 @@
     )(*small, *ff)
 
 
-def block_grads(sz, tall, flat, target, slot):
+def apart_block_grads(sz, tall, flat, target, slot):
     blocks_side = target.shape[1] // sz.hid
     size = sz.half // blocks_side
     rows = sz.padded // blocks_side
@@ -582,7 +1602,7 @@
             ).astype(target.dtype)
 
 
-def ff_backward_tile(normed, grad, up_ref, down_ref, total, out_total):
+def apart_ff_backward_tile(normed, grad, up_ref, down_ref, total, out_total):
     gate = nn(normed, up_ref[0, 0])
     up = nn(normed, up_ref[0, 1])
     grad_hidden = nn(grad, down_ref[0])
@@ -594,7 +1614,7 @@
     total[...] += nt(grad_gate, up_ref[0, 0]) + nt(grad_up, up_ref[0, 1])
 
 
-def mixer_backward(
+def apart_mixer_backward(
     sz, grad_next, middle, total, gain, mixed, summed, gate, w_out, outs
 ):
     grad_middle, mixer_grad, grad_gate, grad_summed, grad_conv, gain_grad = outs
@@ -603,7 +1623,7 @@
     result = grad_next + back
     grad_middle[...] = result
     grad_o = result.astype(BF16)
-    block_grads(sz, mixed, grad_o, mixer_grad, 0)
+    apart_block_grads(sz, mixed, grad_o, mixer_grad, 0)
     for side in range(sz.hid):
         rows = slice(side * sz.padded, (side + 1) * sz.padded)
         grad_mixed = nt(w_out[side], grad_o[:, side * sz.half : (side + 1) * sz.half])
@@ -613,7 +1633,7 @@
         grad_conv[rows, :] = through.astype(BF16)
 
 
-def mixer_outs(sz, tokens, blocks):
+def apart_mixer_outs(sz, tokens, blocks):
     size = sz.width // blocks
     return (
         ((tokens, sz.width), F32),
@@ -625,7 +1645,7 @@
     )
 
 
-def turn_kernel(
+def apart_turn_kernel(
     sz,
     steps,
     conv_ref,
@@ -660,14 +1680,14 @@
     def _():
         summed[...] = conv_ref[...].astype(F32) + skip_ref[...] * inner_ref[...].astype(F32)
         mixed[...] = (gate_ref[...] * summed[...]).astype(BF16)
-        middle[...] = x_ref[...].astype(F32) + mix_out(sz, mixed, w_out)
+        middle[...] = x_ref[...].astype(F32) + apart_mix_out(sz, mixed, w_out)
         normal, _ = normalize(middle[...])
         normed_two[...] = (normal * gain_ref[1:2, :]).astype(BF16)
         out_total[...] = middle[...]
         total[...] = jnp.zeros_like(total)
 
     def accumulate(up_ref, down_ref):
-        ff_backward_tile(normed_two[...], grad_ref[...], up_ref, down_ref, total, out_total)
+        apart_ff_backward_tile(normed_two[...], grad_ref[...], up_ref, down_ref, total, out_total)
 
     pl.when(index < steps)(lambda: accumulate(up_a, down_a))
     pl.when(index >= steps)(lambda: accumulate(up_b, down_b))
@@ -676,7 +1696,7 @@
     def _():
         hidden_out[...] = out_total[...].astype(BF16)
         outs = (grad_middle, mixer_grad, grad_gate, grad_summed, grad_conv, gain_grad)
-        mixer_backward(
+        apart_mixer_backward(
             sz,
             grad_ref[...].astype(F32),
             middle[...],
@@ -690,17 +1710,17 @@
         )
 
 
-def turn(sz, layer, blocks, conv, inner, gate, skip, x, gains, grad, w_out, ff):
+def apart_turn(sz, layer, blocks, conv, inner, gate, skip, x, gains, grad, w_out, ff):
     tokens = x.shape[0]
-    specs, steps = ff_specs(sz, layer, 512)
+    specs, steps = apart_ff_specs(sz, layer, 512)
     small = (conv, inner, gate, skip, x, gains, grad, w_out)
-    outs = (((tokens, sz.width), BF16), ((tokens, sz.width), BF16)) + mixer_outs(sz, tokens, blocks)
+    outs = (((tokens, sz.width), BF16), ((tokens, sz.width), BF16)) + apart_mixer_outs(sz, tokens, blocks)
     return pl.pallas_call(
-        functools.partial(turn_kernel, sz, steps),
+        functools.partial(apart_turn_kernel, sz, steps),
         grid=(2 * steps,),
         out_shape=tuple(jax.ShapeDtypeStruct(shape, kind) for shape, kind in outs),
-        in_specs=[full(entry.shape) for entry in small] + specs,
-        out_specs=tuple(full(shape) for shape, kind in outs),
+        in_specs=[apart_full(entry.shape) for entry in small] + specs,
+        out_specs=tuple(apart_full(shape) for shape, kind in outs),
         scratch_shapes=[
             pltpu.VMEM((sz.channels, tokens), F32),
             pltpu.VMEM((sz.channels, tokens), BF16),
@@ -715,12 +1735,12 @@
     )(*small, *ff)
 
 
-def input_backward(
+def apart_input_backward(
     sz, back, through, grad_gate, skip, normed, x, gain, w_in, w_gate, grad_middle, mixer_grad
 ):
     inner_grad = (skip * through + back.astype(F32)).astype(BF16)
-    block_grads(sz, inner_grad, normed, mixer_grad, 0)
-    block_grads(sz, grad_gate, normed, mixer_grad, 1)
+    apart_block_grads(sz, inner_grad, normed, mixer_grad, 0)
+    apart_block_grads(sz, grad_gate, normed, mixer_grad, 1)
     parts = []
     for side in range(sz.hid):
         rows = slice(side * sz.padded, (side + 1) * sz.padded)
@@ -730,7 +1750,7 @@
     return grad_middle + result, gain_grad
 
 
-def backward_kernel(
+def apart_backward_kernel(
     sz,
     steps,
     back_ref,
@@ -770,7 +1790,7 @@
 
     @pl.when(index == 0)
     def _():
-        result, input_gain[...] = input_backward(
+        result, input_gain[...] = apart_input_backward(
             sz,
             back_ref[...],
             through_ref[...],
@@ -789,7 +1809,7 @@
         total[...] = jnp.zeros_like(total)
 
     def accumulate(up_ref, down_ref):
-        ff_backward_tile(normed_two[...], grad_ff[...], up_ref, down_ref, total, None)
+        apart_ff_backward_tile(normed_two[...], grad_ff[...], up_ref, down_ref, total, None)
 
     pl.when(index < steps)(lambda: accumulate(up_a, down_a))
     pl.when(index >= steps)(lambda: accumulate(up_b, down_b))
@@ -797,7 +1817,7 @@
     @pl.when(index == 2 * steps - 1)
     def _():
         outs = (grad_middle, mixer_grad, grad_gate, grad_summed, grad_conv, gain_grad)
-        mixer_backward(
+        apart_mixer_backward(
             sz,
             grad_next[...],
             middle_ref[...],
@@ -811,12 +1831,12 @@
         )
 
 
-def input_outs(sz, blocks):
+def apart_input_outs(sz, blocks):
     size = sz.width // blocks
     return (((2, blocks, sz.channels // blocks, size), BF16), ((1, sz.width), F32))
 
 
-def backward(
+def apart_backward(
     sz,
     layer,
     blocks,
@@ -840,7 +1860,7 @@
     ff,
 ):
     tokens = x.shape[0]
-    specs, steps = ff_specs(sz, layer, 512)
+    specs, steps = apart_ff_specs(sz, layer, 512)
     small = (
         back,
         through,
@@ -861,14 +1881,14 @@
         w_out,
     )
     outs = (
-        input_outs(sz, blocks) + (((tokens, sz.width), BF16),) + mixer_outs(sz, tokens, blocks)
+        apart_input_outs(sz, blocks) + (((tokens, sz.width), BF16),) + apart_mixer_outs(sz, tokens, blocks)
     )
     return pl.pallas_call(
-        functools.partial(backward_kernel, sz, steps),
+        functools.partial(apart_backward_kernel, sz, steps),
         grid=(2 * steps,),
         out_shape=tuple(jax.ShapeDtypeStruct(shape, kind) for shape, kind in outs),
-        in_specs=[full(entry.shape) for entry in small] + specs,
-        out_specs=tuple(full(shape) for shape, kind in outs),
+        in_specs=[apart_full(entry.shape) for entry in small] + specs,
+        out_specs=tuple(apart_full(shape) for shape, kind in outs),
         scratch_shapes=[
             pltpu.VMEM((tokens, sz.width), F32),
             pltpu.VMEM((tokens, sz.width), F32),
@@ -880,7 +1900,7 @@
     )(*small, *ff)
 
 
-def last_kernel(
+def apart_last_kernel(
     sz,
     back_ref,
     through_ref,
@@ -896,7 +1916,7 @@
     input_gain,
     grad_in,
 ):
-    grad_in[...], input_gain[...] = input_backward(
+    grad_in[...], input_gain[...] = apart_input_backward(
         sz,
         back_ref[...],
         through_ref[...],
@@ -912,11 +1932,11 @@
     )
 
 
-def last(sz, blocks, *args):
+def apart_last(sz, blocks, *args):
     tokens = args[5].shape[0]
-    outs = input_outs(sz, blocks) + (((tokens, sz.width), F32),)
+    outs = apart_input_outs(sz, blocks) + (((tokens, sz.width), F32),)
     return pl.pallas_call(
-        functools.partial(last_kernel, sz),
+        functools.partial(apart_last_kernel, sz),
         out_shape=tuple(jax.ShapeDtypeStruct(shape, kind) for shape, kind in outs),
         in_specs=[whole()] * len(args),
         out_specs=(whole(),) * len(outs),
@@ -925,7 +1945,7 @@
     )(*args)
 
 
-def ff_grads_kernel(normed_ref, grad_ref, up_ref, down_ref, out_ref, hidden, grad_gate, grad_up):
+def apart_ff_grads_kernel(normed_ref, grad_ref, up_ref, down_ref, out_ref, hidden, grad_gate, grad_up):
     tokens = normed_ref.shape[0]
     chunk = 256
     for start in range(0, tokens, chunk):
@@ -943,11 +1963,11 @@
     out_ref[2] = tn(grad_ref[...], hidden[...]).astype(BF16)
 
 
-def ff_grads(normed, grad, up, down):
+def apart_ff_grads(normed, grad, up, down):
     tokens, width = normed.shape
     units = down.shape[1]
     return pl.pallas_call(
-        ff_grads_kernel,
+        apart_ff_grads_kernel,
         out_shape=jax.ShapeDtypeStruct((3, width, units), BF16),
         in_specs=[whole()] * 4,
         out_specs=whole(),
@@ -957,7 +1977,7 @@
     )(normed, grad, up, down)
 
 
-def row_exchange_kernel(rows, parts, *refs):
+def apart_row_exchange_kernel(rows, parts, *refs):
     sources, targets, sems = refs[:parts], refs[parts : 2 * parts], refs[2 * parts]
     row = lax.axis_index("rows")
     col = lax.axis_index("hid")
@@ -1004,10 +2024,10 @@
         ).wait()
 
 
-def row_exchange(arrays, rows, cid):
+def apart_row_exchange(arrays, rows, cid):
     parts = len(arrays)
     return pl.pallas_call(
-        functools.partial(row_exchange_kernel, rows, parts),
+        functools.partial(apart_row_exchange_kernel, rows, parts),
         out_shape=tuple(jax.ShapeDtypeStruct(entry.shape, entry.dtype) for entry in arrays),
         in_specs=[pl.BlockSpec(memory_space=pl.ANY)] * parts,
         out_specs=(pl.BlockSpec(memory_space=pl.ANY),) * parts,
@@ -1017,35 +2037,35 @@
     )(*arrays)
 
 
-def swap(value):
+def apart_swap(value):
     return lax.ppermute(value, "hid", [(0, 1), (1, 0)])
 
 
-def both_halves(own, axis):
-    other = swap(own)
+def apart_both_halves(own, axis):
+    other = apart_swap(own)
     low = lax.axis_index("hid") == 0
     return jnp.concatenate([jnp.where(low, own, other), jnp.where(low, other, own)], axis=axis)
 
 
-def own_tokens(part):
+def apart_own_tokens(part):
     tokens = part.shape[0] // 2
     side = lax.axis_index("hid")
     keep = lax.dynamic_slice_in_dim(part, side * tokens, tokens, 0)
-    other = swap(lax.dynamic_slice_in_dim(part, (1 - side) * tokens, tokens, 0))
+    other = apart_swap(lax.dynamic_slice_in_dim(part, (1 - side) * tokens, tokens, 0))
     low = side == 0
     return jnp.concatenate([jnp.where(low, keep, other), jnp.where(low, other, keep)], axis=1)
 
 
-def own_features(part):
+def apart_own_features(part):
     half = part.shape[1] // 2
     side = lax.axis_index("hid")
     keep = lax.dynamic_slice_in_dim(part, side * half, half, 1)
-    other = swap(lax.dynamic_slice_in_dim(part, (1 - side) * half, half, 1))
+    other = apart_swap(lax.dynamic_slice_in_dim(part, (1 - side) * half, half, 1))
     low = side == 0
     return jnp.concatenate([jnp.where(low, keep, other), jnp.where(low, other, keep)], axis=0)
 
 
-def padded_mixer(sz, mixer):
+def apart_padded_mixer(sz, mixer):
     layers, kinds, blocks, size, _ = mixer.shape
     chan_first = jnp.concatenate([jnp.swapaxes(mixer[:, :2], 3, 4), mixer[:, 2:]], axis=1)
     grouped = chan_first.reshape(layers, kinds, blocks, size // sz.chans, sz.chans, size)
@@ -1058,14 +2078,14 @@
     return jnp.concatenate(parts, axis=2)
 
 
-def padded_channels(sz, values):
+def apart_padded_channels(sz, values):
     lead = values.shape[:-1]
     grouped = values.reshape(lead + (sz.rows, sz.chans))
     grouped = jnp.pad(grouped, ((0, 0),) * (len(lead) + 1) + ((0, sz.piece - sz.chans),))
     return grouped.reshape(lead + (sz.padded,))
 
 
-def envelopes(sz):
+def apart_envelopes(sz):
     row = lax.axis_index("rows")
     first_chan = lax.axis_index("hid") * sz.half + row * sz.chans
     channels = first_chan + jnp.arange(sz.piece, dtype=jnp.int32)
@@ -1078,15 +2098,15 @@
     return jnp.concatenate([shape, shape * (steps > 0)[None, :]], axis=0)
 
 
-def plane_gather(value):
+def apart_plane_gather(value):
     size = lax.axis_size("rows")
     for bit in (1, 2):
         other = lax.ppermute(value, "rows", [(r, r ^ bit) for r in range(size)])
         value = jnp.concatenate([value, other], axis=0)
-    return jnp.concatenate([value, swap(value)], axis=0)
-
-
-def on_device(hidden_in, d_out, gains, mixer, skip, filters, gate_up, down):
+    return jnp.concatenate([value, apart_swap(value)], axis=0)
+
+
+def apart_on_device(hidden_in, d_out, gains, mixer, skip, filters, gate_up, down):
     layers = gate_up.shape[0]
     rows = lax.axis_size("rows")
     hid = lax.axis_size("hid")
@@ -1094,32 +2114,32 @@
     hidden = gate_up.shape[3] * hid
     blocks = mixer.shape[2] * hid
     block_size = mixer.shape[3]
-    sz = Sizes(rows, hid, width, hidden, hidden_in.shape[0] * rows)
+    sz = apart_Sizes(rows, hid, width, hidden, hidden_in.shape[0] * rows)
     row = lax.axis_index("rows")
 
-    x = own_tokens(hidden_in)
-    gains_all = both_halves(gains, 2)
-    skip_all = both_halves(padded_channels(sz, skip), 1)[:, :, None]
-    weights = both_halves(padded_mixer(sz, mixer)[:, :, None], 2)
-    gate_up_b = swap(gate_up)
-    down_b = swap(down)
+    x = apart_own_tokens(hidden_in)
+    gains_all = apart_both_halves(gains, 2)
+    skip_all = apart_both_halves(apart_padded_channels(sz, skip), 1)[:, :, None]
+    weights = apart_both_halves(apart_padded_mixer(sz, mixer)[:, :, None], 2)
+    gate_up_b = apart_swap(gate_up)
+    down_b = apart_swap(down)
     ff = (gate_up, down, gate_up_b, down_b)
-    grad_out = own_tokens(d_out)
+    grad_out = apart_own_tokens(d_out)
 
     tables = dft_tables(sz.length)
     pos = jnp.asarray(position_table(sz.length).T, F32).astype(BF16)
-    env = envelopes(sz)
+    env = apart_envelopes(sz)
     taps = lax.dynamic_slice_in_dim(filters, row * sz.chans, sz.chans, 3)
     taps = jnp.pad(taps, ((0, 0),) * 3 + ((0, sz.piece - sz.chans),))
     taps = jnp.swapaxes(taps, 2, 3).reshape(layers, 2 * sz.piece, ORDER).astype(BF16)
 
-    normed, inner, gate = first(sz, x, gains_all[0], weights[0, 0], weights[0, 1])
+    normed, inner, gate = apart_first(sz, x, gains_all[0], weights[0, 0], weights[0, 1])
     stored = []
     for layer in range(layers):
-        conv, filt_spec, sig_spec = conv_forward(sz, inner, taps[layer], pos, env, tables, 0)
+        conv, filt_spec, sig_spec = apart_conv_forward(sz, inner, taps[layer], pos, env, tables, 0)
         stored.append(dict(x=x, normed=normed, inner=inner, gate=gate, f=filt_spec, s=sig_spec))
         if layer < layers - 1:
-            summed, mixed, middle, normed_two, x, normed, next_inner, next_gate = forward(
+            summed, mixed, middle, normed_two, x, normed, next_inner, next_gate = apart_forward(
                 sz,
                 layer,
                 conv,
@@ -1138,7 +2158,7 @@
             inner, gate = next_inner, next_gate
 
     top = layers - 1
-    hidden_out, normed_two, *rest = turn(
+    hidden_out, normed_two, *rest = apart_turn(
         sz,
         top,
         blocks,
@@ -1162,14 +2182,14 @@
         grad_middle, out_grad, grad_gate, grad_summed, grad_conv, gain_two = rest
         ff_parts.insert(
             0,
-            ff_grads(
-                plane_gather(kept["normed_two"]),
-                plane_gather(grad_ff),
+            apart_ff_grads(
+                apart_plane_gather(kept["normed_two"]),
+                apart_plane_gather(grad_ff),
                 lax.dynamic_slice_in_dim(gate_up[layer], unit_start, units, 2),
                 lax.dynamic_slice_in_dim(down[layer], unit_start, units, 1),
             ),
         )
-        back, taps_grad = conv_backward(
+        back, taps_grad = apart_conv_backward(
             sz, grad_conv, kept["f"], kept["s"], taps[layer], pos, env, tables, 1
         )
         skip_parts.insert(0, jnp.sum(grad_summed * kept["inner"].astype(F32), axis=1))
@@ -1188,7 +2208,7 @@
         )
         if layer > 0:
             low = stored[layer - 1]
-            in_grad, gain_one, grad_ff, *rest = backward(
+            in_grad, gain_one, grad_ff, *rest = apart_backward(
                 sz,
                 layer - 1,
                 blocks,
@@ -1203,7 +2223,7 @@
                 ff,
             )
         else:
-            in_grad, gain_one, grad_in = last(sz, blocks, *common)
+            in_grad, gain_one, grad_in = apart_last(sz, blocks, *common)
         mixer_parts.insert(0, jnp.concatenate([in_grad, out_grad], axis=0))
         gain_parts.insert(0, jnp.concatenate([gain_one, gain_two], axis=0))
 
@@ -1212,7 +2232,7 @@
     pieces = jnp.stack(ff_parts).reshape(layers, 3, rows, piece_rows, units)
     pieces = jnp.pad(pieces, ((0, 0),) * 3 + ((0, padded_rows - piece_rows), (0, 0)))
     pieces = jnp.moveaxis(pieces, 2, 0)
-    (arrived,) = row_exchange((pieces,), rows, 2)
+    (arrived,) = apart_row_exchange((pieces,), rows, 2)
     arrived = arrived.reshape(rows // 4, 4, layers, 3, padded_rows, units)[:, :, :, :, :piece_rows]
     summed_ff = jnp.sum(arrived.astype(F32), axis=0)
     summed_ff = jnp.moveaxis(summed_ff, 0, 3).reshape(layers, 3, piece_rows, 4 * units)
@@ -1235,8 +2255,8 @@
     taps_out = jnp.stack(taps_parts).reshape(layers, 2, sz.piece, ORDER)[:, :, : sz.chans]
     taps_out = lax.all_gather(taps_out, "rows", axis=2, tiled=True)
     return (
-        own_features(hidden_out),
-        own_features(grad_in),
+        apart_own_features(hidden_out),
+        apart_own_features(grad_in),
         gain_out,
         mixers,
         skip_out,
@@ -1244,6 +2264,22 @@
         summed_ff[:, :2],
         summed_ff[:, 2],
     )
+
+
+def vmem_bytes(sz):
+    total = 0
+    for spec in layout(sz)[1]:
+        size = jnp.dtype(spec.dtype).itemsize
+        *lead, rows, lanes = spec.shape
+        total += math.prod(lead) * round_up(rows, 32 // size) * round_up(lanes, LANES) * size
+    return total
+
+
+def on_device(*arrays):
+    sz = Sizes.of(*arrays)
+    if vmem_bytes(sz) <= 60 * MIB:
+        return together(sz, *arrays)
+    return apart_on_device(*arrays)
 
 
 def solution(mesh):

time: 526 us -> 211 us (0.40)
  waiting for transfers between devices: 112 us -> 0 us
  blocking collectives: 88.3 us -> 0 us
  other arithmetic: 40.6 us -> 3.09 us
  local copies, waits for them, and re-layouts: 38.9 us -> 10.2 us
  Pallas kernels: 213 us -> 197 us
  between operations: 15.3 us -> 0.85 us
  starting transfers between devices: 12.8 us -> 0 us
    psum x1 -> x0, waiting for transfers between devices: 73.7 us -> none  [on_device(): mixers, small = lax.psum((mixers.astype(F32), small), ('rows', 'hid'))]
    all_gather x1 -> x0, blocking collectives: 47.8 us -> none  [on_device(): taps_out = lax.all_gather(taps_out, 'rows', axis=2, tiled=True)]
    psum x1 -> x0, blocking collectives: 40.4 us -> none  [on_device(): mixers, small = lax.psum((mixers.astype(F32), small), ('rows', 'hid'))]
    ppermute x21 -> x0, waiting for transfers between devices: 38.5 us -> none  [the longest x8 37.8 us: plane_gather(): other = lax.ppermute(value, 'rows', [(r, r ^ bit) for r in range(size)])]
    concatenate x22 -> x0, other arithmetic: 18.9 us -> none  [the longest x8 7.92 us: plane_gather(): value = jnp.concatenate([value, other], axis=0)]
    pallas_call x12 -> x1, Pallas kernels: 213 us -> 197 us  [program(): pl.pallas_call(functools.partial(program_kernel, sz), out_shape=tuple((ja...]
    ppermute x21 -> x0, starting transfers between devices: 12.8 us -> none  [the longest x8 10.1 us: plane_gather(): other = lax.ppermute(value, 'rows', [(r, r ^ bit) for r in range(size)])]
    slice x15 -> x6, local copies, waits for them, and re-layouts: 12.4 us -> 4.53 us  [the longest x1 1.1 us: together(): units[:, :2]]
  transfers between devices with their start and end apart: 22 -> 0, of which waited for: 7 -> 0; matrix products, arithmetic and copies ran while one was open for 13% -> 0% of each run, Pallas kernels for 39% -> 0%
where the time goes in v2:
time: 211 us
  Pallas kernels  197 us (93%)
  local copies, waits for them, and re-layouts  10.2 us (5%)
  other arithmetic  3.09 us (1%)
    pallas_call x1, Pallas kernels, program(): pl.pallas_call(functools.partial(program_kernel, sz), out_shape=tuple((ja...  197 us

profile of v2, /device:TPU:0, one launch (start us, length us, event | category | flops | bytes accessed | tf_op | source)
XLA Modules:
  0.0 210.8 jit_solution(2119663858687107097)
XLA Ops:
  0.6 196.7 %program.1 = (bf16[256,384]{1,0:T(8,128)(2,1)}, f32[256,384]{1,0:T(8,128)}, bf16[16,64,384]{2,1,0:T(8,128)(2,1)}, bf16[16,16,384]{2,1,0:T(8,128)(2,1)}, bf16[16,...) custom-call(bf16[256,384]{1,0:T(8,128)(2,1)} %refs_0_.1, bf16[256,384]{1,0:T(8,128)(2,1)} %refs_1_.1, ...), custom_call_target="tpu_custom_call" | custom-call | tf_op jit(solution)/shard_map/program/pallas_call | solution.py:1059
  197.3 0.7 slice.102
  198.0 0.7 slice.103
  198.7 0.6 reshape.70
  199.3 0.8 slice_convert_fusion
  200.2 1.0 slice.99
  201.2 0.7 reshape.78
  201.9 0.9 slice.80
  202.9 0.1 slice_bitcast_fusion.12
  203.0 0.0 copy-start.1
  203.0 0.1 copy.25
  203.0 1.1 copy.27
  204.2 0.0 copy-done.1
  204.2 0.1 fusion
  204.3 0.1 slice_bitcast_fusion.10
  204.4 0.1 maximum_bitcast_fusion.2
  204.5 0.1 bitcast_convert_fusion
  204.6 0.1 slice_bitcast_fusion.2
  204.7 0.1 slice_bitcast_fusion.4
  204.9 0.1 bitcast_convert_fusion.2
  205.0 0.1 slice_bitcast_fusion.6
  205.1 0.1 maximum_bitcast_fusion.1
  205.2 0.1 slice_bitcast_fusion.8
  205.4 0.1 maximum_bitcast_fusion
  205.4 0.0 copy-start
  205.5 1.6 pad_maximum_fusion
  207.0 0.0 copy-done
  207.0 0.1 convert_bitcast_fusion
  207.2 0.2 copy.28
  207.4 0.9 slice_bitcast_fusion
  208.2 0.0 copy-start.3
  208.2 0.0 copy-start.2
  208.3 1.1 slice.116
  209.3 0.0 copy-done.3
  209.4 0.7 copy.31
  210.0 0.0 copy-done.2
  210.0 0.7 copy.32
  (8 shorter events, 0.2 us)
Async XLA Ops:
  203.0 1.2 copy-start.1
  205.4 1.6 copy-start
  208.2 1.1 copy-start.3
  208.2 1.8 copy-start.2
